TPU v7x, 512 devices: a whole 4x8x8 slice. The times are simulated.
512 devices in a mesh: dp: 8 (over x, z_lo), ctx: 64 (over z_hi, y, core).
Axes of the slice: x: 4, y: 8, z: 8 (z_hi: 4, z_lo: 2; z = z_hi * 2 + z_lo), core: 2. Of those that a mesh axis runs over, the one named last changes fastest.
Arguments:
- level_input: bfloat16 [8, 65536, 256], P('dp', 'ctx'), may hold values from -6 to 6
- saved_forward: bfloat16 [3, 8, 65536, 256], P(None, 'dp', 'ctx'), may hold values from -6 to 6
- saved_reverse: bfloat16 [3, 8, 65536, 256], P(None, 'dp', 'ctx'), may hold values from -6 to 6
- filters: float32 [2, 2, 2, 256], replicated, may hold values from -2.5 to 2.5
- mixing: float32 [2, 5, 256], replicated, may hold values from -3 to 3
- cotangent: bfloat16 [8, 65536, 256], P('dp', 'ctx'), may hold values from -33 to 33
Outputs:
- grad_input: bfloat16 [8, 65536, 256], P('dp', 'ctx')
- grad_filters: float32 [2, 2, 2, 256], replicated
- grad_mixing: float32 [2, 5, 256], replicated
All inputs are finite; a program needn't handle non-finite values.
Results may differ from a plain program's by a relative error of at most 0.0065.
Values may be sent and summed in bfloat16 or wider, within the bound.
No kernel may reach another device: no remote copies, remote signals or barrier semaphores. Data moves between devices by JAX's collectives and lax.ppermute only.
A program may use at most 64 MiB of HBM per device.

v0:
```python
import math

import jax
import jax.numpy as jnp
from jax import lax
from jax.sharding import PartitionSpec as P

BASE = 128


def from_behind(block, axis, distance):
    devices = range(lax.axis_size(axis))
    route = [(i - distance, i) for i in devices if i - distance in devices]
    return lax.ppermute(block, axis, route)


def totals(values):
    return jnp.sum(values, axis=(0, 1))


def level_terms(gains, weight, s_a, s_y, t_a, t_y):
    filt = jnp.stack([jnp.stack([s_a, t_a]), jnp.stack([weight * s_y, weight * t_y])])
    high = gains[1, 0] * s_y + gains[1, 1] * t_y
    final = gains[0, 0] * s_y + gains[0, 1] * t_y
    return (filt, high, final)


def body(level_input, saved_forward, saved_reverse, filters, mixing, cotangent):
    levels = saved_forward.shape[0] + 1
    span = level_input.shape[1]
    width = level_input.shape[2]
    dy = cotangent.astype(jnp.float32)
    inputs_fwd = [level_input] + [saved_forward[i] for i in range(levels - 1)]
    inputs_rev = [level_input] + [saved_reverse[i] for i in range(levels - 1)]
    gains_fwd = filters[0]
    gains_rev = filters[1]
    grad_fwd = mixing[0, levels] * dy
    grad_rev = mixing[1, levels] * dy
    filt_total = jnp.zeros((2, 2, 2, width), jnp.float32)
    mix_total = jnp.zeros((2, levels + 1, width), jnp.float32)
    for level in reversed(range(levels)):
        dist = BASE * 2**level
        keep = span - dist
        plain_fwd = inputs_fwd[level].astype(jnp.float32)
        plain_rev = inputs_rev[level].astype(jnp.float32)
        weight_fwd = mixing[0, level]
        weight_rev = mixing[1, level]
        rim_fwd = from_behind(inputs_fwd[level][:, keep:], "ctx", 1)
        rim_rev = from_behind(inputs_rev[level][:, :dist], "ctx", -1)
        near_fwd = jnp.concatenate([rim_fwd.astype(jnp.float32), plain_fwd[:, :keep]], axis=1)
        near_rev = jnp.concatenate([plain_rev[:, dist:], rim_rev.astype(jnp.float32)], axis=1)
        cross_fwd = (totals(grad_fwd * near_fwd), totals(dy * near_fwd))
        cross_rev = (totals(grad_rev * near_rev), totals(dy * near_rev))
        tapped_fwd = gains_fwd[0, 0] * grad_fwd + gains_fwd[1, 0] * (weight_fwd * dy)
        tapped_rev = gains_rev[0, 0] * grad_rev + gains_rev[1, 0] * (weight_rev * dy)
        back_fwd = from_behind(tapped_fwd[:, :dist], "ctx", -1)
        back_rev = from_behind(tapped_rev[:, keep:], "ctx", 1)
        moved_fwd = jnp.concatenate([tapped_fwd[:, dist:], back_fwd], axis=1)
        moved_rev = jnp.concatenate([back_rev, tapped_rev[:, :keep]], axis=1)
        last = level == levels - 1
        filt_fwd, high_fwd, final_fwd = level_terms(
            gains_fwd,
            weight_fwd,
            cross_fwd[0],
            cross_fwd[1],
            totals(grad_fwd * plain_fwd),
            totals(dy * plain_fwd),
        )
        filt_rev, high_rev, final_rev = level_terms(
            gains_rev,
            weight_rev,
            cross_rev[0],
            cross_rev[1],
            totals(grad_rev * plain_rev),
            totals(dy * plain_rev),
        )
        filt_part = jnp.stack([filt_fwd, filt_rev])
        mix_part = jnp.zeros((2, levels + 1, width), jnp.float32)
        mix_part = mix_part.at[0, level].set(high_fwd).at[1, level].set(high_rev)
        if last:
            mix_part = mix_part.at[0, levels].set(final_fwd).at[1, levels].set(final_rev)
        filt_sum, mix_sum = lax.psum((filt_part, mix_part), ("dp", "ctx"))
        filt_total = filt_total + filt_sum
        mix_total = mix_total + mix_sum
        grad_fwd = gains_fwd[0, 1] * grad_fwd + gains_fwd[1, 1] * (weight_fwd * dy) + moved_fwd
        grad_rev = gains_rev[0, 1] * grad_rev + gains_rev[1, 1] * (weight_rev * dy) + moved_rev
    count = level_input.shape[0] * lax.axis_size("dp") * span * lax.axis_size("ctx")
    factor = 1.0 / math.sqrt(count)
    grad_input = (grad_fwd + grad_rev).astype(jnp.bfloat16)
    return (grad_input, filt_total * factor, mix_total * factor)


def solution(mesh):
    return jax.shard_map(
        body,
        mesh=mesh,
        in_specs=(
            P("dp", "ctx", None),
            P(None, "dp", "ctx", None),
            P(None, "dp", "ctx", None),
            P(),
            P(),
            P("dp", "ctx", None),
        ),
        out_specs=(P("dp", "ctx", None), P(), P()),
        check_vma=False,
    )
```

profile of v0, /device:TPU:57, one launch (start us, length us, event | category | flops | bytes accessed | tf_op | source)
XLA Modules:
  0.0 292.3 jit_solution(12166774043847606948)
XLA Ops:
  3.6 5.7 %collective-permute-start.4 = (f32[1,1024,256]{2,1,0:T(8,128)S(1)}, f32[1,1024,256]{2,1,0:T(8,128)S(1)}, u32[]{:S(2)}, u32[]{:S(2)}) collective-permute-start(f32[1,1024,256]{2,1,0:T(8,128)S(1)} %fusion.37), channel_id=1, source_target_pairs={{0,1},{1,2},{2,3},{3,4},{4,5},{5,6},{6,7},{7,8},{8,9},{9,10},{10,1... | collective-permute-start | bytes 3145736 | tf_op jit(solution)/shard_map/ppermute | solution.py:14
  9.6 1.9 collective-permute-start.13
  11.6 1.9 collective-permute-start.11
  13.5 15.0 %collective-permute-done.4 = f32[1,1024,256]{2,1,0:T(8,128)S(1)} collective-permute-done((f32[1,1024,256]{2,1,0:T(8,128)S(1)}, f32[1,1024,256]{2,1,0:T(8,128)S(1)}, u32[]{:S(2)}, u32[]{:S(2)}) %collective-permute-start.4) | collective-permute-done | bytes 1048608 | tf_op jit(solution)/shard_map/ppermute | solution.py:14
  29.0 10.9 %collective-permute-start.5 = (f32[1,512,256]{2,1,0:T(8,128)S(1)}, f32[1,512,256]{2,1,0:T(8,128)S(1)}, u32[]{:S(2)}, u32[]{:S(2)}) collective-permute-start(f32[1,512,256]{2,1,0:T(8,128)S(1)} %get-tuple-element.177), channel_id=1, source_target_pairs={{0,1},{1,2},{2,3},{3,4},{4,5},{5,6},{6,7},{7,8},{8,9},{9,10},{10,1... | collective-permute-start | bytes 1572872 | tf_op jit(solution)/shard_map/ppermute | solution.py:14
  40.1 1.9 collective-permute-start.12
  42.1 1.9 collective-permute-start.8
  44.3 2.4 collective-permute-start.9
  46.7 3.6 %collective-permute-start.15 = (bf16[1,128,256]{2,1,0:T(8,128)(2,1)S(1)}, bf16[1,128,256]{2,1,0:T(8,128)(2,1)S(1)}, u32[]{:S(2)}, u32[]{:S(2)}) collective-permute-start(bf16[1,128,256]{2,1,0:T(8,128)(2,1)S(1)} %get-tuple-element.185), channel_id=1, source_target_pairs={{1,0},{2,1},{3,2},{4,3},{5,4},{6,5},{7,6},{8,7},{9,8},{10,9},{11,1... | collective-permute-start | bytes 196616 | tf_op jit(solution)/shard_map/ppermute | solution.py:14
  51.9 7.3 %collective-permute-start.6 = (f32[1,256,256]{2,1,0:T(8,128)S(1)}, f32[1,256,256]{2,1,0:T(8,128)S(1)}, u32[]{:S(2)}, u32[]{:S(2)}) collective-permute-start(f32[1,256,256]{2,1,0:T(8,128)S(1)} %slice.496), channel_id=1, source_target_pairs={{0,1},{1,2},{2,3},{3,4},{4,5},{5,6},{6,7},{7,8},{8,9},{9,10},{10,1... | collective-permute-start | bytes 786440 | tf_op jit(solution)/shard_map/ppermute | solution.py:14
  59.9 2.2 collective-permute-done.15
  64.1 1.9 collective-permute-start.14
  74.9 10.7 %collective-permute-start.7 = (f32[1,128,256]{2,1,0:T(8,128)}, f32[1,128,256]{2,1,0:T(8,128)}, u32[]{:S(2)}, u32[]{:S(2)}) collective-permute-start(f32[1,128,256]{2,1,0:T(8,128)} %slice.498), channel_id=1, source_target_pairs={{0,1},{1,2},{2,3},{3,4},{4,5},{5,6},{6,7},{7,8},{8,9},{9,10},{10,1... | collective-permute-start | bytes 393224 | tf_op jit(solution)/shard_map/ppermute | solution.py:14
  87.5 12.3 %collective-permute-done = f32[1,1024,256]{2,1,0:T(8,128)S(1)} collective-permute-done((f32[1,1024,256]{2,1,0:T(8,128)S(1)}, f32[1,1024,256]{2,1,0:T(8,128)S(1)}, u32[]{:S(2)}, u32[]{:S(2)}) %collective-permute-start) | collective-permute-done | bytes 1048608 | tf_op jit(solution)/shard_map/ppermute | solution.py:14
  104.0 9.8 %collective-permute-done.1 = f32[1,512,256]{2,1,0:T(8,128)S(1)} collective-permute-done((f32[1,512,256]{2,1,0:T(8,128)S(1)}, f32[1,512,256]{2,1,0:T(8,128)S(1)}, u32[]{:S(2)}, u32[]{:S(2)}) %collective-permute-start.1) | collective-permute-done | bytes 524320 | tf_op jit(solution)/shard_map/ppermute | solution.py:14
  115.2 1.9 collective-permute-start.2
  118.9 6.9 %collective-permute-done.2 = f32[1,256,256]{2,1,0:T(8,128)S(1)} collective-permute-done((f32[1,256,256]{2,1,0:T(8,128)S(1)}, f32[1,256,256]{2,1,0:T(8,128)S(1)}, u32[]{:S(2)}, u32[]{:S(2)}) %collective-permute-start.2) | collective-permute-done | bytes 262176 | tf_op jit(solution)/shard_map/ppermute | solution.py:14
  134.7 2.6 broadcast_select_fusion.1
  139.4 2.6 scatter.44
  155.6 2.4 scatter.40
  162.0 116.6 %all-reduce.1 = (f32[2,2,2,256]{3,2,1,0:T(2,128)S(1)}, f32[2,5,256]{2,0,1:T(2,128)}) all-reduce(f32[2,2,2,256]{3,2,1,0:T(2,128)S(1)} %fusion.70, f32[2,5,256]{2,0,1:T(2,128)} %add_add_fusion), channel_id=1, replica_groups=mesh['dp'=8,'ctx'=64] {'dp','ctx'}, use_global_device_ids=true, to_apply=%region_8.0 | all-reduce | flops 4608 | bytes 36864 | tf_op jit(solution)/shard_map/psum | solution.py:82
  279.9 2.6 collective-permute-start.3
  283.1 6.6 %collective-permute-done.3 = f32[1,128,256]{2,1,0:T(8,128)S(1)} collective-permute-done((f32[1,128,256]{2,1,0:T(8,128)}, f32[1,128,256]{2,1,0:T(8,128)S(1)}, u32[]{:S(2)}, u32[]{:S(2)}) %collective-permute-start.3) | collective-permute-done | bytes 131104 | tf_op jit(solution)/shard_map/ppermute | solution.py:14
  289.8 2.5 fusion.27
  (160 shorter events, 56.6 us)
Async XLA Ops:
  1.6 67.0 %copy-start.23 = (f32[1,1,256]{2,0,1:T(1,128)}, f32[1,1,256]{2,0,1:T(1,128)S(1)}, u32[]{:S(2)}) copy-start(f32[1,1,256]{2,0,1:T(1,128)S(1)} %get-tuple-element.205) | copy-start | bytes 3076
  1.6 125.4 %copy-start.24 = (f32[1,1,256]{2,0,1:T(1,128)}, f32[1,1,256]{2,0,1:T(1,128)S(1)}, u32[]{:S(2)}) copy-start(f32[1,1,256]{2,0,1:T(1,128)S(1)} %get-tuple-element.209) | copy-start | bytes 3076
  2.3 126.5 %copy-start.4 = (f32[2,2,256]{2,0,1:T(2,128)}, f32[2,2,256]{2,0,1:T(2,128)S(1)}, u32[]{:S(2)}) copy-start(f32[2,2,256]{2,0,1:T(2,128)S(1)} %get-tuple-element.245) | copy-start | bytes 12292
  2.3 64.6 %copy-start.5 = (f32[1,1,256]{2,0,1:T(1,128)}, f32[1,1,256]{2,0,1:T(1,128)S(1)}, u32[]{:S(2)}) copy-start(f32[1,1,256]{2,0,1:T(1,128)S(1)} %get-tuple-element.228) | copy-start | bytes 3076
  2.3 64.6 %copy-start.6 = (f32[1,1,256]{2,0,1:T(1,128)}, f32[1,1,256]{2,0,1:T(1,128)S(1)}, u32[]{:S(2)}) copy-start(f32[1,1,256]{2,0,1:T(1,128)S(1)} %get-tuple-element.231) | copy-start | bytes 3076
  3.6 24.9 %collective-permute-start.4 = (f32[1,1024,256]{2,1,0:T(8,128)S(1)}, f32[1,1024,256]{2,1,0:T(8,128)S(1)}, u32[]{:S(2)}, u32[]{:S(2)}) collective-permute-start(f32[1,1024,256]{2,1,0:T(8,128)S(1)} %fusion.37), channel_id=1, source_target_pairs={{0,1},{1,2},{2,3},{3,4},{4,5},{5,6},{6,7},{7,8},{8,9},{9,10},{10,1... | collective-permute-start | bytes 3145736 | tf_op jit(solution)/shard_map/ppermute | solution.py:14
  9.6 34.6 %collective-permute-start.13 = (bf16[1,256,256]{2,1,0:T(8,128)(2,1)S(1)}, bf16[1,256,256]{2,1,0:T(8,128)(2,1)S(1)}, u32[]{:S(2)}, u32[]{:S(2)}) collective-permute-start(bf16[1,256,256]{2,1,0:T(8,128)(2,1)S(1)} %slice.507), channel_id=1, source_target_pairs={{1,0},{2,1},{3,2},{4,3},{5,4},{6,5},{7,6},{8,7},{9,8},{10,9},{11,1... | collective-permute-start | bytes 393224 | tf_op jit(solution)/shard_map/ppermute | solution.py:14
  11.6 35.1 %collective-permute-start.11 = (bf16[1,512,256]{2,1,0:T(8,128)(2,1)S(1)}, bf16[1,512,256]{2,1,0:T(8,128)(2,1)S(1)}, u32[]{:S(2)}, u32[]{:S(2)}) collective-permute-start(bf16[1,512,256]{2,1,0:T(8,128)(2,1)S(1)} %slice.503), channel_id=1, source_target_pairs={{1,0},{2,1},{3,2},{4,3},{5,4},{6,5},{7,6},{8,7},{9,8},{10,9},{11,1... | collective-permute-start | bytes 786440 | tf_op jit(solution)/shard_map/ppermute | solution.py:14
  29.0 21.4 %collective-permute-start.5 = (f32[1,512,256]{2,1,0:T(8,128)S(1)}, f32[1,512,256]{2,1,0:T(8,128)S(1)}, u32[]{:S(2)}, u32[]{:S(2)}) collective-permute-start(f32[1,512,256]{2,1,0:T(8,128)S(1)} %get-tuple-element.177), channel_id=1, source_target_pairs={{0,1},{1,2},{2,3},{3,4},{4,5},{5,6},{6,7},{7,8},{8,9},{9,10},{10,1... | collective-permute-start | bytes 1572872 | tf_op jit(solution)/shard_map/ppermute | solution.py:14
  40.1 24.0 %collective-permute-start.12 = (bf16[1,256,256]{2,1,0:T(8,128)(2,1)S(1)}, bf16[1,256,256]{2,1,0:T(8,128)(2,1)S(1)}, u32[]{:S(2)}, u32[]{:S(2)}) collective-permute-start(bf16[1,256,256]{2,1,0:T(8,128)(2,1)S(1)} %slice.504), channel_id=1, source_target_pairs={{0,1},{1,2},{2,3},{3,4},{4,5},{5,6},{6,7},{7,8},{8,9},{9,10},{10,1... | collective-permute-start | bytes 393224 | tf_op jit(solution)/shard_map/ppermute | solution.py:14
  42.1 24.1 %collective-permute-start.8 = (bf16[1,1024,256]{2,1,0:T(8,128)(2,1)S(1)}, bf16[1,1024,256]{2,1,0:T(8,128)(2,1)S(1)}, u32[]{:S(2)}, u32[]{:S(2)}) collective-permute-start(bf16[1,1024,256]{2,1,0:T(8,128)(2,1)S(1)} %get-tuple-element.172), channel_id=1, source_target_pairs={{0,1},{1,2},{2,3},{3,4},{4,5},{5,6},{6,7},{7,8},{8,9},{9,10},{10,1... | collective-permute-start | bytes 1572872 | tf_op jit(solution)/shard_map/ppermute | solution.py:14
  44.3 21.9 %collective-permute-start.9 = (bf16[1,1024,256]{2,1,0:T(8,128)(2,1)S(1)}, bf16[1,1024,256]{2,1,0:T(8,128)(2,1)S(1)}, u32[]{:S(2)}, u32[]{:S(2)}) collective-permute-start(bf16[1,1024,256]{2,1,0:T(8,128)(2,1)S(1)} %get-tuple-element.169), channel_id=1, source_target_pairs={{1,0},{2,1},{3,2},{4,3},{5,4},{6,5},{7,6},{8,7},{9,8},{10,9},{11,1... | collective-permute-start | bytes 1572872 | tf_op jit(solution)/shard_map/ppermute | solution.py:14
  46.7 15.4 %collective-permute-start.15 = (bf16[1,128,256]{2,1,0:T(8,128)(2,1)S(1)}, bf16[1,128,256]{2,1,0:T(8,128)(2,1)S(1)}, u32[]{:S(2)}, u32[]{:S(2)}) collective-permute-start(bf16[1,128,256]{2,1,0:T(8,128)(2,1)S(1)} %get-tuple-element.185), channel_id=1, source_target_pairs={{1,0},{2,1},{3,2},{4,3},{5,4},{6,5},{7,6},{8,7},{9,8},{10,9},{11,1... | collective-permute-start | bytes 196616 | tf_op jit(solution)/shard_map/ppermute | solution.py:14
  51.9 15.1 %collective-permute-start.6 = (f32[1,256,256]{2,1,0:T(8,128)S(1)}, f32[1,256,256]{2,1,0:T(8,128)S(1)}, u32[]{:S(2)}, u32[]{:S(2)}) collective-permute-start(f32[1,256,256]{2,1,0:T(8,128)S(1)} %slice.496), channel_id=1, source_target_pairs={{0,1},{1,2},{2,3},{3,4},{4,5},{5,6},{6,7},{7,8},{8,9},{9,10},{10,1... | collective-permute-start | bytes 786440 | tf_op jit(solution)/shard_map/ppermute | solution.py:14
  59.2 66.7 %copy-start.7 = (f32[1,1,256]{2,0,1:T(1,128)}, f32[1,1,256]{2,0,1:T(1,128)S(1)}, u32[]{:S(2)}) copy-start(f32[1,1,256]{2,0,1:T(1,128)S(1)} %get-tuple-element.232) | copy-start | bytes 3076
  59.2 66.7 %copy-start.8 = (f32[1,1,256]{2,0,1:T(1,128)}, f32[1,1,256]{2,0,1:T(1,128)S(1)}, u32[]{:S(2)}) copy-start(f32[1,1,256]{2,0,1:T(1,128)S(1)} %get-tuple-element.235) | copy-start | bytes 3076
  62.2 11.9 %collective-permute-start.10 = (bf16[1,512,256]{2,1,0:T(8,128)(2,1)S(1)}, bf16[1,512,256]{2,1,0:T(8,128)(2,1)S(1)}, u32[]{:S(2)}, u32[]{:S(2)}) collective-permute-start(bf16[1,512,256]{2,1,0:T(8,128)(2,1)S(1)} %slice.500), channel_id=1, source_target_pairs={{0,1},{1,2},{2,3},{3,4},{4,5},{5,6},{6,7},{7,8},{8,9},{9,10},{10,1... | collective-permute-start | bytes 786440 | tf_op jit(solution)/shard_map/ppermute | solution.py:14
  64.1 10.0 %collective-permute-start.14 = (bf16[1,128,256]{2,1,0:T(8,128)(2,1)S(1)}, bf16[1,128,256]{2,1,0:T(8,128)(2,1)S(1)}, u32[]{:S(2)}, u32[]{:S(2)}) collective-permute-start(bf16[1,128,256]{2,1,0:T(8,128)(2,1)S(1)} %get-tuple-element.186), channel_id=1, source_target_pairs={{0,1},{1,2},{2,3},{3,4},{4,5},{5,6},{6,7},{7,8},{8,9},{9,10},{10,1... | collective-permute-start | bytes 196616 | tf_op jit(solution)/shard_map/ppermute | solution.py:14
  68.6 60.3 %copy-start.18 = (f32[256]{0:T(256)}, f32[256]{0:T(256)S(1)}, u32[]{:S(2)}) copy-start(f32[256]{0:T(256)S(1)} %get-tuple-element.156) | copy-start | bytes 3076
  68.9 30.9 %collective-permute-start = (f32[1,1024,256]{2,1,0:T(8,128)S(1)}, f32[1,1024,256]{2,1,0:T(8,128)S(1)}, u32[]{:S(2)}, u32[]{:S(2)}) collective-permute-start(f32[1,1024,256]{2,1,0:T(8,128)S(1)} %get-tuple-element.182), channel_id=1, source_target_pairs={{1,0},{2,1},{3,2},{4,3},{5,4},{6,5},{7,6},{8,7},{9,8},{10,9},{11,1... | collective-permute-start | bytes 3145736 | tf_op jit(solution)/shard_map/ppermute | solution.py:14
  74.9 208.3 %collective-permute-start.7 = (f32[1,128,256]{2,1,0:T(8,128)}, f32[1,128,256]{2,1,0:T(8,128)}, u32[]{:S(2)}, u32[]{:S(2)}) collective-permute-start(f32[1,128,256]{2,1,0:T(8,128)} %slice.498), channel_id=1, source_target_pairs={{0,1},{1,2},{2,3},{3,4},{4,5},{5,6},{6,7},{7,8},{8,9},{9,10},{10,1... | collective-permute-start | bytes 393224 | tf_op jit(solution)/shard_map/ppermute | solution.py:14
  100.2 13.5 %collective-permute-start.1 = (f32[1,512,256]{2,1,0:T(8,128)S(1)}, f32[1,512,256]{2,1,0:T(8,128)S(1)}, u32[]{:S(2)}, u32[]{:S(2)}) collective-permute-start(f32[1,512,256]{2,1,0:T(8,128)S(1)} %get-tuple-element.180), channel_id=1, source_target_pairs={{1,0},{2,1},{3,2},{4,3},{5,4},{6,5},{7,6},{8,7},{9,8},{10,9},{11,1... | collective-permute-start | bytes 1572872 | tf_op jit(solution)/shard_map/ppermute | solution.py:14
  115.2 10.7 %collective-permute-start.2 = (f32[1,256,256]{2,1,0:T(8,128)S(1)}, f32[1,256,256]{2,1,0:T(8,128)S(1)}, u32[]{:S(2)}, u32[]{:S(2)}) collective-permute-start(f32[1,256,256]{2,1,0:T(8,128)S(1)} %slice.487), channel_id=1, source_target_pairs={{1,0},{2,1},{3,2},{4,3},{5,4},{6,5},{7,6},{8,7},{9,8},{10,9},{11,1... | collective-permute-start | bytes 786440 | tf_op jit(solution)/shard_map/ppermute | solution.py:14
  279.9 9.8 %collective-permute-start.3 = (f32[1,128,256]{2,1,0:T(8,128)}, f32[1,128,256]{2,1,0:T(8,128)S(1)}, u32[]{:S(2)}, u32[]{:S(2)}) collective-permute-start(f32[1,128,256]{2,1,0:T(8,128)} %slice.489), channel_id=1, source_target_pairs={{1,0},{2,1},{3,2},{4,3},{5,4},{6,5},{7,6},{8,7},{9,8},{10,9},{11,1... | collective-permute-start | bytes 393224 | tf_op jit(solution)/shard_map/ppermute | solution.py:14
  (18 other events, 356.6 us)
where the time goes:
time: 294 us; the launch traced here: 292 us
  blocking collectives  117 us (40%)
  starting transfers between devices  60.5 us (21%)
  waiting for transfers between devices  54.1 us (18%)
  other arithmetic  36.5 us (12%)
  local copies, waits for them, and re-layouts  23.2 us (8%)
    psum x1, blocking collectives, body(): filt_sum, mix_sum = lax.psum((filt_part, mix_part), ('dp', 'ctx'))  117 us
    ppermute x16, starting transfers between devices, from_behind(): return lax.ppermute(block, axis, route)  60.5 us
    ppermute x16, waiting for transfers between devices, from_behind(): return lax.ppermute(block, axis, route)  54.1 us
    scatter x8, local copies, waits for them, and re-layouts, body(): mix_part = mix_part.at[0, level].set(high_fwd).at[1, level].set(high_rev)  12.7 us
    another operation x8, other arithmetic, body(): filt_part = jnp.stack([filt_fwd, filt_rev])  7.51 us
  transfers between devices with their start and end apart: 16, of which 8 were waited for; matrix products, arithmetic and copies ran while one was open for 19% of the time, Pallas kernels for 0%

commit v1 on v0

v1 whole, which is shorter than its diff:
```python
import math

import jax
import jax.numpy as jnp
from jax import lax
from jax.experimental import pallas as pl
from jax.experimental.pallas import tpu as pltpu
from jax.sharding import Mesh
from jax.sharding import PartitionSpec as P

BLOCK = 128
NB = 8
LEVELS = 4
STEP = 16
LANES = 128
TAPS = 16
LAGS = tuple(
    (level, k)
    for level in range(LEVELS)
    for k in range(0, TAPS, 2**level)
)
ROW = {key: i for i, key in enumerate(LAGS)}
ROWS = 32
SUMS = 18
F32 = jnp.float32
DP = ("x", "zl")
CTX = ("zh", "y", "core")


def piece(ref, lead, n, r, cols):
    rows = pl.ds(pl.multiple_of(n * BLOCK + r * STEP, STEP), STEP)
    value = ref[rows, cols] if lead is None else ref[lead, rows, cols]
    return value.astype(F32).reshape(2, STEP // 2, LANES)


def columns(h):
    return pl.ds(h * LANES, LANES)


def add_corr(corr_ref, b, first, saved, dy_ref, delta):
    sign = 1 - 2 * b
    plan = []
    for level in range(LEVELS):
        for n in range(NB):
            for m in range(NB):
                key = (level, delta + sign * (m - n))
                if key in ROW:
                    plan.append((level, n, m, key))
    keys = sorted({p[3] for p in plan})
    slot = {key: i for i, key in enumerate(keys)}
    for h in range(2):
        cols = columns(h)

        def body(r, accs):
            accs = list(accs)
            dys = {m: piece(dy_ref, None, m, r, cols) for m in sorted({p[2] for p in plan})}
            for level in range(LEVELS):
                for n in range(NB):
                    mine = [p for p in plan if p[0] == level and p[1] == n]
                    if not mine:
                        continue
                    value = piece(first, None, n, r, cols) if level == 0 else piece(saved, level - 1, n, r, cols)
                    for _, _, m, key in mine:
                        prod = value * dys[m]
                        accs[slot[key]] = accs[slot[key]] + (prod[0] + prod[1])
            return tuple(accs)

        zero = jnp.zeros((STEP // 2, LANES), F32)
        accs = lax.fori_loop(0, BLOCK // STEP, body, (zero,) * len(keys))
        for key, acc in zip(keys, accs):
            at = (b, pl.ds(ROW[key], 1), cols)
            corr_ref[at] = corr_ref[at] + jnp.sum(acc, axis=0, keepdims=True)


def weights(filters_ref, mixing_ref):
    f = [[filters_ref[:, i, j, :] for j in range(2)] for i in range(2)]
    mix = [mixing_ref[:, i, :] for i in range(LEVELS + 1)]
    now = {0: mix[LEVELS]}
    out = {LEVELS - 1: now}
    for level in reversed(range(LEVELS)):
        d = 2**level
        new = {}
        for k, w in now.items():
            for at, term in ((k, f[0][1] * w), (k + d, f[0][0] * w)):
                new[at] = new[at] + term if at in new else term
        new[0] = new[0] + f[1][1] * mix[level]
        new[d] = new[d] + f[1][0] * mix[level]
        now = new
        out[level - 1] = now
    return f, mix, out


def put_taps(taps_ref, filters_ref, mixing_ref):
    taps = weights(filters_ref, mixing_ref)[2][-1]
    for k in range(TAPS):
        for b in range(2):
            taps_ref[b, k] = jnp.broadcast_to(taps[k][b : b + 1], taps_ref.shape[2:])


def add_filter(taps_ref, terms, r, cols, accs):
    accs = list(accs)
    for b, dy_ref, delta in terms:
        sign = 1 - 2 * b
        for m in range(NB):
            hits = [(n, delta + sign * (m - n)) for n in range(NB) if 0 <= delta + sign * (m - n) < TAPS]
            if not hits:
                continue
            value = piece(dy_ref, None, m, r, cols)
            for n, k in hits:
                accs[n] = accs[n] + value * taps_ref[b, k, :, cols][None]
    return accs


def near_kernel(core_ref, dy_ref, swap_ref, first, fwd, rev, filters_ref, mixing_ref, corr_ref, part_ref, taps_ref):
    core = core_ref[0]
    put_taps(taps_ref, filters_ref, mixing_ref)
    corr_ref[...] = jnp.zeros_like(corr_ref)
    add_corr(corr_ref, 0, first, fwd, dy_ref, 0)
    add_corr(corr_ref, 1, first, rev, dy_ref, 0)

    def side(b, saved):
        add_corr(corr_ref, b, first, saved, swap_ref, NB)
        for h in range(2):
            cols = columns(h)

            def body(r, carry):
                zero = jnp.zeros((2, STEP // 2, LANES), F32)
                accs = add_filter(taps_ref, ((0, dy_ref, 0), (1, dy_ref, 0), (b, swap_ref, NB)), r, cols, [zero] * NB)
                for n in range(NB):
                    rows = pl.ds(pl.multiple_of(n * BLOCK + r * STEP, STEP), STEP)
                    part_ref[rows, cols] = accs[n].reshape(STEP, LANES)
                return carry

            lax.fori_loop(0, BLOCK // STEP, body, 0)

    @pl.when(core == 0)
    def _():
        side(0, fwd)

    @pl.when(core == 1)
    def _():
        side(1, rev)


def far_kernel(core_ref, right_ref, left_ref, relay_ref, first, fwd, rev, filters_ref, mixing_ref, near_ref, part_ref, sums_ref, grad_ref, corr_ref, taps_ref):
    core = core_ref[0]
    put_taps(taps_ref, filters_ref, mixing_ref)
    corr_ref[...] = near_ref[...]
    add_corr(corr_ref, 0, first, fwd, right_ref, 2 * NB)
    add_corr(corr_ref, 1, first, rev, left_ref, 2 * NB)

    def side(b, saved):
        add_corr(corr_ref, b, first, saved, relay_ref, NB)
        for h in range(2):
            cols = columns(h)

            def body(r, carry):
                def rows(n):
                    return pl.ds(pl.multiple_of(n * BLOCK + r * STEP, STEP), STEP)

                accs = [part_ref[rows(n), cols].reshape(2, STEP // 2, LANES) for n in range(NB)]
                accs = add_filter(taps_ref, ((0, right_ref, 2 * NB), (1, left_ref, 2 * NB), (b, relay_ref, NB)), r, cols, accs)
                for n in range(NB):
                    grad_ref[rows(n), cols] = accs[n].reshape(STEP, LANES).astype(jnp.bfloat16)
                return carry

            lax.fori_loop(0, BLOCK // STEP, body, 0)

    @pl.when(core == 0)
    def _():
        side(1, rev)

    @pl.when(core == 1)
    def _():
        side(0, fwd)

    f, mix, w = weights(filters_ref, mixing_ref)
    filt = [[0.0, 0.0], [0.0, 0.0]]
    mixes = [None] * (LEVELS + 1)
    for level in range(LEVELS):
        d = 2**level
        s = {k: corr_ref[:, ROW[level, k], :] for k in range(0, TAPS, d)}
        for k, wk in w[level].items():
            filt[0][0] = filt[0][0] + wk * s[k + d]
            filt[0][1] = filt[0][1] + wk * s[k]
        filt[1][0] = filt[1][0] + mix[level] * s[d]
        filt[1][1] = filt[1][1] + mix[level] * s[0]
        mixes[level] = f[1][0] * s[d] + f[1][1] * s[0]
        if level == LEVELS - 1:
            mixes[LEVELS] = f[0][0] * s[d] + f[0][1] * s[0]
    sums = [filt[0][0], filt[0][1], filt[1][0], filt[1][1], *mixes]
    for copy in range(sums_ref.shape[0]):
        for b in range(2):
            for j, value in enumerate(sums):
                sums_ref[copy, pl.ds(b * 9 + j, 1), :] = value[b : b + 1]


def specs(n):
    return [pl.BlockSpec(memory_space=pltpu.SMEM)] + [pl.BlockSpec(memory_space=pltpu.VMEM)] * n


def route(value, axes, size, distance):
    pairs = [(i - distance, i) for i in range(size) if 0 <= i - distance < size]
    return lax.ppermute(value, axes, pairs)


def body(level_input, saved_forward, saved_reverse, filters, mixing, cotangent):
    width = level_input.shape[2]
    rows = level_input.shape[1]
    ctx = lax.axis_size(CTX)
    core = lax.axis_index("core")
    dy, first = cotangent[0], level_input[0]
    fwd, rev = saved_forward[:, 0], saved_reverse[:, 0]
    right = route(dy, CTX, ctx, -2)
    left = route(dy, CTX, ctx, 2)
    swap = lax.ppermute(dy, "core", [(0, 1), (1, 0)])
    relay = lax.ppermute(jnp.where(core == 0, right, left), "core", [(0, 1), (1, 0)])
    core_id = core.astype(jnp.int32).reshape(1)
    taps = pltpu.VMEM((2, TAPS, STEP // 2, width), F32)
    params = pltpu.CompilerParams(vmem_limit_bytes=24 * 1024 * 1024)
    near, part = pl.pallas_call(
        near_kernel,
        out_shape=(
            jax.ShapeDtypeStruct((2, ROWS, width), F32),
            jax.ShapeDtypeStruct((rows, width), F32),
        ),
        in_specs=specs(7),
        out_specs=(pl.BlockSpec(memory_space=pltpu.VMEM),) * 2,
        scratch_shapes=[taps],
        compiler_params=params,
        cost_estimate=pl.CostEstimate(flops=30_000_000, bytes_accessed=6_000_000, transcendentals=0),
        name="near",
    )(core_id, dy, swap, first, fwd, rev, filters, mixing)
    sums, grad = pl.pallas_call(
        far_kernel,
        out_shape=(
            jax.ShapeDtypeStruct((8, SUMS, width), F32),
            jax.ShapeDtypeStruct((rows, width), jnp.bfloat16),
        ),
        in_specs=specs(10),
        out_specs=(pl.BlockSpec(memory_space=pltpu.VMEM),) * 2,
        scratch_shapes=[pltpu.VMEM((2, ROWS, width), F32), taps],
        compiler_params=params,
        cost_estimate=pl.CostEstimate(flops=20_000_000, bytes_accessed=6_000_000, transcendentals=0),
        name="far",
    )(core_id, right, left, relay, first, fwd, rev, filters, mixing, near, part)
    groups = (DP, ("y",), ("zh", "core"))
    for i, axes in enumerate(groups):
        got = lax.all_to_all(sums, axes, 0, 0)
        total = jnp.sum(got, axis=0)
        if i + 1 < len(groups):
            sums = jnp.broadcast_to(total[None], sums.shape)
    count = level_input.shape[0] * lax.axis_size(DP) * rows * ctx
    total = (total * (1.0 / math.sqrt(count))).reshape(2, 9, width)
    return grad[None], total[:, :4].reshape(2, 2, 2, width), total[:, 4:]


def solution(mesh):
    fine = Mesh(mesh.devices.reshape(4, 2, 4, 8, 2), DP + CTX)
    return jax.shard_map(
        body,
        mesh=fine,
        in_specs=(
            P(DP, CTX, None),
            P(None, DP, CTX, None),
            P(None, DP, CTX, None),
            P(),
            P(),
            P(DP, CTX, None),
        ),
        out_specs=(P(DP, CTX, None), P(), P()),
        check_vma=False,
    )
```

time: 294 us -> 97.5 us (0.33)
  the two profiles are of different devices: /device:TPU:57 before, /device:TPU:1 now
where the time goes in v1:
time: 97.5 us; the launch traced here: 97.1 us
  blocking collectives  58.6 us (60%)
  starting transfers between devices  18.5 us (19%)
  Pallas kernels  10.2 us (10%)
  local copies, waits for them, and re-layouts  4.76 us (5%)
  waiting for transfers between devices  4.02 us (4%)
    all_to_all x3, blocking collectives, body(): got = lax.all_to_all(sums, axes, 0, 0)  58.6 us
    ppermute x1, starting transfers between devices, body(): lax.ppermute(jnp.where(core == 0, right, left), 'core', [(0, 1), (1, 0)])  6.97 us
    ppermute x1, starting transfers between devices, body(): swap = lax.ppermute(dy, 'core', [(0, 1), (1, 0)])  6.05 us
    ppermute x2, starting transfers between devices, route(): return lax.ppermute(value, axes, pairs)  5.49 us
    pallas_call x1, Pallas kernels, body(): pl.pallas_call(far_kernel, out_shape=(jax.ShapeDtypeStruct((8, SUMS, widt...  5.24 us
    pallas_call x1, Pallas kernels, body(): pl.pallas_call(near_kernel, out_shape=(jax.ShapeDtypeStruct((2, ROWS, wid...  4.96 us
    unnamed x15, local copies, waits for them, and re-layouts  4.71 us
    ppermute x2, waiting for transfers between devices, route(): return lax.ppermute(value, axes, pairs)  4.02 us
  transfers between devices with their start and end apart: 4, of which 2 were waited for; matrix products, arithmetic and copies ran while one was open for 0% of the time, Pallas kernels for 5%

profile of v1, /device:TPU:1, one launch (start us, length us, event | category | flops | bytes accessed | tf_op | source)
XLA Modules:
  0.0 97.1 jit_solution(14226998221036332946)
XLA Ops:
  0.6 0.0 copy-start.5
  0.6 0.0 copy-start.4
  0.7 0.0 copy-start
  0.7 4.2 %collective-permute-start.1 = (bf16[1024,256]{1,0:T(8,128)(2,1)}, bf16[1024,256]{1,0:T(8,128)(2,1)S(1)}, u32[]{:S(2)}, u32[]{:S(2)}) collective-permute-start(bf16[1024,256]{1,0:T(8,128)(2,1)} %bitcast.13), channel_id=1, source_target_pairs={{0,2},{1,3},{2,4},{3,5},{4,6},{5,7},{6,8},{7,9},{8,10},{9,11},{10,... | collective-permute-start | bytes 1572872 | tf_op jit(solution)/shard_map/ppermute | solution.py:204
  4.9 1.3 %collective-permute-start = (bf16[1024,256]{1,0:T(8,128)(2,1)}, bf16[1024,256]{1,0:T(8,128)(2,1)S(1)}, u32[]{:S(2)}, u32[]{:S(2)}) collective-permute-start(bf16[1024,256]{1,0:T(8,128)(2,1)} %bitcast.14), channel_id=1, source_target_pairs={{2,0},{3,1},{4,2},{5,3},{6,4},{7,5},{8,6},{9,7},{10,8},{11,9},{12,... | collective-permute-start | bytes 1572872 | tf_op jit(solution)/shard_map/ppermute | solution.py:204
  6.2 6.0 %collective-permute-start.3 = (bf16[1024,256]{1,0:T(8,128)(2,1)}, bf16[1024,256]{1,0:T(8,128)(2,1)S(1)}, u32[]{:S(2)}, u32[]{:S(2)}) collective-permute-start(bf16[1024,256]{1,0:T(8,128)(2,1)} %bitcast.15), channel_id=1, source_target_pairs={{0,1},{1,0},{2,3},{3,2},{4,5},{5,4},{6,7},{7,6},{8,9},{9,8},{10,11... | collective-permute-start | bytes 1572872 | tf_op jit(solution)/shard_map/ppermute | solution.py:216
  12.2 0.5 collective-permute-done.1.left_ref
  12.8 3.5 %collective-permute-done.right_ref = bf16[1024,256]{1,0:T(8,128)(2,1)S(1)} collective-permute-done((bf16[1024,256]{1,0:T(8,128)(2,1)}, bf16[1024,256]{1,0:T(8,128)(2,1)S(1)}, u32[]{:S(2)}, u32[]{:S(2)}) %collective-permute-start) | collective-permute-done | bytes 524320 | tf_op jit(solution)/shard_map/ppermute | solution.py:204
  16.2 0.1 broadcast_select_fusion
  16.3 7.0 %collective-permute-start.2 = (bf16[1024,256]{1,0:T(8,128)(2,1)S(1)}, bf16[1024,256]{1,0:T(8,128)(2,1)S(1)}, u32[]{:S(2)}, u32[]{:S(2)}) collective-permute-start(bf16[1024,256]{1,0:T(8,128)(2,1)S(1)} %broadcast_select_fusion), channel_id=1, source_target_pairs={{0,1},{1,0},{2,3},{3,2},{4,5},{5,4},{6,7},{7,6},{8,9},{9,8},{10,11... | collective-permute-start | bytes 1572872 | tf_op jit(solution)/shard_map/ppermute | solution.py:217
  23.3 0.0 copy-done.5
  23.3 0.0 collective-permute-done.3.swap_ref
  23.3 0.0 copy-start.1
  23.4 1.4 %copy-done.1 = bf16[3,1,1024,256]{3,2,1,0:T(8,128)(2,1)S(1)} copy-done((bf16[3,1,1024,256]{3,2,1,0:T(8,128)(2,1)S(1)}, bf16[3,1,1024,256]{3,2,1,0:T(8,128)(2,1)}, u32[]{:S(2)}) %copy-start.1) | copy-done | bytes 1572888
  24.8 1.0 %copy-done.2 = bf16[1,1024,256]{2,1,0:T(8,128)(2,1)S(1)} copy-done((bf16[1,1024,256]{2,1,0:T(8,128)(2,1)S(1)}, bf16[1,1024,256]{2,1,0:T(8,128)(2,1)}, u32[]{:S(2)}) %copy-start.2) | copy-done | bytes 524312
  25.8 1.0 %copy-done.3 = bf16[1,1024,256]{2,1,0:T(8,128)(2,1)S(1)} copy-done((bf16[1,1024,256]{2,1,0:T(8,128)(2,1)S(1)}, bf16[1,1024,256]{2,1,0:T(8,128)(2,1)}, u32[]{:S(2)}) %copy-start.3) | copy-done | bytes 524312
  26.8 5.0 %near.1 = (f32[2,32,256]{2,1,0:T(8,128)S(1)}, f32[1024,256]{1,0:T(8,128)S(1)}) custom-call(s32[1]{0:T(128)} %bitcast.core_ref, bf16[1024,256]{1,0:T(8,128)(2,1)S(1)} %bitcast.16, bf16[1024,256]{1,0:T(8,128)(2,1)S(1)} %collective-permute-done.3.swap_ref, bf16[1024,256]{1,0:T(8,128)(2,1)S(1)} %bitcast.11, bf16[3,1024,256]{2,1,0:T(8,128)(2,1)S(1)} %bitcast.7, ...), custom_call_target="tpu_custom_call" | custom-call | flops 30000000 | bytes 6000000 | tf_op jit(solution)/shard_map/near/pallas_call | solution.py:221
  31.8 0.0 collective-permute-done.2.relay_ref
  31.8 5.2 %far.1 = (f32[8,18,256]{2,1,0:T(8,128)S(1)}, bf16[1024,256]{1,0:T(8,128)(2,1)}) custom-call(s32[1]{0:T(128)} %bitcast.core_ref, bf16[1024,256]{1,0:T(8,128)(2,1)S(1)} %collective-permute-done.right_ref, bf16[1024,256]{1,0:T(8,128)(2,1)S(1)} %collective-permute-done.1.left_ref, bf16[1024,256]{1,0:T(8,128)(2,1)S(1)} %collective-permute-done.2.relay_ref, ...), custom_call_target="tpu_custom_call" | custom-call | flops 20000000 | bytes 6000000 | tf_op jit(solution)/shard_map/far/pallas_call | solution.py:234
  37.0 11.8 %all_to_all.15 = f32[8,18,256]{2,1,0:T(8,128)S(1)} all-to-all(f32[8,18,256]{2,1,0:T(8,128)S(1)} %get-tuple-element.10), channel_id=1, replica_groups=mesh['x'=4,'zl'=2,'zh'=4,'y'=8,'core'=2] {'x','zl'}, dimensions={0} | all-to-all | bytes 294912 | tf_op jit(solution)/shard_map/all_to_all | solution.py:249
  48.8 28.6 %all_to_all.16 = f32[8,18,256]{2,1,0:T(8,128)S(1)} all-to-all(f32[8,18,256]{2,1,0:T(8,128)S(1)} %broadcast_in_dim.7), channel_id=1, replica_groups=mesh['x'=4,'zl'=2,'zh'=4,'y'=8,'core'=2] {'y'}, dimensions={0} | all-to-all | bytes 294912 | tf_op jit(solution)/shard_map/all_to_all | solution.py:249
  77.5 18.3 %all_to_all.17 = f32[8,18,256]{2,1,0:T(8,128)S(1)} all-to-all(f32[8,18,256]{2,1,0:T(8,128)S(1)} %broadcast_in_dim.8), channel_id=1, replica_groups=mesh['x'=4,'zl'=2,'zh'=4,'y'=8,'core'=2] {'zh','core'}, dimensions={0} | all-to-all | bytes 294912 | tf_op jit(solution)/shard_map/all_to_all | solution.py:249
  95.8 0.6 copy.27
  96.5 0.6 copy.26
  (15 shorter events, 0.1 us)
Async XLA Ops:
  0.6 22.7 %copy-start.5 = (f32[2,5,256]{2,0,1:T(2,128)S(1)}, f32[2,5,256]{2,0,1:T(2,128)}, u32[]{:S(2)}) copy-start(f32[2,5,256]{2,0,1:T(2,128)} %param.10) | copy-start | bytes 30724
  0.6 22.7 %copy-start.4 = (f32[2,2,2,256]{3,2,1,0:T(2,128)S(1)}, f32[2,2,2,256]{3,2,1,0:T(2,128)}, u32[]{:S(2)}) copy-start(f32[2,2,2,256]{3,2,1,0:T(2,128)} %filters_ref.3) | copy-start | bytes 24580
  0.7 22.7 %copy-start = (bf16[3,1,1024,256]{3,2,1,0:T(8,128)(2,1)S(1)}, bf16[3,1,1024,256]{3,2,1,0:T(8,128)(2,1)}, u32[]{:S(2)}) copy-start(bf16[3,1,1024,256]{3,2,1,0:T(8,128)(2,1)} %param.7) | copy-start | bytes 4718596
  0.7 12.1 %collective-permute-start.1 = (bf16[1024,256]{1,0:T(8,128)(2,1)}, bf16[1024,256]{1,0:T(8,128)(2,1)S(1)}, u32[]{:S(2)}, u32[]{:S(2)}) collective-permute-start(bf16[1024,256]{1,0:T(8,128)(2,1)} %bitcast.13), channel_id=1, source_target_pairs={{0,2},{1,3},{2,4},{3,5},{4,6},{5,7},{6,8},{7,9},{8,10},{9,11},{10,... | collective-permute-start | bytes 1572872 | tf_op jit(solution)/shard_map/ppermute | solution.py:204
  4.9 11.4 %collective-permute-start = (bf16[1024,256]{1,0:T(8,128)(2,1)}, bf16[1024,256]{1,0:T(8,128)(2,1)S(1)}, u32[]{:S(2)}, u32[]{:S(2)}) collective-permute-start(bf16[1024,256]{1,0:T(8,128)(2,1)} %bitcast.14), channel_id=1, source_target_pairs={{2,0},{3,1},{4,2},{5,3},{6,4},{7,5},{8,6},{9,7},{10,8},{11,9},{12,... | collective-permute-start | bytes 1572872 | tf_op jit(solution)/shard_map/ppermute | solution.py:204
  6.2 17.1 %collective-permute-start.3 = (bf16[1024,256]{1,0:T(8,128)(2,1)}, bf16[1024,256]{1,0:T(8,128)(2,1)S(1)}, u32[]{:S(2)}, u32[]{:S(2)}) collective-permute-start(bf16[1024,256]{1,0:T(8,128)(2,1)} %bitcast.15), channel_id=1, source_target_pairs={{0,1},{1,0},{2,3},{3,2},{4,5},{5,4},{6,7},{7,6},{8,9},{9,8},{10,11... | collective-permute-start | bytes 1572872 | tf_op jit(solution)/shard_map/ppermute | solution.py:216
  16.3 15.5 %collective-permute-start.2 = (bf16[1024,256]{1,0:T(8,128)(2,1)S(1)}, bf16[1024,256]{1,0:T(8,128)(2,1)S(1)}, u32[]{:S(2)}, u32[]{:S(2)}) collective-permute-start(bf16[1024,256]{1,0:T(8,128)(2,1)S(1)} %broadcast_select_fusion), channel_id=1, source_target_pairs={{0,1},{1,0},{2,3},{3,2},{4,5},{5,4},{6,7},{7,6},{8,9},{9,8},{10,11... | collective-permute-start | bytes 1572872 | tf_op jit(solution)/shard_map/ppermute | solution.py:217
  23.3 1.4 %copy-start.1 = (bf16[3,1,1024,256]{3,2,1,0:T(8,128)(2,1)S(1)}, bf16[3,1,1024,256]{3,2,1,0:T(8,128)(2,1)}, u32[]{:S(2)}) copy-start(bf16[3,1,1024,256]{3,2,1,0:T(8,128)(2,1)} %param.8) | copy-start | bytes 4718596
  24.8 1.0 %copy-start.2 = (bf16[1,1024,256]{2,1,0:T(8,128)(2,1)S(1)}, bf16[1,1024,256]{2,1,0:T(8,128)(2,1)}, u32[]{:S(2)}) copy-start(bf16[1,1024,256]{2,1,0:T(8,128)(2,1)} %param.6) | copy-start | bytes 1572868
  25.8 1.0 %copy-start.3 = (bf16[1,1024,256]{2,1,0:T(8,128)(2,1)S(1)}, bf16[1,1024,256]{2,1,0:T(8,128)(2,1)}, u32[]{:S(2)}) copy-start(bf16[1,1024,256]{2,1,0:T(8,128)(2,1)} %param.11) | copy-start | bytes 1572868

commit v2 on v0

v2 whole, which is shorter than its diff:
```python
import math

import jax
import jax.numpy as jnp
from jax import lax
from jax.experimental import pallas as pl
from jax.experimental.pallas import tpu as pltpu
from jax.sharding import Mesh
from jax.sharding import PartitionSpec as P

BLOCK = 128
NB = 8
LEVELS = 4
STEP = 16
LANES = 128
F32 = jnp.float32
DP = ("x", "zl")
CTX = ("zh", "y", "core")
SA, TA, SY, TY = 0, 1, 2, 6
SUMS = 10
ROWS = 16
F00, F01, W0, W8, C0, CD = 0, 1, 2, 3, 4, 7
COEFS = 10


def rows_of(b, n, r):
    block = n if b == 0 else NB - 1 - n
    return pl.ds(pl.multiple_of(block * BLOCK + r * STEP, STEP), STEP)


def wide(value):
    return value.astype(F32).reshape(2, STEP // 2, LANES)


def times(c, v):
    return None if v is None else c * v


def plus(*terms):
    total = None
    for term in terms:
        if term is not None:
            total = term if total is None else total + term
    return total


def share(c, dys, p):
    dy = dys.get
    sums = [None] * SUMS

    def take(row, level, n, value):
        if value is not None:
            sums[row] = plus(sums[row], p(level, n) * value)

    g = {n: plus(times(c[W0], dy(n)), times(c[W8], dy(n + 8))) for n in range(15)}
    for n in range(NB):
        take(SY + 3, 3, n, dy(n + 8))
        take(TY + 3, 3, n, dy(n))
    for level in (2, 1, 0):
        d = 2**level
        for n in range(NB):
            take(SA, level, n, g[n + d])
            take(TA, level, n, g[n])
            take(SY + level, level, n, dy(n + d))
            take(TY + level, level, n, dy(n))
        need = {2: 11, 1: 9, 0: NB}[level]
        g = {
            n: plus(
                times(c[F01], g[n]),
                times(c[F00], g[n + d]),
                times(c[C0 + level], dy(n)),
                times(c[CD + level], dy(n + d)),
            )
            for n in range(need)
        }
    return sums, g


def run(work, first, saved, coef_ref, acc_ref, start, finish):
    for h in range(2):
        cols = pl.ds(h * LANES, LANES)

        def step(r, accs):
            accs = list(accs)
            grads = [start(n, r, cols) for n in range(NB)]
            at = 0
            for b, sources in work:
                c = [coef_ref[b, i, :, cols][None] for i in range(COEFS)]
                dys = {}
                for ref, base in sources:
                    for j in range(NB):
                        if base + j < 23:
                            dys[base + j] = wide(ref[rows_of(b, j, r), cols])

                def p(level, n):
                    rows = rows_of(b, n, r)
                    return wide(first[rows, cols] if level == 0 else saved[b][level - 1, rows, cols])

                sums, g = share(c, dys, p)
                for row in range(SUMS):
                    if sums[row] is not None:
                        accs[at + row] = accs[at + row] + (sums[row][0] + sums[row][1])
                at += SUMS
                for n in range(NB):
                    block = n if b == 0 else NB - 1 - n
                    grads[block] = plus(grads[block], g[n])
            for n in range(NB):
                finish(n, r, cols, grads[n].reshape(STEP, LANES))
            return tuple(accs)

        zero = jnp.zeros((STEP // 2, LANES), F32)
        accs = lax.fori_loop(0, BLOCK // STEP, step, (zero,) * (SUMS * len(work)))
        for i, (b, _) in enumerate(work):
            for row in range(SUMS):
                at = (b, pl.ds(row, 1), cols)
                acc_ref[at] = acc_ref[at] + jnp.sum(accs[i * SUMS + row], axis=0, keepdims=True)


def near_kernel(core_ref, dy_ref, swap_ref, first, fwd, rev, filters_ref, mixing_ref, acc_ref, part_ref, coef_ref):
    core = core_ref[0]
    acc_ref[...] = jnp.zeros_like(acc_ref)
    for b in range(2):
        f = [[filters_ref[b, i, pl.ds(j, 1), :] for j in range(2)] for i in range(2)]
        mix = [mixing_ref[i, pl.ds(b, 1), :] for i in range(LEVELS + 1)]
        c = [None] * COEFS
        c[F00], c[F01] = f[0]
        c[W0] = f[0][1] * mix[4] + f[1][1] * mix[3]
        c[W8] = f[0][0] * mix[4] + f[1][0] * mix[3]
        for level in range(3):
            c[C0 + level] = f[1][1] * mix[level]
            c[CD + level] = f[1][0] * mix[level]
        for i in range(COEFS):
            coef_ref[b, i] = jnp.broadcast_to(c[i], coef_ref.shape[2:])

    def keep(n, r, cols, value):
        part_ref[rows_of(0, n, r), cols] = value

    def side(b):
        own, both = [(dy_ref, 0)], [(dy_ref, 0), (swap_ref, NB)]
        work = [(b, both), (1 - b, own)]
        run(work, first, (fwd, rev), coef_ref, acc_ref, lambda n, r, cols: None, keep)

    for b in range(2):
        pl.when(core == b)(lambda b=b: side(b))


def far_kernel(right_ref, left_ref, first, fwd, rev, coef_ref, near_ref, part_ref, acc_ref, out_ref):
    acc_ref[...] = near_ref[...]

    def start(n, r, cols):
        return part_ref[rows_of(0, n, r), cols].reshape(2, STEP // 2, LANES)

    def keep(n, r, cols, value):
        out_ref[rows_of(0, n, r), cols] = value

    work = [(0, [(right_ref, 2 * NB)]), (1, [(left_ref, 2 * NB)])]
    run(work, first, (fwd, rev), coef_ref, acc_ref, start, keep)


def last_kernel(core_ref, relay_ref, first, fwd, rev, filters_ref, mixing_ref, coef_ref, far_ref, part_ref, sums_ref, grad_ref, acc_ref):
    core = core_ref[0]
    acc_ref[...] = far_ref[...]

    def start(n, r, cols):
        return part_ref[rows_of(0, n, r), cols].reshape(2, STEP // 2, LANES)

    def keep(n, r, cols, value):
        grad_ref[rows_of(0, n, r), cols] = value.astype(grad_ref.dtype)

    for b in range(2):
        work = [(b, [(relay_ref, NB)])]
        pl.when(core == 1 - b)(
            lambda work=work: run(work, first, (fwd, rev), coef_ref, acc_ref, start, keep)
        )
    f = [[filters_ref[:, i, j, :] for j in range(2)] for i in range(2)]
    mix = [mixing_ref[i] for i in range(LEVELS + 1)]
    acc = [acc_ref[:, i, :] for i in range(SUMS)]
    s, t = acc[SY : SY + LEVELS], acc[TY : TY + LEVELS]
    sums = [
        acc[SA] + mix[4] * s[3],
        acc[TA] + mix[4] * t[3],
        sum(mix[i] * s[i] for i in range(LEVELS)),
        sum(mix[i] * t[i] for i in range(LEVELS)),
        *(f[1][0] * s[i] + f[1][1] * t[i] for i in range(LEVELS)),
        f[0][0] * s[3] + f[0][1] * t[3],
    ]
    for copy in range(sums_ref.shape[0]):
        for b in range(2):
            for j, value in enumerate(sums):
                sums_ref[copy, pl.ds(b * 9 + j, 1), :] = value[b : b + 1]


def finish_kernel(factor, got_ref, filters_ref, mixing_ref):
    total = got_ref[0]
    for i in range(1, got_ref.shape[0]):
        total = total + got_ref[i]
    total = total * factor
    for b in range(2):
        for i in range(2):
            for j in range(2):
                at = b * 9 + i * 2 + j
                filters_ref[b, i, pl.ds(j, 1), :] = total[at : at + 1]
        for i in range(LEVELS + 1):
            at = b * 9 + 4 + i
            mixing_ref[i, pl.ds(b, 1), :] = total[at : at + 1]


def call(kernel, name, outs, args, scratch=(), flops=0):
    smem = args[0].dtype == jnp.int32
    vmem = pl.BlockSpec(memory_space=pltpu.VMEM)
    return pl.pallas_call(
        kernel,
        out_shape=outs,
        in_specs=[pl.BlockSpec(memory_space=pltpu.SMEM) if i == 0 and smem else vmem for i in range(len(args))],
        out_specs=(vmem,) * len(outs),
        scratch_shapes=scratch,
        compiler_params=pltpu.CompilerParams(vmem_limit_bytes=24 * 1024 * 1024),
        cost_estimate=pl.CostEstimate(flops=flops, bytes_accessed=6_000_000, transcendentals=0),
        name=name,
    )(*args)


def route(value, axes, size, distance):
    pairs = [(i - distance, i) for i in range(size) if 0 <= i - distance < size]
    return lax.ppermute(value, axes, pairs)


def body(level_input, saved_forward, saved_reverse, filters, mixing, cotangent):
    width = level_input.shape[2]
    rows = level_input.shape[1]
    ctx = lax.axis_size(CTX)
    core = lax.axis_index("core")
    core_id = core.astype(jnp.int32).reshape(1)
    dy = cotangent[0]
    mixing = jnp.swapaxes(mixing, 0, 1)
    inputs = (level_input[0], saved_forward[:, 0], saved_reverse[:, 0])
    acc = jax.ShapeDtypeStruct((2, ROWS, width), F32)
    part = jax.ShapeDtypeStruct((rows, width), F32)
    right = route(dy, CTX, ctx, -2)
    left = route(dy, CTX, ctx, 2)
    swap = lax.ppermute(dy, "core", [(0, 1), (1, 0)])
    acc_near, part_near, coef = call(
        near_kernel,
        "near",
        (acc, part, jax.ShapeDtypeStruct((2, COEFS, STEP // 2, width), F32)),
        (core_id, dy, swap, *inputs, filters, mixing),
        flops=100_000_000,
    )
    right, left, acc_near = lax.optimization_barrier((right, left, acc_near))
    relay = lax.ppermute(jnp.where(core == 0, right, left), "core", [(0, 1), (1, 0)])
    acc_far, part_far = call(
        far_kernel,
        "far",
        (acc, part),
        (right, left, *inputs, coef, acc_near, part_near),
        flops=100_000_000,
    )
    sums, grad = call(
        last_kernel,
        "last",
        (jax.ShapeDtypeStruct((8, 18, width), F32), jax.ShapeDtypeStruct((rows, width), jnp.bfloat16)),
        (core_id, relay, *inputs, filters, mixing, coef, acc_far, part_far),
        scratch=[pltpu.VMEM((2, ROWS, width), F32)],
        flops=100_000_000,
    )
    groups = (("x", "core"), ("y",), ("zl", "zh"))
    for i, axes in enumerate(groups):
        got = lax.all_to_all(sums, axes, 0, 0)
        if i + 1 < len(groups):
            sums = jnp.broadcast_to(jnp.sum(got, axis=0)[None], sums.shape)
    count = level_input.shape[0] * lax.axis_size(DP) * rows * ctx
    grad_filters, grad_mixing = call(
        lambda *refs: finish_kernel(1.0 / math.sqrt(count), *refs),
        "finish",
        (jax.ShapeDtypeStruct(filters.shape, F32), jax.ShapeDtypeStruct(mixing.shape, F32)),
        (got,),
    )
    return grad[None], grad_filters, jnp.swapaxes(grad_mixing, 0, 1)


def solution(mesh):
    fine = Mesh(mesh.devices.reshape(4, 2, 4, 8, 2), DP + CTX)
    return jax.shard_map(
        body,
        mesh=fine,
        in_specs=(
            P(DP, CTX, None),
            P(None, DP, CTX, None),
            P(None, DP, CTX, None),
            P(),
            P(),
            P(DP, CTX, None),
        ),
        out_specs=(P(DP, CTX, None), P(), P()),
        check_vma=False,
    )
```

time: 294 us -> 87.5 us (0.30)
  the two profiles are of different devices: /device:TPU:57 before, /device:TPU:64 now
where the time goes in v2:
time: 87.5 us; the launch traced here: 87 us
  blocking collectives  59.6 us (68%)
  starting transfers between devices  9.71 us (11%)
  Pallas kernels  8.47 us (10%)
  local copies, waits for them, and re-layouts  6.33 us (7%)
  waiting for transfers between devices  1.97 us (2%)
    all_to_all x3, blocking collectives, body(): got = lax.all_to_all(sums, axes, 0, 0)  59.6 us
    pallas_call x4, Pallas kernels, call(): pl.pallas_call(kernel, out_shape=outs, in_specs=[pl.BlockSpec(memory_spac...  8.47 us
    unnamed x16, local copies, waits for them, and re-layouts  6.3 us
    ppermute x2, starting transfers between devices, route(): return lax.ppermute(value, axes, pairs)  5.87 us
    ppermute x1, starting transfers between devices, body(): lax.ppermute(jnp.where(core == 0, right, left), 'core', [(0, 1), (1, 0)])  1.92 us
    ppermute x1, starting transfers between devices, body(): swap = lax.ppermute(dy, 'core', [(0, 1), (1, 0)])  1.92 us
  transfers between devices with their start and end apart: 4, of which 3 were waited for; matrix products, arithmetic and copies ran while one was open for 0% of the time, Pallas kernels for 6%

profile of v2, /device:TPU:64, one launch (start us, length us, event | category | flops | bytes accessed | tf_op | source)
XLA Modules:
  0.0 87.0 jit_solution(6919899660129301849)
XLA Ops:
  0.6 1.9 %collective-permute-start.2 = (bf16[1024,256]{1,0:T(8,128)(2,1)}, bf16[1024,256]{1,0:T(8,128)(2,1)S(1)}, u32[]{:S(2)}, u32[]{:S(2)}) collective-permute-start(bf16[1024,256]{1,0:T(8,128)(2,1)} %bitcast.17), channel_id=1, source_target_pairs={{0,1},{1,0},{2,3},{3,2},{4,5},{5,4},{6,7},{7,6},{8,9},{9,8},{10,11... | collective-permute-start | bytes 1572872 | tf_op jit(solution)/shard_map/ppermute | solution.py:241
  2.6 1.3 %collective-permute-start = (bf16[1024,256]{1,0:T(8,128)(2,1)}, bf16[1024,256]{1,0:T(8,128)(2,1)S(1)}, u32[]{:S(2)}, u32[]{:S(2)}) collective-permute-start(bf16[1024,256]{1,0:T(8,128)(2,1)} %bitcast.18), channel_id=1, source_target_pairs={{2,0},{3,1},{4,2},{5,3},{6,4},{7,5},{8,6},{9,7},{10,8},{11,9},{12,... | collective-permute-start | bytes 1572872 | tf_op jit(solution)/shard_map/ppermute | solution.py:225
  3.9 4.6 %collective-permute-start.1 = (bf16[1024,256]{1,0:T(8,128)(2,1)}, bf16[1024,256]{1,0:T(8,128)(2,1)S(1)}, u32[]{:S(2)}, u32[]{:S(2)}) collective-permute-start(bf16[1024,256]{1,0:T(8,128)(2,1)} %bitcast.19), channel_id=1, source_target_pairs={{0,2},{1,3},{2,4},{3,5},{4,6},{5,7},{6,8},{7,9},{8,10},{9,11},{10,... | collective-permute-start | bytes 1572872 | tf_op jit(solution)/shard_map/ppermute | solution.py:225
  8.5 0.0 collective-permute-done.2.swap_ref
  8.5 0.0 copy-start
  8.5 1.4 %copy-done = bf16[3,1,1024,256]{3,2,1,0:T(8,128)(2,1)S(1)} copy-done((bf16[3,1,1024,256]{3,2,1,0:T(8,128)(2,1)S(1)}, bf16[3,1,1024,256]{3,2,1,0:T(8,128)(2,1)}, u32[]{:S(2)}) %copy-start) | copy-done | bytes 1572888
  9.9 1.4 %copy-done.2 = bf16[3,1,1024,256]{3,2,1,0:T(8,128)(2,1)S(1)} copy-done((bf16[3,1,1024,256]{3,2,1,0:T(8,128)(2,1)S(1)}, bf16[3,1,1024,256]{3,2,1,0:T(8,128)(2,1)}, u32[]{:S(2)}) %copy-start.2) | copy-done | bytes 1572888
  11.3 1.0 %copy-done.4 = bf16[1,1024,256]{2,1,0:T(8,128)(2,1)S(1)} copy-done((bf16[1,1024,256]{2,1,0:T(8,128)(2,1)S(1)}, bf16[1,1024,256]{2,1,0:T(8,128)(2,1)}, u32[]{:S(2)}) %copy-start.4) | copy-done | bytes 524312
  12.3 1.0 %copy-done.5 = bf16[1,1024,256]{2,1,0:T(8,128)(2,1)S(1)} copy-done((bf16[1,1024,256]{2,1,0:T(8,128)(2,1)S(1)}, bf16[1,1024,256]{2,1,0:T(8,128)(2,1)}, u32[]{:S(2)}) %copy-start.5) | copy-done | bytes 524312
  13.4 0.7 copy-done.6
  14.1 0.7 copy-done.7
  14.8 4.0 %near.1 = (f32[2,16,256]{2,1,0:T(8,128)S(1)}, f32[1024,256]{1,0:T(8,128)S(1)}, f32[2,10,8,256]{3,2,1,0:T(8,128)S(1)}) custom-call(s32[1]{0:T(128)} %bitcast.core_ref, bf16[1024,256]{1,0:T(8,128)(2,1)S(1)} %bitcast.20, bf16[1024,256]{1,0:T(8,128)(2,1)S(1)} %collective-permute-done.2.swap_ref, bf16[1024,256]{1,0:T(8,128)(2,1)S(1)} %bitcast.14, ...), custom_call_target="tpu_custom_call" | custom-call | flops 100000000 | bytes 6000000 | tf_op jit(solution)/shard_map/near/pallas_call | solution.py:211
  18.8 0.0 copy-start.1
  18.8 0.2 collective-permute-done.right_ref
  19.0 1.3 %collective-permute-done.1.left_ref = bf16[1024,256]{1,0:T(8,128)(2,1)S(1)} collective-permute-done((bf16[1024,256]{1,0:T(8,128)(2,1)}, bf16[1024,256]{1,0:T(8,128)(2,1)S(1)}, u32[]{:S(2)}, u32[]{:S(2)}) %collective-permute-start.1) | collective-permute-done | bytes 524320 | tf_op jit(solution)/shard_map/ppermute | solution.py:225
  20.3 0.1 broadcast_select_fusion
  20.3 1.9 %collective-permute-start.3 = (bf16[1024,256]{1,0:T(8,128)(2,1)S(1)}, bf16[1024,256]{1,0:T(8,128)(2,1)S(1)}, u32[]{:S(2)}, u32[]{:S(2)}) collective-permute-start(bf16[1024,256]{1,0:T(8,128)(2,1)S(1)} %broadcast_select_fusion), channel_id=1, source_target_pairs={{0,1},{1,0},{2,3},{3,2},{4,5},{5,4},{6,7},{7,6},{8,9},{9,8},{10,11... | collective-permute-start | bytes 1572872 | tf_op jit(solution)/shard_map/ppermute | solution.py:250
  22.3 1.4 %far.1 = (f32[2,16,256]{2,1,0:T(8,128)S(1)}, f32[1024,256]{1,0:T(8,128)S(1)}) custom-call(bf16[1024,256]{1,0:T(8,128)(2,1)S(1)} %collective-permute-done.right_ref, bf16[1024,256]{1,0:T(8,128)(2,1)S(1)} %collective-permute-done.1.left_ref, bf16[1024,256]{1,0:T(8,128)(2,1)S(1)} %bitcast.15, bf16[3,1024,256]{2,1,0:T(8,128)(2,1)S(1)} %bitcast.9, ...), custom_call_target="tpu_custom_call" | custom-call | flops 100000000 | bytes 6000000 | tf_op jit(solution)/shard_map/far/pallas_call | solution.py:211
  23.7 0.5 collective-permute-done.3.relay_ref
  24.1 2.5 %last.1 = (f32[8,18,256]{2,1,0:T(8,128)S(1)}, bf16[1024,256]{1,0:T(8,128)(2,1)}) custom-call(s32[1]{0:T(128)} %bitcast.core_ref, bf16[1024,256]{1,0:T(8,128)(2,1)S(1)} %collective-permute-done.3.relay_ref, bf16[1024,256]{1,0:T(8,128)(2,1)S(1)} %bitcast.16, bf16[3,1024,256]{2,1,0:T(8,128)(2,1)S(1)} %bitcast.10, bf16[3,1024,256]{2,1,0:T(8,128)(2,1)S(1)} %bitcast.13, ...), custom_call_target="tpu_custom_call" | custom-call | flops 100000000 | bytes 6000000 | tf_op jit(solution)/shard_map/last/pallas_call | solution.py:211
  26.6 10.9 %all_to_all.15 = f32[8,18,256]{2,1,0:T(8,128)S(1)} all-to-all(f32[8,18,256]{2,1,0:T(8,128)S(1)} %get-tuple-element.24), channel_id=1, replica_groups=mesh['x'=4,'zl'=2,'zh'=4,'y'=8,'core'=2] {'x','core'}, dimensions={0} | all-to-all | bytes 294912 | tf_op jit(solution)/shard_map/all_to_all | solution.py:268
  37.6 27.6 %all_to_all.16 = f32[8,18,256]{2,1,0:T(8,128)S(1)} all-to-all(f32[8,18,256]{2,1,0:T(8,128)S(1)} %broadcast_in_dim.7), channel_id=1, replica_groups=mesh['x'=4,'zl'=2,'zh'=4,'y'=8,'core'=2] {'y'}, dimensions={0} | all-to-all | bytes 294912 | tf_op jit(solution)/shard_map/all_to_all | solution.py:268
  65.3 21.1 %all_to_all.17.refs_0_ = f32[8,18,256]{2,1,0:T(8,128)S(1)} all-to-all(f32[8,18,256]{2,1,0:T(8,128)S(1)} %broadcast_in_dim.8), channel_id=1, replica_groups=mesh['x'=4,'zl'=2,'zh'=4,'y'=8,'core'=2] {'zl','zh'}, dimensions={0} | all-to-all | bytes 294912 | tf_op jit(solution)/shard_map/all_to_all | solution.py:268
  86.4 0.6 finish.1
  (12 shorter events, 0.1 us)
Async XLA Ops:
  0.6 7.8 %collective-permute-start.2 = (bf16[1024,256]{1,0:T(8,128)(2,1)}, bf16[1024,256]{1,0:T(8,128)(2,1)S(1)}, u32[]{:S(2)}, u32[]{:S(2)}) collective-permute-start(bf16[1024,256]{1,0:T(8,128)(2,1)} %bitcast.17), channel_id=1, source_target_pairs={{0,1},{1,0},{2,3},{3,2},{4,5},{5,4},{6,7},{7,6},{8,9},{9,8},{10,11... | collective-permute-start | bytes 1572872 | tf_op jit(solution)/shard_map/ppermute | solution.py:241
  2.6 16.4 %collective-permute-start = (bf16[1024,256]{1,0:T(8,128)(2,1)}, bf16[1024,256]{1,0:T(8,128)(2,1)S(1)}, u32[]{:S(2)}, u32[]{:S(2)}) collective-permute-start(bf16[1024,256]{1,0:T(8,128)(2,1)} %bitcast.18), channel_id=1, source_target_pairs={{2,0},{3,1},{4,2},{5,3},{6,4},{7,5},{8,6},{9,7},{10,8},{11,9},{12,... | collective-permute-start | bytes 1572872 | tf_op jit(solution)/shard_map/ppermute | solution.py:225
  3.9 16.4 %collective-permute-start.1 = (bf16[1024,256]{1,0:T(8,128)(2,1)}, bf16[1024,256]{1,0:T(8,128)(2,1)S(1)}, u32[]{:S(2)}, u32[]{:S(2)}) collective-permute-start(bf16[1024,256]{1,0:T(8,128)(2,1)} %bitcast.19), channel_id=1, source_target_pairs={{0,2},{1,3},{2,4},{3,5},{4,6},{5,7},{6,8},{7,9},{8,10},{9,11},{10,... | collective-permute-start | bytes 1572872 | tf_op jit(solution)/shard_map/ppermute | solution.py:225
  8.5 1.4 %copy-start = (bf16[3,1,1024,256]{3,2,1,0:T(8,128)(2,1)S(1)}, bf16[3,1,1024,256]{3,2,1,0:T(8,128)(2,1)}, u32[]{:S(2)}) copy-start(bf16[3,1,1024,256]{3,2,1,0:T(8,128)(2,1)} %param.7) | copy-start | bytes 4718596
  9.9 1.4 %copy-start.2 = (bf16[3,1,1024,256]{3,2,1,0:T(8,128)(2,1)S(1)}, bf16[3,1,1024,256]{3,2,1,0:T(8,128)(2,1)}, u32[]{:S(2)}) copy-start(bf16[3,1,1024,256]{3,2,1,0:T(8,128)(2,1)} %param.8) | copy-start | bytes 4718596
  11.3 1.0 %copy-start.4 = (bf16[1,1024,256]{2,1,0:T(8,128)(2,1)S(1)}, bf16[1,1024,256]{2,1,0:T(8,128)(2,1)}, u32[]{:S(2)}) copy-start(bf16[1,1024,256]{2,1,0:T(8,128)(2,1)} %param.6) | copy-start | bytes 1572868
  12.3 1.0 %copy-start.5 = (bf16[1,1024,256]{2,1,0:T(8,128)(2,1)S(1)}, bf16[1,1024,256]{2,1,0:T(8,128)(2,1)}, u32[]{:S(2)}) copy-start(bf16[1,1024,256]{2,1,0:T(8,128)(2,1)} %param.11) | copy-start | bytes 1572868
  13.4 0.7 copy-start.6
  14.1 0.7 copy-start.7
  14.8 7.5 %copy-start.3 = (bf16[3,1,1024,256]{3,2,1,0:T(8,128)(2,1)S(1)}, bf16[3,1,1024,256]{3,2,1,0:T(8,128)(2,1)}, u32[]{:S(2)}) copy-start(bf16[3,1,1024,256]{3,2,1,0:T(8,128)(2,1)} %param.8) | copy-start | bytes 4718596
  18.8 3.5 %copy-start.1 = (bf16[3,1,1024,256]{3,2,1,0:T(8,128)(2,1)S(1)}, bf16[3,1,1024,256]{3,2,1,0:T(8,128)(2,1)}, u32[]{:S(2)}) copy-start(bf16[3,1,1024,256]{3,2,1,0:T(8,128)(2,1)} %param.7) | copy-start | bytes 4718596
  20.3 3.8 %collective-permute-start.3 = (bf16[1024,256]{1,0:T(8,128)(2,1)S(1)}, bf16[1024,256]{1,0:T(8,128)(2,1)S(1)}, u32[]{:S(2)}, u32[]{:S(2)}) collective-permute-start(bf16[1024,256]{1,0:T(8,128)(2,1)S(1)} %broadcast_select_fusion), channel_id=1, source_target_pairs={{0,1},{1,0},{2,3},{3,2},{4,5},{5,4},{6,7},{7,6},{8,9},{9,8},{10,11... | collective-permute-start | bytes 1572872 | tf_op jit(solution)/shard_map/ppermute | solution.py:250

commit v3 on v2

--- a/solution.py
+++ b/solution.py
@@ -9,6 +9,7 @@
 from jax.sharding import PartitionSpec as P
 
 BLOCK = 128
+HEAD = 3 * BLOCK
 NB = 8
 LEVELS = 4
 STEP = 16
@@ -76,7 +77,7 @@
     return sums, g
 
 
-def run(work, first, saved, coef_ref, acc_ref, start, finish):
+def run(work, saved, coef_ref, acc_ref, start, finish):
     for h in range(2):
         cols = pl.ds(h * LANES, LANES)
 
@@ -93,8 +94,7 @@
                             dys[base + j] = wide(ref[rows_of(b, j, r), cols])
 
                 def p(level, n):
-                    rows = rows_of(b, n, r)
-                    return wide(first[rows, cols] if level == 0 else saved[b][level - 1, rows, cols])
+                    return wide(saved[3 * b + level if level else 0, rows_of(b, n, r), cols])
 
                 sums, g = share(c, dys, p)
                 for row in range(SUMS):
@@ -116,9 +116,34 @@
                 acc_ref[at] = acc_ref[at] + jnp.sum(accs[i * SUMS + row], axis=0, keepdims=True)
 
 
-def near_kernel(core_ref, dy_ref, swap_ref, first, fwd, rev, filters_ref, mixing_ref, acc_ref, part_ref, coef_ref):
+def split_kernel(dy_ref, head_ref, tail_ref, sems):
+    head = head_ref.shape[0]
+    copies = [
+        pltpu.make_async_copy(dy_ref.at[pl.ds(0, head)], head_ref, sems.at[0]),
+        pltpu.make_async_copy(dy_ref.at[pl.ds(head, tail_ref.shape[0])], tail_ref, sems.at[1]),
+    ]
+    for copy in copies:
+        copy.start()
+    for copy in copies:
+        copy.wait()
+
+
+def near_kernel(core_ref, swap_ref, dy_hbm, first, fwd, rev, filters_hbm, mixing_hbm, acc_ref, part_ref, coef_ref, par_ref, saved, dy_ref, filters_ref, mixing_ref, sems):
+    moves = [
+        (filters_hbm, filters_ref),
+        (mixing_hbm, mixing_ref),
+        (dy_hbm, dy_ref),
+        (first, saved.at[0]),
+        (fwd, saved.at[pl.ds(1, LEVELS - 1)]),
+        (rev, saved.at[pl.ds(LEVELS, LEVELS - 1)]),
+    ]
+    copies = [pltpu.make_async_copy(a, b, sems.at[i]) for i, (a, b) in enumerate(moves)]
+    for copy in copies:
+        copy.start()
     core = core_ref[0]
     acc_ref[...] = jnp.zeros_like(acc_ref)
+    for copy in copies[:2]:
+        copy.wait()
     for b in range(2):
         f = [[filters_ref[b, i, pl.ds(j, 1), :] for j in range(2)] for i in range(2)]
         mix = [mixing_ref[i, pl.ds(b, 1), :] for i in range(LEVELS + 1)]
@@ -131,6 +156,10 @@
             c[CD + level] = f[1][0] * mix[level]
         for i in range(COEFS):
             coef_ref[b, i] = jnp.broadcast_to(c[i], coef_ref.shape[2:])
+        for i, value in enumerate([*f[0], *f[1], *mix]):
+            par_ref[i, pl.ds(b, 1), :] = value
+    for copy in copies[2:]:
+        copy.wait()
 
     def keep(n, r, cols, value):
         part_ref[rows_of(0, n, r), cols] = value
@@ -138,13 +167,13 @@
     def side(b):
         own, both = [(dy_ref, 0)], [(dy_ref, 0), (swap_ref, NB)]
         work = [(b, both), (1 - b, own)]
-        run(work, first, (fwd, rev), coef_ref, acc_ref, lambda n, r, cols: None, keep)
+        run(work, saved, coef_ref, acc_ref, lambda n, r, cols: None, keep)
 
     for b in range(2):
         pl.when(core == b)(lambda b=b: side(b))
 
 
-def far_kernel(right_ref, left_ref, first, fwd, rev, coef_ref, near_ref, part_ref, acc_ref, out_ref):
+def far_kernel(right_ref, left_ref, saved, coef_ref, near_ref, part_ref, acc_ref, out_ref):
     acc_ref[...] = near_ref[...]
 
     def start(n, r, cols):
@@ -154,10 +183,10 @@
         out_ref[rows_of(0, n, r), cols] = value
 
     work = [(0, [(right_ref, 2 * NB)]), (1, [(left_ref, 2 * NB)])]
-    run(work, first, (fwd, rev), coef_ref, acc_ref, start, keep)
-
-
-def last_kernel(core_ref, relay_ref, first, fwd, rev, filters_ref, mixing_ref, coef_ref, far_ref, part_ref, sums_ref, grad_ref, acc_ref):
+    run(work, saved, coef_ref, acc_ref, start, keep)
+
+
+def last_kernel(core_ref, relay_ref, saved, par_ref, coef_ref, far_ref, part_ref, sums_ref, grad_ref, acc_ref):
     core = core_ref[0]
     acc_ref[...] = far_ref[...]
 
@@ -170,10 +199,10 @@
     for b in range(2):
         work = [(b, [(relay_ref, NB)])]
         pl.when(core == 1 - b)(
-            lambda work=work: run(work, first, (fwd, rev), coef_ref, acc_ref, start, keep)
+            lambda work=work: run(work, saved, coef_ref, acc_ref, start, keep)
         )
-    f = [[filters_ref[:, i, j, :] for j in range(2)] for i in range(2)]
-    mix = [mixing_ref[i] for i in range(LEVELS + 1)]
+    f = [[par_ref[2 * i + j] for j in range(2)] for i in range(2)]
+    mix = [par_ref[4 + i] for i in range(LEVELS + 1)]
     acc = [acc_ref[:, i, :] for i in range(SUMS)]
     s, t = acc[SY : SY + LEVELS], acc[TY : TY + LEVELS]
     sums = [
@@ -187,7 +216,9 @@
     for copy in range(sums_ref.shape[0]):
         for b in range(2):
             for j, value in enumerate(sums):
-                sums_ref[copy, pl.ds(b * 9 + j, 1), :] = value[b : b + 1]
+                for h in range(2):
+                    at = 2 * (b * 9 + j) + h
+                    sums_ref[copy, pl.ds(at, 1), :] = value[b : b + 1, h * LANES : (h + 1) * LANES]
 
 
 def finish_kernel(factor, got_ref, filters_ref, mixing_ref):
@@ -196,23 +227,24 @@
         total = total + got_ref[i]
     total = total * factor
     for b in range(2):
-        for i in range(2):
-            for j in range(2):
-                at = b * 9 + i * 2 + j
-                filters_ref[b, i, pl.ds(j, 1), :] = total[at : at + 1]
-        for i in range(LEVELS + 1):
-            at = b * 9 + 4 + i
-            mixing_ref[i, pl.ds(b, 1), :] = total[at : at + 1]
-
-
-def call(kernel, name, outs, args, scratch=(), flops=0):
-    smem = args[0].dtype == jnp.int32
-    vmem = pl.BlockSpec(memory_space=pltpu.VMEM)
+        for j in range(9):
+            for h in range(2):
+                row = total[2 * (b * 9 + j) + h : 2 * (b * 9 + j) + h + 1]
+                cols = pl.ds(h * LANES, LANES)
+                if j < 4:
+                    filters_ref[b, j // 2, pl.ds(j % 2, 1), cols] = row
+                else:
+                    mixing_ref[j - 4, pl.ds(b, 1), cols] = row
+
+
+def call(kernel, name, outs, args, spaces, scratch=(), flops=0):
+    space = {"s": pltpu.SMEM, "v": pltpu.VMEM, "h": pltpu.HBM}
+    args = [pltpu.with_memory_space_constraint(a, pltpu.HBM) if k == "h" else a for a, k in zip(args, spaces)]
     return pl.pallas_call(
         kernel,
         out_shape=outs,
-        in_specs=[pl.BlockSpec(memory_space=pltpu.SMEM) if i == 0 and smem else vmem for i in range(len(args))],
-        out_specs=(vmem,) * len(outs),
+        in_specs=[pl.BlockSpec(memory_space=space[k]) for k in spaces],
+        out_specs=(pl.BlockSpec(memory_space=pltpu.VMEM),) * len(outs),
         scratch_shapes=scratch,
         compiler_params=pltpu.CompilerParams(vmem_limit_bytes=24 * 1024 * 1024),
         cost_estimate=pl.CostEstimate(flops=flops, bytes_accessed=6_000_000, transcendentals=0),
@@ -220,9 +252,21 @@
     )(*args)
 
 
-def route(value, axes, size, distance):
-    pairs = [(i - distance, i) for i in range(size) if 0 <= i - distance < size]
-    return lax.ppermute(value, axes, pairs)
+def routes():
+    zs, ys, cores = (lax.axis_size(axis) for axis in CTX)
+
+    def at(z, y, c):
+        return (z * ys + y) * cores + c
+
+    spots = [(z, c) for z in range(zs) for c in range(cores)]
+    inner = [(at(z, y, c), at(z, y + 1, c)) for z, c in spots for y in range(ys - 1)]
+    cross = [(at(z, ys - 1, c), at(z + 1, 0, c)) for z, c in spots if z + 1 < zs]
+    hop = [(at(z, ys - 1, c), at(z + 1, ys - 1, c)) for z, c in spots if z + 1 < zs]
+    hop += [(at(z + 1, 0, c), at(z, 0, c)) for z, c in spots if z + 1 < zs]
+    turn_left = [(at(z + 1, ys - 1, c), at(z + 1, 0, c)) for z, c in spots if z + 1 < zs]
+    turn_right = [(at(z, 0, c), at(z, ys - 1, c)) for z, c in spots if z + 1 < zs]
+    back = [(b, a) for a, b in inner]
+    return hop, inner + cross, back + [(b, a) for a, b in cross], inner + turn_left, back + turn_right
 
 
 def body(level_input, saved_forward, saved_reverse, filters, mixing, cotangent):
@@ -233,35 +277,66 @@
     core_id = core.astype(jnp.int32).reshape(1)
     dy = cotangent[0]
     mixing = jnp.swapaxes(mixing, 0, 1)
-    inputs = (level_input[0], saved_forward[:, 0], saved_reverse[:, 0])
     acc = jax.ShapeDtypeStruct((2, ROWS, width), F32)
     part = jax.ShapeDtypeStruct((rows, width), F32)
-    right = route(dy, CTX, ctx, -2)
-    left = route(dy, CTX, ctx, 2)
-    swap = lax.ppermute(dy, "core", [(0, 1), (1, 0)])
-    acc_near, part_near, coef = call(
+    pair = [(0, 1), (1, 0)]
+    hop, left_tail, right_tail, left_head, right_head = routes()
+    head, tail = call(
+        split_kernel,
+        "split",
+        tuple(jax.ShapeDtypeStruct((n, width), dy.dtype) for n in (HEAD, rows - HEAD)),
+        (dy,),
+        "h",
+        scratch=[pltpu.SemaphoreType.DMA((2,))],
+    )
+    dy, head, tail = lax.optimization_barrier((dy, head, tail))
+    hopped = lax.ppermute(head, CTX, hop)
+    left5 = lax.ppermute(tail, CTX, left_tail)
+    right5 = lax.ppermute(tail, CTX, right_tail)
+    swap = lax.ppermute(dy, "core", pair)
+    row = lax.axis_index("y")
+    left3 = lax.ppermute(jnp.where(row == lax.axis_size("y") - 1, hopped, head), CTX, left_head)
+    right3 = lax.ppermute(jnp.where(row == 0, hopped, head), CTX, right_head)
+    acc_near, part_near, coef, par, saved = call(
         near_kernel,
         "near",
-        (acc, part, jax.ShapeDtypeStruct((2, COEFS, STEP // 2, width), F32)),
-        (core_id, dy, swap, *inputs, filters, mixing),
-        flops=100_000_000,
-    )
-    right, left, acc_near = lax.optimization_barrier((right, left, acc_near))
-    relay = lax.ppermute(jnp.where(core == 0, right, left), "core", [(0, 1), (1, 0)])
+        (
+            acc,
+            part,
+            jax.ShapeDtypeStruct((2, COEFS, STEP // 2, width), F32),
+            jax.ShapeDtypeStruct((LEVELS + 5, 2, width), F32),
+            jax.ShapeDtypeStruct((2 * LEVELS - 1, rows, width), dy.dtype),
+        ),
+        (core_id, swap, dy, level_input[0], saved_forward[:, 0], saved_reverse[:, 0], filters, mixing),
+        "svhhhhhh",
+        scratch=[
+            pltpu.VMEM((rows, width), dy.dtype),
+            pltpu.VMEM(filters.shape, F32),
+            pltpu.VMEM(mixing.shape, F32),
+            pltpu.SemaphoreType.DMA((6,)),
+        ],
+        flops=20_000_000,
+    )
+    left3, left5, right3, right5, acc_near = lax.optimization_barrier((left3, left5, right3, right5, acc_near))
+    left = jnp.concatenate([left3, left5])
+    right = jnp.concatenate([right3, right5])
+    relay = lax.ppermute(jnp.where(core == 0, right, left), "core", pair)
     acc_far, part_far = call(
         far_kernel,
         "far",
         (acc, part),
-        (right, left, *inputs, coef, acc_near, part_near),
-        flops=100_000_000,
+        (right, left, saved, coef, acc_near, part_near),
+        "vvvvvv",
+        flops=20_000_000,
     )
     sums, grad = call(
         last_kernel,
         "last",
-        (jax.ShapeDtypeStruct((8, 18, width), F32), jax.ShapeDtypeStruct((rows, width), jnp.bfloat16)),
-        (core_id, relay, *inputs, filters, mixing, coef, acc_far, part_far),
+        (jax.ShapeDtypeStruct((8, 18 * width // LANES, LANES), F32), jax.ShapeDtypeStruct((rows, width), jnp.bfloat16)),
+        (core_id, relay, saved, par, coef, acc_far, part_far),
+        "svvvvvv",
         scratch=[pltpu.VMEM((2, ROWS, width), F32)],
-        flops=100_000_000,
+        flops=20_000_000,
     )
     groups = (("x", "core"), ("y",), ("zl", "zh"))
     for i, axes in enumerate(groups):
@@ -274,6 +349,7 @@
         "finish",
         (jax.ShapeDtypeStruct(filters.shape, F32), jax.ShapeDtypeStruct(mixing.shape, F32)),
         (got,),
+        "v",
     )
     return grad[None], grad_filters, jnp.swapaxes(grad_mixing, 0, 1)
 

time: 87.5 us -> 82.4 us (0.942)
  blocking collectives: 59.6 us -> 46.1 us
  starting transfers between devices: 9.71 us -> 17.8 us
  local copies, waits for them, and re-layouts: 6.33 us -> 0.1 us
  Pallas kernels: 8.47 us -> 11.8 us
  waiting for transfers between devices: 1.97 us -> 5.18 us
    all_to_all x3, blocking collectives: 59.6 us -> 46.1 us  [body(): got = lax.all_to_all(sums, axes, 0, 0)]
    ppermute x4 -> x7, starting transfers between devices: 9.71 us -> 17.8 us  [the longest x1 7.15 us: body(): right3 = lax.ppermute(jnp.where(row == 0, hopped, head), CTX, right_head)]
    unnamed x16 -> x2, local copies, waits for them, and re-layouts: 6.3 us -> 0.03 us
    pallas_call x4 -> x5, Pallas kernels: 8.47 us -> 11.8 us  [call(): pl.pallas_call(kernel, out_shape=outs, in_specs=[pl.BlockSpec(memory_spac...]
    ppermute x4 -> x7, waiting for transfers between devices: 1.97 us -> 5.18 us  [the longest x1 4.71 us: body(): hopped = lax.ppermute(head, CTX, hop)]
  transfers between devices with their start and end apart: 4 -> 7, of which waited for: 3 -> 2; matrix products, arithmetic and copies ran while one was open for 0% -> 0% of each run, Pallas kernels for 6% -> 9%
where the time goes in v3:
time: 82.4 us; the launch traced here: 81.9 us
  blocking collectives  46.1 us (56%)
  starting transfers between devices  17.8 us (22%)
  Pallas kernels  11.8 us (14%)
  waiting for transfers between devices  5.18 us (6%)
    all_to_all x3, blocking collectives, body(): got = lax.all_to_all(sums, axes, 0, 0)  46.1 us
    pallas_call x5, Pallas kernels, call(): pl.pallas_call(kernel, out_shape=outs, in_specs=[pl.BlockSpec(memory_spac...  11.8 us
    ppermute x1, starting transfers between devices, body(): right3 = lax.ppermute(jnp.where(row == 0, hopped, head), CTX, right_head)  7.15 us
    ppermute x1, waiting for transfers between devices, body(): hopped = lax.ppermute(head, CTX, hop)  4.71 us
    ppermute x1, starting transfers between devices, body(): left5 = lax.ppermute(tail, CTX, left_tail)  2.88 us
    ppermute x1, starting transfers between devices, body(): swap = lax.ppermute(dy, 'core', pair)  1.92 us
    ppermute x1, starting transfers between devices, body(): relay = lax.ppermute(jnp.where(core == 0, right, left), 'core', pair)  1.92 us
  transfers between devices with their start and end apart: 7, of which 2 were waited for; matrix products, arithmetic and copies ran while one was open for 0% of the time, Pallas kernels for 9%

profile of v3, /device:TPU:64, one launch (start us, length us, event | category | flops | bytes accessed | tf_op | source)
XLA Modules:
  0.0 81.9 jit_solution(950143419316909373)
XLA Ops:
  0.6 1.1 %split.1 = (bf16[384,256]{1,0:T(8,128)(2,1)S(1)}, bf16[640,256]{1,0:T(8,128)(2,1)S(1)}) custom-call(bf16[1024,256]{1,0:T(8,128)(2,1)} %bitcast.8), custom_call_target="tpu_custom_call" | custom-call | bytes 6000000 | tf_op jit(solution)/shard_map/split/pallas_call | solution.py:243
  1.7 1.3 %collective-permute-start = (bf16[384,256]{1,0:T(8,128)(2,1)S(1)}, bf16[384,256]{1,0:T(8,128)(2,1)S(1)}, u32[]{:S(2)}, u32[]{:S(2)}) collective-permute-start(bf16[384,256]{1,0:T(8,128)(2,1)S(1)} %get-tuple-element.26), channel_id=1, source_target_pairs={{14,30},{15,31},{30,46},{31,47},{46,62},{47,63},{16,0},{17,1},{32,... | collective-permute-start | bytes 589832 | tf_op jit(solution)/shard_map/ppermute | solution.py:293
  3.0 1.9 %collective-permute-start.5 = (bf16[1024,256]{1,0:T(8,128)(2,1)}, bf16[1024,256]{1,0:T(8,128)(2,1)S(1)}, u32[]{:S(2)}, u32[]{:S(2)}) collective-permute-start(bf16[1024,256]{1,0:T(8,128)(2,1)} %bitcast.9), channel_id=1, source_target_pairs={{0,1},{1,0},{2,3},{3,2},{4,5},{5,4},{6,7},{7,6},{8,9},{9,8},{10,11... | collective-permute-start | bytes 1572872 | tf_op jit(solution)/shard_map/ppermute | solution.py:296
  5.0 2.9 %collective-permute-start.2 = (bf16[640,256]{1,0:T(8,128)(2,1)S(1)}, bf16[640,256]{1,0:T(8,128)(2,1)S(1)}, u32[]{:S(2)}, u32[]{:S(2)}) collective-permute-start(bf16[640,256]{1,0:T(8,128)(2,1)S(1)} %get-tuple-element.27), channel_id=1, source_target_pairs={{0,2},{2,4},{4,6},{6,8},{8,10},{10,12},{12,14},{1,3},{3,5},{5,7},{... | collective-permute-start | bytes 983048 | tf_op jit(solution)/shard_map/ppermute | solution.py:294
  7.9 1.3 %collective-permute-start.4 = (bf16[640,256]{1,0:T(8,128)(2,1)S(1)}, bf16[640,256]{1,0:T(8,128)(2,1)S(1)}, u32[]{:S(2)}, u32[]{:S(2)}) collective-permute-start(bf16[640,256]{1,0:T(8,128)(2,1)S(1)} %get-tuple-element.27), channel_id=1, source_target_pairs={{2,0},{4,2},{6,4},{8,6},{10,8},{12,10},{14,12},{3,1},{5,3},{7,5},{... | collective-permute-start | bytes 983048 | tf_op jit(solution)/shard_map/ppermute | solution.py:295
  9.2 4.7 %collective-permute-done = bf16[384,256]{1,0:T(8,128)(2,1)S(1)} collective-permute-done((bf16[384,256]{1,0:T(8,128)(2,1)S(1)}, bf16[384,256]{1,0:T(8,128)(2,1)S(1)}, u32[]{:S(2)}, u32[]{:S(2)}) %collective-permute-start) | collective-permute-done | bytes 196640 | tf_op jit(solution)/shard_map/ppermute | solution.py:293
  13.9 1.3 %collective-permute-start.1 = (bf16[384,256]{1,0:T(8,128)(2,1)S(1)}, bf16[384,256]{1,0:T(8,128)(2,1)S(1)}, u32[]{:S(2)}, u32[]{:S(2)}) collective-permute-start(bf16[384,256]{1,0:T(8,128)(2,1)S(1)} %get-tuple-element.46), channel_id=1, source_target_pairs={{0,2},{2,4},{4,6},{6,8},{8,10},{10,12},{12,14},{1,3},{3,5},{5,7},{... | collective-permute-start | bytes 589832 | tf_op jit(solution)/shard_map/ppermute | solution.py:298
  15.2 7.2 %collective-permute-start.3 = (bf16[384,256]{1,0:T(8,128)(2,1)S(1)}, bf16[384,256]{1,0:T(8,128)(2,1)S(1)}, u32[]{:S(2)}, u32[]{:S(2)}) collective-permute-start(bf16[384,256]{1,0:T(8,128)(2,1)S(1)} %get-tuple-element.45), channel_id=1, source_target_pairs={{2,0},{4,2},{6,4},{8,6},{10,8},{12,10},{14,12},{3,1},{5,3},{7,5},{... | collective-permute-start | bytes 589832 | tf_op jit(solution)/shard_map/ppermute | solution.py:299
  22.4 0.0 collective-permute-done.5.swap_ref
  22.4 6.2 %near.1 = (f32[2,16,256]{2,1,0:T(8,128)S(1)}, f32[1024,256]{1,0:T(8,128)S(1)}, f32[2,10,8,256]{3,2,1,0:T(8,128)S(1)}, f32[9,2,256]{2,1,0:T(2,128)S(1)}, bf16[7,1024,256]{2,1,0:T(8,128)(2,1)S(1)}) custom-call(s32[1]{0:T(128)} %bitcast.core_ref, bf16[1024,256]{1,0:T(8,128)(2,1)S(1)} %collective-permute-done.5.swap_ref, bf16[1024,256]{1,0:T(8,128)(2,1)} %bitcast.10, ...), custom_call_target="tpu_custom_call" | custom-call | flops 20000000 | bytes 6000000 | tf_op jit(solution)/shard_map/near/pallas_call | solution.py:243
  28.6 0.0 collective-permute-done.2
  28.6 0.0 collective-permute-done.4
  28.6 0.0 collective-permute-done.1
  28.7 0.0 collective-permute-done.3
  28.8 0.1 broadcast_select_fusion
  28.8 1.9 %collective-permute-start.6 = (bf16[1024,256]{1,0:T(8,128)(2,1)S(1)}, bf16[1024,256]{1,0:T(8,128)(2,1)S(1)}, u32[]{:S(2)}, u32[]{:S(2)}) collective-permute-start(bf16[1024,256]{1,0:T(8,128)(2,1)S(1)} %broadcast_select_fusion), channel_id=1, source_target_pairs={{0,1},{1,0},{2,3},{3,2},{4,5},{5,4},{6,7},{7,6},{8,9},{9,8},{10,11... | collective-permute-start | bytes 1572872 | tf_op jit(solution)/shard_map/ppermute | solution.py:323
  30.8 1.4 %far.1 = (f32[2,16,256]{2,1,0:T(8,128)S(1)}, f32[1024,256]{1,0:T(8,128)S(1)}) custom-call(bf16[1024,256]{1,0:T(8,128)(2,1)S(1)} %get-tuple-element.47.right_ref, bf16[1024,256]{1,0:T(8,128)(2,1)S(1)} %get-tuple-element.48.left_ref, bf16[7,1024,256]{2,1,0:T(8,128)(2,1)S(1)} %get-tuple-element.34.saved, f32[2,10,8,256]{3,2,1,0:T(8,128)S(1)} %get-tuple-element.36.coef_ref, ...), custom_call_target="tpu_custom_call" | custom-call | flops 20000000 | bytes 6000000 | tf_op jit(solution)/shard_map/far/pallas_call | solution.py:243
  32.2 0.5 collective-permute-done.6.relay_ref
  32.6 2.5 %last.1 = (f32[8,36,128]{2,1,0:T(8,128)S(1)}, bf16[1024,256]{1,0:T(8,128)(2,1)}) custom-call(s32[1]{0:T(128)} %bitcast.core_ref, bf16[1024,256]{1,0:T(8,128)(2,1)S(1)} %collective-permute-done.6.relay_ref, bf16[7,1024,256]{2,1,0:T(8,128)(2,1)S(1)} %get-tuple-element.34.saved, f32[9,2,256]{2,1,0:T(2,128)S(1)} %get-tuple-element.35.par_ref, ...), custom_call_target="tpu_custom_call" | custom-call | flops 20000000 | bytes 6000000 | tf_op jit(solution)/shard_map/last/pallas_call | solution.py:243
  35.1 10.6 %all_to_all.15 = f32[8,36,128]{2,1,0:T(8,128)S(1)} all-to-all(f32[8,36,128]{2,1,0:T(8,128)S(1)} %get-tuple-element.42), channel_id=1, replica_groups=mesh['x'=4,'zl'=2,'zh'=4,'y'=8,'core'=2] {'x','core'}, dimensions={0} | all-to-all | bytes 294912 | tf_op jit(solution)/shard_map/all_to_all | solution.py:343
  45.7 18.6 %all_to_all.16 = f32[8,36,128]{2,1,0:T(8,128)S(1)} all-to-all(f32[8,36,128]{2,1,0:T(8,128)S(1)} %broadcast_in_dim.7), channel_id=1, replica_groups=mesh['x'=4,'zl'=2,'zh'=4,'y'=8,'core'=2] {'y'}, dimensions={0} | all-to-all | bytes 294912 | tf_op jit(solution)/shard_map/all_to_all | solution.py:343
  64.4 17.0 %all_to_all.17.refs_0_ = f32[8,36,128]{2,1,0:T(8,128)S(1)} all-to-all(f32[8,36,128]{2,1,0:T(8,128)S(1)} %broadcast_in_dim.8), channel_id=1, replica_groups=mesh['x'=4,'zl'=2,'zh'=4,'y'=8,'core'=2] {'zl','zh'}, dimensions={0} | all-to-all | bytes 294912 | tf_op jit(solution)/shard_map/all_to_all | solution.py:343
  81.3 0.6 finish.1
  (8 shorter events, 0.2 us)
Async XLA Ops:
  1.7 12.1 %collective-permute-start = (bf16[384,256]{1,0:T(8,128)(2,1)S(1)}, bf16[384,256]{1,0:T(8,128)(2,1)S(1)}, u32[]{:S(2)}, u32[]{:S(2)}) collective-permute-start(bf16[384,256]{1,0:T(8,128)(2,1)S(1)} %get-tuple-element.26), channel_id=1, source_target_pairs={{14,30},{15,31},{30,46},{31,47},{46,62},{47,63},{16,0},{17,1},{32,... | collective-permute-start | bytes 589832 | tf_op jit(solution)/shard_map/ppermute | solution.py:293
  3.0 19.3 %collective-permute-start.5 = (bf16[1024,256]{1,0:T(8,128)(2,1)}, bf16[1024,256]{1,0:T(8,128)(2,1)S(1)}, u32[]{:S(2)}, u32[]{:S(2)}) collective-permute-start(bf16[1024,256]{1,0:T(8,128)(2,1)} %bitcast.9), channel_id=1, source_target_pairs={{0,1},{1,0},{2,3},{3,2},{4,5},{5,4},{6,7},{7,6},{8,9},{9,8},{10,11... | collective-permute-start | bytes 1572872 | tf_op jit(solution)/shard_map/ppermute | solution.py:296
  5.0 23.7 %collective-permute-start.2 = (bf16[640,256]{1,0:T(8,128)(2,1)S(1)}, bf16[640,256]{1,0:T(8,128)(2,1)S(1)}, u32[]{:S(2)}, u32[]{:S(2)}) collective-permute-start(bf16[640,256]{1,0:T(8,128)(2,1)S(1)} %get-tuple-element.27), channel_id=1, source_target_pairs={{0,2},{2,4},{4,6},{6,8},{8,10},{10,12},{12,14},{1,3},{3,5},{5,7},{... | collective-permute-start | bytes 983048 | tf_op jit(solution)/shard_map/ppermute | solution.py:294
  7.9 20.8 %collective-permute-start.4 = (bf16[640,256]{1,0:T(8,128)(2,1)S(1)}, bf16[640,256]{1,0:T(8,128)(2,1)S(1)}, u32[]{:S(2)}, u32[]{:S(2)}) collective-permute-start(bf16[640,256]{1,0:T(8,128)(2,1)S(1)} %get-tuple-element.27), channel_id=1, source_target_pairs={{2,0},{4,2},{6,4},{8,6},{10,8},{12,10},{14,12},{3,1},{5,3},{7,5},{... | collective-permute-start | bytes 983048 | tf_op jit(solution)/shard_map/ppermute | solution.py:295
  13.9 14.7 %collective-permute-start.1 = (bf16[384,256]{1,0:T(8,128)(2,1)S(1)}, bf16[384,256]{1,0:T(8,128)(2,1)S(1)}, u32[]{:S(2)}, u32[]{:S(2)}) collective-permute-start(bf16[384,256]{1,0:T(8,128)(2,1)S(1)} %get-tuple-element.46), channel_id=1, source_target_pairs={{0,2},{2,4},{4,6},{6,8},{8,10},{10,12},{12,14},{1,3},{3,5},{5,7},{... | collective-permute-start | bytes 589832 | tf_op jit(solution)/shard_map/ppermute | solution.py:298
  15.2 13.4 %collective-permute-start.3 = (bf16[384,256]{1,0:T(8,128)(2,1)S(1)}, bf16[384,256]{1,0:T(8,128)(2,1)S(1)}, u32[]{:S(2)}, u32[]{:S(2)}) collective-permute-start(bf16[384,256]{1,0:T(8,128)(2,1)S(1)} %get-tuple-element.45), channel_id=1, source_target_pairs={{2,0},{4,2},{6,4},{8,6},{10,8},{12,10},{14,12},{3,1},{5,3},{7,5},{... | collective-permute-start | bytes 589832 | tf_op jit(solution)/shard_map/ppermute | solution.py:299
  28.8 3.8 %collective-permute-start.6 = (bf16[1024,256]{1,0:T(8,128)(2,1)S(1)}, bf16[1024,256]{1,0:T(8,128)(2,1)S(1)}, u32[]{:S(2)}, u32[]{:S(2)}) collective-permute-start(bf16[1024,256]{1,0:T(8,128)(2,1)S(1)} %broadcast_select_fusion), channel_id=1, source_target_pairs={{0,1},{1,0},{2,3},{3,2},{4,5},{5,4},{6,7},{7,6},{8,9},{9,8},{10,11... | collective-permute-start | bytes 1572872 | tf_op jit(solution)/shard_map/ppermute | solution.py:323

commit v4 on v3

--- a/solution.py
+++ b/solution.py
@@ -128,7 +128,7 @@
         copy.wait()
 
 
-def near_kernel(core_ref, swap_ref, dy_hbm, first, fwd, rev, filters_hbm, mixing_hbm, acc_ref, part_ref, coef_ref, par_ref, saved, dy_ref, filters_ref, mixing_ref, sems):
+def near_kernel(dy_hbm, first, fwd, rev, filters_hbm, mixing_hbm, acc_ref, part_ref, coef_ref, par_ref, saved, dy_ref, filters_ref, mixing_ref, sems):
     moves = [
         (filters_hbm, filters_ref),
         (mixing_hbm, mixing_ref),
@@ -140,7 +140,6 @@
     copies = [pltpu.make_async_copy(a, b, sems.at[i]) for i, (a, b) in enumerate(moves)]
     for copy in copies:
         copy.start()
-    core = core_ref[0]
     acc_ref[...] = jnp.zeros_like(acc_ref)
     for copy in copies[:2]:
         copy.wait()
@@ -164,16 +163,12 @@
     def keep(n, r, cols, value):
         part_ref[rows_of(0, n, r), cols] = value
 
-    def side(b):
-        own, both = [(dy_ref, 0)], [(dy_ref, 0), (swap_ref, NB)]
-        work = [(b, both), (1 - b, own)]
-        run(work, saved, coef_ref, acc_ref, lambda n, r, cols: None, keep)
-
-    for b in range(2):
-        pl.when(core == b)(lambda b=b: side(b))
-
-
-def far_kernel(right_ref, left_ref, saved, coef_ref, near_ref, part_ref, acc_ref, out_ref):
+    work = [(0, [(dy_ref, 0)]), (1, [(dy_ref, 0)])]
+    run(work, saved, coef_ref, acc_ref, lambda n, r, cols: None, keep)
+
+
+def far_kernel(core_ref, swap_ref, right_ref, left_ref, saved, coef_ref, near_ref, part_ref, acc_ref, out_ref):
+    core = core_ref[0]
     acc_ref[...] = near_ref[...]
 
     def start(n, r, cols):
@@ -182,8 +177,11 @@
     def keep(n, r, cols, value):
         out_ref[rows_of(0, n, r), cols] = value
 
-    work = [(0, [(right_ref, 2 * NB)]), (1, [(left_ref, 2 * NB)])]
-    run(work, saved, coef_ref, acc_ref, start, keep)
+    for b in range(2):
+        far = [[(right_ref, 2 * NB)], [(left_ref, 2 * NB)]]
+        far[b] = [(swap_ref, NB)] + far[b]
+        work = list(enumerate(far))
+        pl.when(core == b)(lambda work=work: run(work, saved, coef_ref, acc_ref, start, keep))
 
 
 def last_kernel(core_ref, relay_ref, saved, par_ref, coef_ref, far_ref, part_ref, sums_ref, grad_ref, acc_ref):
@@ -213,12 +211,13 @@
         *(f[1][0] * s[i] + f[1][1] * t[i] for i in range(LEVELS)),
         f[0][0] * s[3] + f[0][1] * t[3],
     ]
-    for copy in range(sums_ref.shape[0]):
-        for b in range(2):
-            for j, value in enumerate(sums):
-                for h in range(2):
-                    at = 2 * (b * 9 + j) + h
-                    sums_ref[copy, pl.ds(at, 1), :] = value[b : b + 1, h * LANES : (h + 1) * LANES]
+    for b in range(2):
+        for j, value in enumerate(sums):
+            for h in range(2):
+                at = 2 * (b * 9 + j) + h
+                sums_ref[0, pl.ds(at, 1), :] = value[b : b + 1, h * LANES : (h + 1) * LANES]
+    for copy in range(1, sums_ref.shape[0]):
+        sums_ref[copy] = sums_ref[0]
 
 
 def finish_kernel(factor, got_ref, filters_ref, mixing_ref):
@@ -259,14 +258,16 @@
         return (z * ys + y) * cores + c
 
     spots = [(z, c) for z in range(zs) for c in range(cores)]
-    inner = [(at(z, y, c), at(z, y + 1, c)) for z, c in spots for y in range(ys - 1)]
-    cross = [(at(z, ys - 1, c), at(z + 1, 0, c)) for z, c in spots if z + 1 < zs]
-    hop = [(at(z, ys - 1, c), at(z + 1, ys - 1, c)) for z, c in spots if z + 1 < zs]
-    hop += [(at(z + 1, 0, c), at(z, 0, c)) for z, c in spots if z + 1 < zs]
-    turn_left = [(at(z + 1, ys - 1, c), at(z + 1, 0, c)) for z, c in spots if z + 1 < zs]
-    turn_right = [(at(z, 0, c), at(z, ys - 1, c)) for z, c in spots if z + 1 < zs]
-    back = [(b, a) for a, b in inner]
-    return hop, inner + cross, back + [(b, a) for a, b in cross], inner + turn_left, back + turn_right
+    seams = [(z, c) for z, c in spots if z + 1 < zs]
+    end = ys - 1
+    inner = [(at(z, y, c), at(z, y + 1, c)) for z, c in spots for y in range(end)]
+    cross = [(at(z, end, c), at(z + 1, 0, c)) for z, c in seams]
+    cross += [(at(z + 1, 0, c), at(z, end, c)) for z, c in seams]
+    hop = [(at(z, end, c), at(z + 1, end, c)) for z, c in seams]
+    hop += [(at(z + 1, 0, c), at(z, 0, c)) for z, c in seams]
+    turn = [(at(z + 1, end, c), at(z + 1, 0, c)) for z, c in seams]
+    turn += [(at(z, 0, c), at(z, end, c)) for z, c in seams]
+    return inner, cross, hop, turn
 
 
 def body(level_input, saved_forward, saved_reverse, filters, mixing, cotangent):
@@ -280,7 +281,7 @@
     acc = jax.ShapeDtypeStruct((2, ROWS, width), F32)
     part = jax.ShapeDtypeStruct((rows, width), F32)
     pair = [(0, 1), (1, 0)]
-    hop, left_tail, right_tail, left_head, right_head = routes()
+    inner, cross, hop, turn = routes()
     head, tail = call(
         split_kernel,
         "split",
@@ -289,14 +290,13 @@
         "h",
         scratch=[pltpu.SemaphoreType.DMA((2,))],
     )
-    dy, head, tail = lax.optimization_barrier((dy, head, tail))
     hopped = lax.ppermute(head, CTX, hop)
-    left5 = lax.ppermute(tail, CTX, left_tail)
-    right5 = lax.ppermute(tail, CTX, right_tail)
+    crossed = lax.ppermute(tail, CTX, cross)
+    left = lax.ppermute(dy, CTX, inner)
+    right = lax.ppermute(dy, CTX, [(b, a) for a, b in inner])
     swap = lax.ppermute(dy, "core", pair)
-    row = lax.axis_index("y")
-    left3 = lax.ppermute(jnp.where(row == lax.axis_size("y") - 1, hopped, head), CTX, left_head)
-    right3 = lax.ppermute(jnp.where(row == 0, hopped, head), CTX, right_head)
+    own, hopped = lax.optimization_barrier((dy, hopped))
+    turned = lax.ppermute(hopped, CTX, turn)
     acc_near, part_near, coef, par, saved = call(
         near_kernel,
         "near",
@@ -307,8 +307,8 @@
             jax.ShapeDtypeStruct((LEVELS + 5, 2, width), F32),
             jax.ShapeDtypeStruct((2 * LEVELS - 1, rows, width), dy.dtype),
         ),
-        (core_id, swap, dy, level_input[0], saved_forward[:, 0], saved_reverse[:, 0], filters, mixing),
-        "svhhhhhh",
+        (own, level_input[0], saved_forward[:, 0], saved_reverse[:, 0], filters, mixing),
+        "hhhhhh",
         scratch=[
             pltpu.VMEM((rows, width), dy.dtype),
             pltpu.VMEM(filters.shape, F32),
@@ -317,16 +317,18 @@
         ],
         flops=20_000_000,
     )
-    left3, left5, right3, right5, acc_near = lax.optimization_barrier((left3, left5, right3, right5, acc_near))
-    left = jnp.concatenate([left3, left5])
-    right = jnp.concatenate([right3, right5])
+    left, right, turned, crossed, acc_near = lax.optimization_barrier((left, right, turned, crossed, acc_near))
+    row = lax.axis_index("y")
+    detour = jnp.concatenate([turned, crossed])
+    left = jnp.where(row == 0, detour, left)
+    right = jnp.where(row == lax.axis_size("y") - 1, detour, right)
     relay = lax.ppermute(jnp.where(core == 0, right, left), "core", pair)
     acc_far, part_far = call(
         far_kernel,
         "far",
         (acc, part),
-        (right, left, saved, coef, acc_near, part_near),
-        "vvvvvv",
+        (core_id, swap, right, left, saved, coef, acc_near, part_near),
+        "svvvvvvv",
         flops=20_000_000,
     )
     sums, grad = call(

time: 82.4 us -> 83.8 us (1.017)
  waiting for transfers between devices: 5.18 us -> 9.88 us
  blocking collectives: 46.1 us -> 41.8 us
  starting transfers between devices: 17.8 us -> 18.7 us
    ppermute x1, waiting for transfers between devices: 4.71 us -> 9.87 us  [body(): hopped = lax.ppermute(head, CTX, hop)]
    all_to_all x3, blocking collectives: 46.1 us -> 41.8 us  [body(): got = lax.all_to_all(sums, axes, 0, 0)]
  transfers between devices with their start and end apart: 7 -> 7, of which waited for: 2 -> 1; matrix products, arithmetic and copies ran while one was open for 0% -> 0% of each run, Pallas kernels for 9% -> 11%
where the time goes in v4:
time: 83.8 us; the launch traced here: 83.4 us
  blocking collectives  41.8 us (50%)
  starting transfers between devices  18.7 us (22%)
  Pallas kernels  12 us (14%)
  waiting for transfers between devices  9.88 us (12%)
    all_to_all x3, blocking collectives, body(): got = lax.all_to_all(sums, axes, 0, 0)  41.8 us
    pallas_call x5, Pallas kernels, call(): pl.pallas_call(kernel, out_shape=outs, in_specs=[pl.BlockSpec(memory_spac...  12 us
    ppermute x1, waiting for transfers between devices, body(): hopped = lax.ppermute(head, CTX, hop)  9.87 us
    ppermute x1, starting transfers between devices, body(): turned = lax.ppermute(hopped, CTX, turn)  7.6 us
    ppermute x1, starting transfers between devices, body(): left = lax.ppermute(dy, CTX, inner)  3.52 us
    ppermute x1, starting transfers between devices, body(): relay = lax.ppermute(jnp.where(core == 0, right, left), 'core', pair)  2.41 us
    ppermute x1, starting transfers between devices, body(): swap = lax.ppermute(dy, 'core', pair)  1.92 us
  transfers between devices with their start and end apart: 7, of which 1 were waited for; matrix products, arithmetic and copies ran while one was open for 0% of the time, Pallas kernels for 11%

profile of v4, /device:TPU:64, one launch (start us, length us, event | category | flops | bytes accessed | tf_op | source)
XLA Modules:
  0.0 83.4 jit_solution(5774259826040688668)
XLA Ops:
  0.6 3.5 %collective-permute-start = (bf16[1024,256]{1,0:T(8,128)(2,1)}, bf16[1024,256]{1,0:T(8,128)(2,1)S(1)}, u32[]{:S(2)}, u32[]{:S(2)}) collective-permute-start(bf16[1024,256]{1,0:T(8,128)(2,1)} %bitcast.8), channel_id=1, source_target_pairs={{0,2},{2,4},{4,6},{6,8},{8,10},{10,12},{12,14},{1,3},{3,5},{5,7},{... | collective-permute-start | bytes 1572872 | tf_op jit(solution)/shard_map/ppermute | solution.py:295
  4.2 1.3 %collective-permute-start.1 = (bf16[1024,256]{1,0:T(8,128)(2,1)}, bf16[1024,256]{1,0:T(8,128)(2,1)S(1)}, u32[]{:S(2)}, u32[]{:S(2)}) collective-permute-start(bf16[1024,256]{1,0:T(8,128)(2,1)} %bitcast.9), channel_id=1, source_target_pairs={{2,0},{4,2},{6,4},{8,6},{10,8},{12,10},{14,12},{3,1},{5,3},{7,5},{... | collective-permute-start | bytes 1572872 | tf_op jit(solution)/shard_map/ppermute | solution.py:296
  5.5 1.1 %split.1 = (bf16[384,256]{1,0:T(8,128)(2,1)S(1)}, bf16[640,256]{1,0:T(8,128)(2,1)S(1)}) custom-call(bf16[1024,256]{1,0:T(8,128)(2,1)} %bitcast.10), custom_call_target="tpu_custom_call" | custom-call | bytes 6000000 | tf_op jit(solution)/shard_map/split/pallas_call | solution.py:242
  6.6 1.3 %collective-permute-start.2 = (bf16[384,256]{1,0:T(8,128)(2,1)S(1)}, bf16[384,256]{1,0:T(8,128)(2,1)S(1)}, u32[]{:S(2)}, u32[]{:S(2)}) collective-permute-start(bf16[384,256]{1,0:T(8,128)(2,1)S(1)} %get-tuple-element.23), channel_id=1, source_target_pairs={{14,30},{15,31},{30,46},{31,47},{46,62},{47,63},{16,0},{17,1},{32,... | collective-permute-start | bytes 589832 | tf_op jit(solution)/shard_map/ppermute | solution.py:293
  7.9 0.7 collective-permute-start.4
  8.5 9.9 %collective-permute-done.2 = bf16[384,256]{1,0:T(8,128)(2,1)S(1)} collective-permute-done((bf16[384,256]{1,0:T(8,128)(2,1)S(1)}, bf16[384,256]{1,0:T(8,128)(2,1)S(1)}, u32[]{:S(2)}, u32[]{:S(2)}) %collective-permute-start.2) | collective-permute-done | bytes 196640 | tf_op jit(solution)/shard_map/ppermute | solution.py:293
  18.4 7.6 %collective-permute-start.3 = (bf16[384,256]{1,0:T(8,128)(2,1)S(1)}, bf16[384,256]{1,0:T(8,128)(2,1)S(1)}, u32[]{:S(2)}, u32[]{:S(2)}) collective-permute-start(bf16[384,256]{1,0:T(8,128)(2,1)S(1)} %collective-permute-done.2), channel_id=1, source_target_pairs={{30,16},{31,17},{46,32},{47,33},{62,48},{63,49},{0,14},{1,15},{16,... | collective-permute-start | bytes 589832 | tf_op jit(solution)/shard_map/ppermute | solution.py:299
  26.0 1.9 %collective-permute-start.6 = (bf16[1024,256]{1,0:T(8,128)(2,1)}, bf16[1024,256]{1,0:T(8,128)(2,1)S(1)}, u32[]{:S(2)}, u32[]{:S(2)}) collective-permute-start(bf16[1024,256]{1,0:T(8,128)(2,1)} %bitcast.11), channel_id=1, source_target_pairs={{0,1},{1,0},{2,3},{3,2},{4,5},{5,4},{6,7},{7,6},{8,9},{9,8},{10,11... | collective-permute-start | bytes 1572872 | tf_op jit(solution)/shard_map/ppermute | solution.py:297
  28.0 5.6 %near.1 = (f32[2,16,256]{2,1,0:T(8,128)S(1)}, f32[1024,256]{1,0:T(8,128)S(1)}, f32[2,10,8,256]{3,2,1,0:T(8,128)S(1)}, f32[9,2,256]{2,1,0:T(2,128)S(1)}, bf16[7,1024,256]{2,1,0:T(8,128)(2,1)S(1)}) custom-call(bf16[1024,256]{1,0:T(8,128)(2,1)} %bitcast.12, bf16[1024,256]{1,0:T(8,128)(2,1)} %bitcast.15, bf16[3,1024,256]{2,1,0:T(8,128)(2,1)} %bitcast.13, ...), custom_call_target="tpu_custom_call" | custom-call | flops 20000000 | bytes 6000000 | tf_op jit(solution)/shard_map/near/pallas_call | solution.py:242
  33.5 0.0 collective-permute-done.4
  33.5 0.0 collective-permute-done.3
  33.5 0.0 collective-permute-done
  33.6 0.0 collective-permute-done.1
  33.6 0.1 broadcast_select_fusion.2
  33.7 2.4 %collective-permute-start.5 = (bf16[1024,256]{1,0:T(8,128)(2,1)S(1)}, bf16[1024,256]{1,0:T(8,128)(2,1)S(1)}, u32[]{:S(2)}, u32[]{:S(2)}) collective-permute-start(bf16[1024,256]{1,0:T(8,128)(2,1)S(1)} %get-tuple-element.43), channel_id=1, source_target_pairs={{0,1},{1,0},{2,3},{3,2},{4,5},{5,4},{6,7},{7,6},{8,9},{9,8},{10,11... | collective-permute-start | bytes 1572872 | tf_op jit(solution)/shard_map/ppermute | solution.py:325
  36.2 0.0 collective-permute-done.6.swap_ref
  36.2 2.2 %far.1 = (f32[2,16,256]{2,1,0:T(8,128)S(1)}, f32[1024,256]{1,0:T(8,128)S(1)}) custom-call(s32[1]{0:T(128)} %bitcast.core_ref, bf16[1024,256]{1,0:T(8,128)(2,1)S(1)} %collective-permute-done.6.swap_ref, bf16[1024,256]{1,0:T(8,128)(2,1)S(1)} %get-tuple-element.45.right_ref, bf16[1024,256]{1,0:T(8,128)(2,1)S(1)} %get-tuple-element.44.left_ref, ...), custom_call_target="tpu_custom_call" | custom-call | flops 20000000 | bytes 6000000 | tf_op jit(solution)/shard_map/far/pallas_call | solution.py:242
  38.4 0.0 collective-permute-done.5.relay_ref
  38.4 2.5 %last.1 = (f32[8,36,128]{2,1,0:T(8,128)S(1)}, bf16[1024,256]{1,0:T(8,128)(2,1)}) custom-call(s32[1]{0:T(128)} %bitcast.core_ref, bf16[1024,256]{1,0:T(8,128)(2,1)S(1)} %collective-permute-done.5.relay_ref, bf16[7,1024,256]{2,1,0:T(8,128)(2,1)S(1)} %get-tuple-element.32.saved, f32[9,2,256]{2,1,0:T(2,128)S(1)} %get-tuple-element.33.par_ref, ...), custom_call_target="tpu_custom_call" | custom-call | flops 20000000 | bytes 6000000 | tf_op jit(solution)/shard_map/last/pallas_call | solution.py:242
  40.9 10.6 %all_to_all.15 = f32[8,36,128]{2,1,0:T(8,128)S(1)} all-to-all(f32[8,36,128]{2,1,0:T(8,128)S(1)} %get-tuple-element.40), channel_id=1, replica_groups=mesh['x'=4,'zl'=2,'zh'=4,'y'=8,'core'=2] {'x','core'}, dimensions={0} | all-to-all | bytes 294912 | tf_op jit(solution)/shard_map/all_to_all | solution.py:345
  51.5 13.9 %all_to_all.16 = f32[8,36,128]{2,1,0:T(8,128)S(1)} all-to-all(f32[8,36,128]{2,1,0:T(8,128)S(1)} %broadcast_in_dim.7), channel_id=1, replica_groups=mesh['x'=4,'zl'=2,'zh'=4,'y'=8,'core'=2] {'y'}, dimensions={0} | all-to-all | bytes 294912 | tf_op jit(solution)/shard_map/all_to_all | solution.py:345
  65.5 17.3 %all_to_all.17.refs_0_ = f32[8,36,128]{2,1,0:T(8,128)S(1)} all-to-all(f32[8,36,128]{2,1,0:T(8,128)S(1)} %broadcast_in_dim.8), channel_id=1, replica_groups=mesh['x'=4,'zl'=2,'zh'=4,'y'=8,'core'=2] {'zl','zh'}, dimensions={0} | all-to-all | bytes 294912 | tf_op jit(solution)/shard_map/all_to_all | solution.py:345
  82.8 0.6 finish.1
  (6 shorter events, 0.1 us)
Async XLA Ops:
  0.6 32.9 %collective-permute-start = (bf16[1024,256]{1,0:T(8,128)(2,1)}, bf16[1024,256]{1,0:T(8,128)(2,1)S(1)}, u32[]{:S(2)}, u32[]{:S(2)}) collective-permute-start(bf16[1024,256]{1,0:T(8,128)(2,1)} %bitcast.8), channel_id=1, source_target_pairs={{0,2},{2,4},{4,6},{6,8},{8,10},{10,12},{12,14},{1,3},{3,5},{5,7},{... | collective-permute-start | bytes 1572872 | tf_op jit(solution)/shard_map/ppermute | solution.py:295
  4.2 29.4 %collective-permute-start.1 = (bf16[1024,256]{1,0:T(8,128)(2,1)}, bf16[1024,256]{1,0:T(8,128)(2,1)S(1)}, u32[]{:S(2)}, u32[]{:S(2)}) collective-permute-start(bf16[1024,256]{1,0:T(8,128)(2,1)} %bitcast.9), channel_id=1, source_target_pairs={{2,0},{4,2},{6,4},{8,6},{10,8},{12,10},{14,12},{3,1},{5,3},{7,5},{... | collective-permute-start | bytes 1572872 | tf_op jit(solution)/shard_map/ppermute | solution.py:296
  6.6 11.9 %collective-permute-start.2 = (bf16[384,256]{1,0:T(8,128)(2,1)S(1)}, bf16[384,256]{1,0:T(8,128)(2,1)S(1)}, u32[]{:S(2)}, u32[]{:S(2)}) collective-permute-start(bf16[384,256]{1,0:T(8,128)(2,1)S(1)} %get-tuple-element.23), channel_id=1, source_target_pairs={{14,30},{15,31},{30,46},{31,47},{46,62},{47,63},{16,0},{17,1},{32,... | collective-permute-start | bytes 589832 | tf_op jit(solution)/shard_map/ppermute | solution.py:293
  7.9 25.7 %collective-permute-start.4 = (bf16[640,256]{1,0:T(8,128)(2,1)S(1)}, bf16[640,256]{1,0:T(8,128)(2,1)S(1)}, u32[]{:S(2)}, u32[]{:S(2)}) collective-permute-start(bf16[640,256]{1,0:T(8,128)(2,1)S(1)} %get-tuple-element.25), channel_id=1, source_target_pairs={{14,16},{15,17},{30,32},{31,33},{46,48},{47,49},{16,14},{17,15},{3... | collective-permute-start | bytes 983048 | tf_op jit(solution)/shard_map/ppermute | solution.py:294
  18.4 15.1 %collective-permute-start.3 = (bf16[384,256]{1,0:T(8,128)(2,1)S(1)}, bf16[384,256]{1,0:T(8,128)(2,1)S(1)}, u32[]{:S(2)}, u32[]{:S(2)}) collective-permute-start(bf16[384,256]{1,0:T(8,128)(2,1)S(1)} %collective-permute-done.2), channel_id=1, source_target_pairs={{30,16},{31,17},{46,32},{47,33},{62,48},{63,49},{0,14},{1,15},{16,... | collective-permute-start | bytes 589832 | tf_op jit(solution)/shard_map/ppermute | solution.py:299
  26.0 10.1 %collective-permute-start.6 = (bf16[1024,256]{1,0:T(8,128)(2,1)}, bf16[1024,256]{1,0:T(8,128)(2,1)S(1)}, u32[]{:S(2)}, u32[]{:S(2)}) collective-permute-start(bf16[1024,256]{1,0:T(8,128)(2,1)} %bitcast.11), channel_id=1, source_target_pairs={{0,1},{1,0},{2,3},{3,2},{4,5},{5,4},{6,7},{7,6},{8,9},{9,8},{10,11... | collective-permute-start | bytes 1572872 | tf_op jit(solution)/shard_map/ppermute | solution.py:297
  33.7 4.7 %collective-permute-start.5 = (bf16[1024,256]{1,0:T(8,128)(2,1)S(1)}, bf16[1024,256]{1,0:T(8,128)(2,1)S(1)}, u32[]{:S(2)}, u32[]{:S(2)}) collective-permute-start(bf16[1024,256]{1,0:T(8,128)(2,1)S(1)} %get-tuple-element.43), channel_id=1, source_target_pairs={{0,1},{1,0},{2,3},{3,2},{4,5},{5,4},{6,7},{7,6},{8,9},{9,8},{10,11... | collective-permute-start | bytes 1572872 | tf_op jit(solution)/shard_map/ppermute | solution.py:325

commit v5 on v4

--- a/solution.py
+++ b/solution.py
@@ -9,7 +9,7 @@
 from jax.sharding import PartitionSpec as P
 
 BLOCK = 128
-HEAD = 3 * BLOCK
+HEAD = 2 * BLOCK
 NB = 8
 LEVELS = 4
 STEP = 16
@@ -295,8 +295,6 @@
     left = lax.ppermute(dy, CTX, inner)
     right = lax.ppermute(dy, CTX, [(b, a) for a, b in inner])
     swap = lax.ppermute(dy, "core", pair)
-    own, hopped = lax.optimization_barrier((dy, hopped))
-    turned = lax.ppermute(hopped, CTX, turn)
     acc_near, part_near, coef, par, saved = call(
         near_kernel,
         "near",
@@ -307,7 +305,7 @@
             jax.ShapeDtypeStruct((LEVELS + 5, 2, width), F32),
             jax.ShapeDtypeStruct((2 * LEVELS - 1, rows, width), dy.dtype),
         ),
-        (own, level_input[0], saved_forward[:, 0], saved_reverse[:, 0], filters, mixing),
+        (dy, level_input[0], saved_forward[:, 0], saved_reverse[:, 0], filters, mixing),
         "hhhhhh",
         scratch=[
             pltpu.VMEM((rows, width), dy.dtype),
@@ -317,6 +315,8 @@
         ],
         flops=20_000_000,
     )
+    hopped, acc_near = lax.optimization_barrier((hopped, acc_near))
+    turned = lax.ppermute(hopped, CTX, turn)
     left, right, turned, crossed, acc_near = lax.optimization_barrier((left, right, turned, crossed, acc_near))
     row = lax.axis_index("y")
     detour = jnp.concatenate([turned, crossed])

time: 83.8 us -> 82.7 us (0.987)
  waiting for transfers between devices: 9.88 us -> 4.85 us
  local copies, waits for them, and re-layouts: 0.06 us -> 3.02 us
  blocking collectives: 41.8 us -> 38.9 us
  starting transfers between devices: 18.7 us -> 21.4 us
  other arithmetic: 0.15 us -> 1.25 us
    ppermute x1, waiting for transfers between devices: 9.87 us -> 4.29 us  [body(): hopped = lax.ppermute(head, CTX, hop)]
    all_to_all x3, blocking collectives: 41.8 us -> 38.9 us  [body(): got = lax.all_to_all(sums, axes, 0, 0)]
    ppermute x1, starting transfers between devices: 7.6 us -> 10.1 us  [body(): turned = lax.ppermute(hopped, CTX, turn)]
    unnamed x1 -> x7, local copies, waits for them, and re-layouts: 0.01 us -> 1.82 us
    concatenate x1, local copies, waits for them, and re-layouts: 0.02 us -> 1.17 us  [body(): detour = jnp.concatenate([turned, crossed])]
    select_n x1, other arithmetic: 0.12 us -> 1.21 us  [body(): relay = lax.ppermute(jnp.where(core == 0, right, left), 'core', pair)]
  transfers between devices with their start and end apart: 7 -> 7, of which waited for: 1 -> 2; matrix products, arithmetic and copies ran while one was open for 0% -> 3% of each run, Pallas kernels for 11% -> 11%
where the time goes in v5:
time: 82.7 us; the launch traced here: 82.3 us
  blocking collectives  38.9 us (47%)
  starting transfers between devices  21.4 us (26%)
  Pallas kernels  12 us (15%)
  waiting for transfers between devices  4.85 us (6%)
  local copies, waits for them, and re-layouts  3.02 us (4%)
  other arithmetic  1.25 us (2%)
    all_to_all x3, blocking collectives, body(): got = lax.all_to_all(sums, axes, 0, 0)  38.9 us
    pallas_call x5, Pallas kernels, call(): pl.pallas_call(kernel, out_shape=outs, in_specs=[pl.BlockSpec(memory_spac...  12 us
    ppermute x1, starting transfers between devices, body(): turned = lax.ppermute(hopped, CTX, turn)  10.1 us
    ppermute x1, waiting for transfers between devices, body(): hopped = lax.ppermute(head, CTX, hop)  4.29 us
    ppermute x1, starting transfers between devices, body(): left = lax.ppermute(dy, CTX, inner)  3.52 us
    ppermute x1, starting transfers between devices, body(): swap = lax.ppermute(dy, 'core', pair)  1.92 us
    ppermute x1, starting transfers between devices, body(): relay = lax.ppermute(jnp.where(core == 0, right, left), 'core', pair)  1.92 us
    unnamed x7, local copies, waits for them, and re-layouts  1.82 us
  transfers between devices with their start and end apart: 7, of which 2 were waited for; matrix products, arithmetic and copies ran while one was open for 3% of the time, Pallas kernels for 11%

profile of v5, /device:TPU:64, one launch (start us, length us, event | category | flops | bytes accessed | tf_op | source)
XLA Modules:
  0.0 82.3 jit_solution(16781708474394909995)
XLA Ops:
  0.6 3.5 %collective-permute-start = (bf16[1024,256]{1,0:T(8,128)(2,1)}, bf16[1024,256]{1,0:T(8,128)(2,1)S(1)}, u32[]{:S(2)}, u32[]{:S(2)}) collective-permute-start(bf16[1024,256]{1,0:T(8,128)(2,1)} %bitcast.8), channel_id=1, source_target_pairs={{0,2},{2,4},{4,6},{6,8},{8,10},{10,12},{12,14},{1,3},{3,5},{5,7},{... | collective-permute-start | bytes 1572872 | tf_op jit(solution)/shard_map/ppermute | solution.py:295
  4.2 1.3 %collective-permute-start.1 = (bf16[1024,256]{1,0:T(8,128)(2,1)}, bf16[1024,256]{1,0:T(8,128)(2,1)}, u32[]{:S(2)}, u32[]{:S(2)}) collective-permute-start(bf16[1024,256]{1,0:T(8,128)(2,1)} %bitcast.9), channel_id=1, source_target_pairs={{2,0},{4,2},{6,4},{8,6},{10,8},{12,10},{14,12},{3,1},{5,3},{7,5},{... | collective-permute-start | bytes 1572872 | tf_op jit(solution)/shard_map/ppermute | solution.py:296
  5.5 1.1 %split.1 = (bf16[256,256]{1,0:T(8,128)(2,1)S(1)}, bf16[768,256]{1,0:T(8,128)(2,1)S(1)}) custom-call(bf16[1024,256]{1,0:T(8,128)(2,1)} %bitcast.10), custom_call_target="tpu_custom_call" | custom-call | bytes 6000000 | tf_op jit(solution)/shard_map/split/pallas_call | solution.py:242
  6.5 1.4 %collective-permute-start.4 = (bf16[768,256]{1,0:T(8,128)(2,1)S(1)}, bf16[768,256]{1,0:T(8,128)(2,1)}, u32[]{:S(2)}, u32[]{:S(2)}) collective-permute-start(bf16[768,256]{1,0:T(8,128)(2,1)S(1)} %get-tuple-element.26), channel_id=1, source_target_pairs={{14,16},{15,17},{30,32},{31,33},{46,48},{47,49},{16,14},{17,15},{3... | collective-permute-start | bytes 1179656 | tf_op jit(solution)/shard_map/ppermute | solution.py:294
  8.0 1.3 %collective-permute-start.2 = (bf16[256,256]{1,0:T(8,128)(2,1)S(1)}, bf16[256,256]{1,0:T(8,128)(2,1)S(1)}, u32[]{:S(2)}, u32[]{:S(2)}) collective-permute-start(bf16[256,256]{1,0:T(8,128)(2,1)S(1)} %get-tuple-element.23), channel_id=1, source_target_pairs={{14,30},{15,31},{30,46},{31,47},{46,62},{47,63},{16,0},{17,1},{32,... | collective-permute-start | bytes 393224 | tf_op jit(solution)/shard_map/ppermute | solution.py:293
  9.3 0.0 copy-start.2
  9.3 5.6 %near.1 = (f32[2,16,256]{2,1,0:T(8,128)S(1)}, f32[1024,256]{1,0:T(8,128)S(1)}, f32[2,10,8,256]{3,2,1,0:T(8,128)S(1)}, f32[9,2,256]{2,1,0:T(2,128)S(1)}, bf16[7,1024,256]{2,1,0:T(8,128)(2,1)S(1)}) custom-call(bf16[1024,256]{1,0:T(8,128)(2,1)} %bitcast.11, bf16[1024,256]{1,0:T(8,128)(2,1)} %bitcast.15, bf16[3,1024,256]{2,1,0:T(8,128)(2,1)} %bitcast.13, ...), custom_call_target="tpu_custom_call" | custom-call | flops 20000000 | bytes 6000000 | tf_op jit(solution)/shard_map/near/pallas_call | solution.py:242
  14.9 1.8 %copy-done = bf16[7,1024,256]{2,1,0:T(8,128)(2,1)} copy-done((bf16[7,1024,256]{2,1,0:T(8,128)(2,1)}, bf16[7,1024,256]{2,1,0:T(8,128)(2,1)S(1)}, u32[]{:S(2)}) %copy-start) | copy-done | bytes 3670040
  16.7 4.3 %collective-permute-done.2 = bf16[256,256]{1,0:T(8,128)(2,1)S(1)} collective-permute-done((bf16[256,256]{1,0:T(8,128)(2,1)S(1)}, bf16[256,256]{1,0:T(8,128)(2,1)S(1)}, u32[]{:S(2)}, u32[]{:S(2)}) %collective-permute-start.2) | collective-permute-done | bytes 131104 | tf_op jit(solution)/shard_map/ppermute | solution.py:293
  21.0 10.1 %collective-permute-start.3 = (bf16[256,256]{1,0:T(8,128)(2,1)S(1)}, bf16[256,256]{1,0:T(8,128)(2,1)S(1)}, u32[]{:S(2)}, u32[]{:S(2)}) collective-permute-start(bf16[256,256]{1,0:T(8,128)(2,1)S(1)} %collective-permute-done.2), channel_id=1, source_target_pairs={{30,16},{31,17},{46,32},{47,33},{62,48},{63,49},{0,14},{1,15},{16,... | collective-permute-start | bytes 393224 | tf_op jit(solution)/shard_map/ppermute | solution.py:319
  31.1 1.9 %collective-permute-start.6 = (bf16[1024,256]{1,0:T(8,128)(2,1)S(1)}, bf16[1024,256]{1,0:T(8,128)(2,1)S(1)}, u32[]{:S(2)}, u32[]{:S(2)}) collective-permute-start(bf16[1024,256]{1,0:T(8,128)(2,1)S(1)} %bitcast.12), channel_id=1, source_target_pairs={{0,1},{1,0},{2,3},{3,2},{4,5},{5,4},{6,7},{7,6},{8,9},{9,8},{10,11... | collective-permute-start | bytes 1572872 | tf_op jit(solution)/shard_map/ppermute | solution.py:297
  33.0 0.5 collective-permute-done.3
  33.6 0.0 collective-permute-done.4
  33.6 0.0 collective-permute-done
  33.6 0.0 collective-permute-done.1
  33.6 1.2 %constant_dynamic-update-slice_fusion = bf16[1024,256]{1,0:T(8,128)(2,1)S(1)} fusion(bf16[1024,256]{1,0:T(8,128)(2,1)S(1)} %constant_dynamic-update-slice_fusion.1, bf16[768,256]{1,0:T(8,128)(2,1)} %collective-permute-done.4), kind=kLoop, calls=%fused_computation.3 | loop fusion | bytes 786432 | tf_op jit(solution)/shard_map/concatenate | solution.py:322
  34.8 1.2 %broadcast_select_fusion.2 = (bf16[1024,256]{1,0:T(8,128)(2,1)S(1)}, bf16[1024,256]{1,0:T(8,128)(2,1)S(1)}, bf16[1024,256]{1,0:T(8,128)(2,1)S(1)}) fusion(pred[]{:T(512)S(6)} %eq.9, bf16[1024,256]{1,0:T(8,128)(2,1)S(1)} %constant_dynamic-update-slice_fusion, bf16[1024,256]{1,0:T(8,128)(2,1)S(1)} %collective-permute-done, pred[]{:T(512)S(6)} %eq.11, ...), kind=kLoop, calls=%fused_computation.2 | loop fusion | flops 786432 | bytes 3145731 | tf_op jit(solution)/shard_map/jit(_where)/select_n | solution.py:325
  36.0 1.9 %collective-permute-start.5 = (bf16[1024,256]{1,0:T(8,128)(2,1)S(1)}, bf16[1024,256]{1,0:T(8,128)(2,1)S(1)}, u32[]{:S(2)}, u32[]{:S(2)}) collective-permute-start(bf16[1024,256]{1,0:T(8,128)(2,1)S(1)} %get-tuple-element.43), channel_id=1, source_target_pairs={{0,1},{1,0},{2,3},{3,2},{4,5},{5,4},{6,7},{7,6},{8,9},{9,8},{10,11... | collective-permute-start | bytes 1572872 | tf_op jit(solution)/shard_map/ppermute | solution.py:325
  37.9 2.2 %far.1 = (f32[2,16,256]{2,1,0:T(8,128)S(1)}, f32[1024,256]{1,0:T(8,128)S(1)}) custom-call(s32[1]{0:T(128)} %bitcast.core_ref, bf16[1024,256]{1,0:T(8,128)(2,1)S(1)} %collective-permute-done.6.swap_ref, bf16[1024,256]{1,0:T(8,128)(2,1)S(1)} %get-tuple-element.45.right_ref, bf16[1024,256]{1,0:T(8,128)(2,1)S(1)} %get-tuple-element.44.left_ref, ...), custom_call_target="tpu_custom_call" | custom-call | flops 20000000 | bytes 6000000 | tf_op jit(solution)/shard_map/far/pallas_call | solution.py:242
  40.2 2.5 %last.1 = (f32[8,36,128]{2,1,0:T(8,128)S(1)}, bf16[1024,256]{1,0:T(8,128)(2,1)}) custom-call(s32[1]{0:T(128)} %bitcast.core_ref, bf16[1024,256]{1,0:T(8,128)(2,1)S(1)} %collective-permute-done.5.relay_ref, bf16[7,1024,256]{2,1,0:T(8,128)(2,1)S(1)} %copy-done.1, f32[9,2,256]{2,1,0:T(2,128)S(1)} %get-tuple-element.33.par_ref, ...), custom_call_target="tpu_custom_call" | custom-call | flops 20000000 | bytes 6000000 | tf_op jit(solution)/shard_map/last/pallas_call | solution.py:242
  42.7 10.7 %all_to_all.15 = f32[8,36,128]{2,1,0:T(8,128)S(1)} all-to-all(f32[8,36,128]{2,1,0:T(8,128)S(1)} %get-tuple-element.40), channel_id=1, replica_groups=mesh['x'=4,'zl'=2,'zh'=4,'y'=8,'core'=2] {'x','core'}, dimensions={0} | all-to-all | bytes 294912 | tf_op jit(solution)/shard_map/all_to_all | solution.py:345
  53.5 13.2 %all_to_all.16 = f32[8,36,128]{2,1,0:T(8,128)S(1)} all-to-all(f32[8,36,128]{2,1,0:T(8,128)S(1)} %broadcast_in_dim.7), channel_id=1, replica_groups=mesh['x'=4,'zl'=2,'zh'=4,'y'=8,'core'=2] {'y'}, dimensions={0} | all-to-all | bytes 294912 | tf_op jit(solution)/shard_map/all_to_all | solution.py:345
  66.7 15.0 %all_to_all.17.refs_0_ = f32[8,36,128]{2,1,0:T(8,128)S(1)} all-to-all(f32[8,36,128]{2,1,0:T(8,128)S(1)} %broadcast_in_dim.8), channel_id=1, replica_groups=mesh['x'=4,'zl'=2,'zh'=4,'y'=8,'core'=2] {'zl','zh'}, dimensions={0} | all-to-all | bytes 294912 | tf_op jit(solution)/shard_map/all_to_all | solution.py:345
  81.7 0.6 finish.1
  (11 shorter events, 0.1 us)
Async XLA Ops:
  0.6 32.9 %collective-permute-start = (bf16[1024,256]{1,0:T(8,128)(2,1)}, bf16[1024,256]{1,0:T(8,128)(2,1)S(1)}, u32[]{:S(2)}, u32[]{:S(2)}) collective-permute-start(bf16[1024,256]{1,0:T(8,128)(2,1)} %bitcast.8), channel_id=1, source_target_pairs={{0,2},{2,4},{4,6},{6,8},{8,10},{10,12},{12,14},{1,3},{3,5},{5,7},{... | collective-permute-start | bytes 1572872 | tf_op jit(solution)/shard_map/ppermute | solution.py:295
  4.2 29.4 %collective-permute-start.1 = (bf16[1024,256]{1,0:T(8,128)(2,1)}, bf16[1024,256]{1,0:T(8,128)(2,1)}, u32[]{:S(2)}, u32[]{:S(2)}) collective-permute-start(bf16[1024,256]{1,0:T(8,128)(2,1)} %bitcast.9), channel_id=1, source_target_pairs={{2,0},{4,2},{6,4},{8,6},{10,8},{12,10},{14,12},{3,1},{5,3},{7,5},{... | collective-permute-start | bytes 1572872 | tf_op jit(solution)/shard_map/ppermute | solution.py:296
  6.5 27.0 %collective-permute-start.4 = (bf16[768,256]{1,0:T(8,128)(2,1)S(1)}, bf16[768,256]{1,0:T(8,128)(2,1)}, u32[]{:S(2)}, u32[]{:S(2)}) collective-permute-start(bf16[768,256]{1,0:T(8,128)(2,1)S(1)} %get-tuple-element.26), channel_id=1, source_target_pairs={{14,16},{15,17},{30,32},{31,33},{46,48},{47,49},{16,14},{17,15},{3... | collective-permute-start | bytes 1179656 | tf_op jit(solution)/shard_map/ppermute | solution.py:294
  8.0 13.0 %collective-permute-start.2 = (bf16[256,256]{1,0:T(8,128)(2,1)S(1)}, bf16[256,256]{1,0:T(8,128)(2,1)S(1)}, u32[]{:S(2)}, u32[]{:S(2)}) collective-permute-start(bf16[256,256]{1,0:T(8,128)(2,1)S(1)} %get-tuple-element.23), channel_id=1, source_target_pairs={{14,30},{15,31},{30,46},{31,47},{46,62},{47,63},{16,0},{17,1},{32,... | collective-permute-start | bytes 393224 | tf_op jit(solution)/shard_map/ppermute | solution.py:293
  9.3 21.8 %copy-start.2 = (bf16[1,1024,256]{2,1,0:T(8,128)(2,1)S(1)}, bf16[1,1024,256]{2,1,0:T(8,128)(2,1)}, u32[]{:S(2)}) copy-start(bf16[1,1024,256]{2,1,0:T(8,128)(2,1)} %param.11) | copy-start | bytes 1572868
  14.9 1.8 %copy-start = (bf16[7,1024,256]{2,1,0:T(8,128)(2,1)}, bf16[7,1024,256]{2,1,0:T(8,128)(2,1)S(1)}, u32[]{:S(2)}) copy-start(bf16[7,1024,256]{2,1,0:T(8,128)(2,1)S(1)} %get-tuple-element.32.saved) | copy-start | bytes 11010052
  21.0 12.6 %collective-permute-start.3 = (bf16[256,256]{1,0:T(8,128)(2,1)S(1)}, bf16[256,256]{1,0:T(8,128)(2,1)S(1)}, u32[]{:S(2)}, u32[]{:S(2)}) collective-permute-start(bf16[256,256]{1,0:T(8,128)(2,1)S(1)} %collective-permute-done.2), channel_id=1, source_target_pairs={{30,16},{31,17},{46,32},{47,33},{62,48},{63,49},{0,14},{1,15},{16,... | collective-permute-start | bytes 393224 | tf_op jit(solution)/shard_map/ppermute | solution.py:319
  31.1 6.9 %collective-permute-start.6 = (bf16[1024,256]{1,0:T(8,128)(2,1)S(1)}, bf16[1024,256]{1,0:T(8,128)(2,1)S(1)}, u32[]{:S(2)}, u32[]{:S(2)}) collective-permute-start(bf16[1024,256]{1,0:T(8,128)(2,1)S(1)} %bitcast.12), channel_id=1, source_target_pairs={{0,1},{1,0},{2,3},{3,2},{4,5},{5,4},{6,7},{7,6},{8,9},{9,8},{10,11... | collective-permute-start | bytes 1572872 | tf_op jit(solution)/shard_map/ppermute | solution.py:297
  33.6 4.3 %copy-start.1 = (bf16[7,1024,256]{2,1,0:T(8,128)(2,1)S(1)}, bf16[7,1024,256]{2,1,0:T(8,128)(2,1)}, u32[]{:S(2)}) copy-start(bf16[7,1024,256]{2,1,0:T(8,128)(2,1)} %copy-done) | copy-start | bytes 11010052
  36.0 4.2 %collective-permute-start.5 = (bf16[1024,256]{1,0:T(8,128)(2,1)S(1)}, bf16[1024,256]{1,0:T(8,128)(2,1)S(1)}, u32[]{:S(2)}, u32[]{:S(2)}) collective-permute-start(bf16[1024,256]{1,0:T(8,128)(2,1)S(1)} %get-tuple-element.43), channel_id=1, source_target_pairs={{0,1},{1,0},{2,3},{3,2},{4,5},{5,4},{6,7},{7,6},{8,9},{9,8},{10,11... | collective-permute-start | bytes 1572872 | tf_op jit(solution)/shard_map/ppermute | solution.py:325

commit v6 on v5

--- a/solution.py
+++ b/solution.py
@@ -9,7 +9,6 @@
 from jax.sharding import PartitionSpec as P
 
 BLOCK = 128
-HEAD = 2 * BLOCK
 NB = 8
 LEVELS = 4
 STEP = 16
@@ -116,18 +115,6 @@
                 acc_ref[at] = acc_ref[at] + jnp.sum(accs[i * SUMS + row], axis=0, keepdims=True)
 
 
-def split_kernel(dy_ref, head_ref, tail_ref, sems):
-    head = head_ref.shape[0]
-    copies = [
-        pltpu.make_async_copy(dy_ref.at[pl.ds(0, head)], head_ref, sems.at[0]),
-        pltpu.make_async_copy(dy_ref.at[pl.ds(head, tail_ref.shape[0])], tail_ref, sems.at[1]),
-    ]
-    for copy in copies:
-        copy.start()
-    for copy in copies:
-        copy.wait()
-
-
 def near_kernel(dy_hbm, first, fwd, rev, filters_hbm, mixing_hbm, acc_ref, part_ref, coef_ref, par_ref, saved, dy_ref, filters_ref, mixing_ref, sems):
     moves = [
         (filters_hbm, filters_ref),
@@ -167,8 +154,25 @@
     run(work, saved, coef_ref, acc_ref, lambda n, r, cols: None, keep)
 
 
-def far_kernel(core_ref, swap_ref, right_ref, left_ref, saved, coef_ref, near_ref, part_ref, acc_ref, out_ref):
-    core = core_ref[0]
+def pick_kernel(ids_ref, cross_ref, left_in, right_in, left_ref, right_ref, send_ref):
+    core, place = ids_ref[0] % 2, ids_ref[0] // 2
+
+    def copy(a, b):
+        def step(i, carry):
+            rows = pl.ds(pl.multiple_of(i * BLOCK, BLOCK), BLOCK)
+            b[rows, :] = a[rows, :]
+            return carry
+
+        lax.fori_loop(0, NB, step, 0)
+
+    pl.when(place == 0)(lambda: copy(cross_ref, left_ref))
+    pl.when(place == 1)(lambda: copy(cross_ref, right_ref))
+    pl.when(core == 0)(lambda: copy(right_ref, send_ref))
+    pl.when(core == 1)(lambda: copy(left_ref, send_ref))
+
+
+def far_kernel(ids_ref, swap_ref, right_ref, left_ref, saved, coef_ref, near_ref, part_ref, acc_ref, out_ref):
+    core = ids_ref[0] % 2
     acc_ref[...] = near_ref[...]
 
     def start(n, r, cols):
@@ -184,8 +188,8 @@
         pl.when(core == b)(lambda work=work: run(work, saved, coef_ref, acc_ref, start, keep))
 
 
-def last_kernel(core_ref, relay_ref, saved, par_ref, coef_ref, far_ref, part_ref, sums_ref, grad_ref, acc_ref):
-    core = core_ref[0]
+def last_kernel(ids_ref, relay_ref, saved, par_ref, coef_ref, far_ref, part_ref, sums_ref, grad_ref, acc_ref):
+    core = ids_ref[0] % 2
     acc_ref[...] = far_ref[...]
 
     def start(n, r, cols):
@@ -236,7 +240,7 @@
                     mixing_ref[j - 4, pl.ds(b, 1), cols] = row
 
 
-def call(kernel, name, outs, args, spaces, scratch=(), flops=0):
+def call(kernel, name, outs, args, spaces, scratch=(), flops=0, aliases={}):
     space = {"s": pltpu.SMEM, "v": pltpu.VMEM, "h": pltpu.HBM}
     args = [pltpu.with_memory_space_constraint(a, pltpu.HBM) if k == "h" else a for a, k in zip(args, spaces)]
     return pl.pallas_call(
@@ -245,7 +249,8 @@
         in_specs=[pl.BlockSpec(memory_space=space[k]) for k in spaces],
         out_specs=(pl.BlockSpec(memory_space=pltpu.VMEM),) * len(outs),
         scratch_shapes=scratch,
-        compiler_params=pltpu.CompilerParams(vmem_limit_bytes=24 * 1024 * 1024),
+        input_output_aliases=aliases,
+        compiler_params=pltpu.CompilerParams(vmem_limit_bytes=8 * 1024 * 1024),
         cost_estimate=pl.CostEstimate(flops=flops, bytes_accessed=6_000_000, transcendentals=0),
         name=name,
     )(*args)
@@ -258,16 +263,9 @@
         return (z * ys + y) * cores + c
 
     spots = [(z, c) for z in range(zs) for c in range(cores)]
-    seams = [(z, c) for z, c in spots if z + 1 < zs]
-    end = ys - 1
-    inner = [(at(z, y, c), at(z, y + 1, c)) for z, c in spots for y in range(end)]
-    cross = [(at(z, end, c), at(z + 1, 0, c)) for z, c in seams]
-    cross += [(at(z + 1, 0, c), at(z, end, c)) for z, c in seams]
-    hop = [(at(z, end, c), at(z + 1, end, c)) for z, c in seams]
-    hop += [(at(z + 1, 0, c), at(z, 0, c)) for z, c in seams]
-    turn = [(at(z + 1, end, c), at(z + 1, 0, c)) for z, c in seams]
-    turn += [(at(z, 0, c), at(z, end, c)) for z, c in seams]
-    return inner, cross, hop, turn
+    inner = [(at(z, y, c), at(z, y + 1, c)) for z, c in spots for y in range(ys - 1)]
+    cross = [(at(z, ys - 1, c), at(z + 1, 0, c)) for z, c in spots if z + 1 < zs]
+    return inner, cross + [(b, a) for a, b in cross]
 
 
 def body(level_input, saved_forward, saved_reverse, filters, mixing, cotangent):
@@ -275,23 +273,17 @@
     rows = level_input.shape[1]
     ctx = lax.axis_size(CTX)
     core = lax.axis_index("core")
-    core_id = core.astype(jnp.int32).reshape(1)
     dy = cotangent[0]
     mixing = jnp.swapaxes(mixing, 0, 1)
     acc = jax.ShapeDtypeStruct((2, ROWS, width), F32)
     part = jax.ShapeDtypeStruct((rows, width), F32)
     pair = [(0, 1), (1, 0)]
-    inner, cross, hop, turn = routes()
-    head, tail = call(
-        split_kernel,
-        "split",
-        tuple(jax.ShapeDtypeStruct((n, width), dy.dtype) for n in (HEAD, rows - HEAD)),
-        (dy,),
-        "h",
-        scratch=[pltpu.SemaphoreType.DMA((2,))],
-    )
-    hopped = lax.ppermute(head, CTX, hop)
-    crossed = lax.ppermute(tail, CTX, cross)
+    inner, cross = routes()
+    y = lax.axis_index("y")
+    place = jnp.where(y == 0, 0, jnp.where(y == lax.axis_size("y") - 1, 1, 2))
+    ids = (core + 2 * place).astype(jnp.int32).reshape(1)
+    ids, dy = lax.optimization_barrier((ids, dy))
+    crossed = lax.ppermute(dy, CTX, cross)
     left = lax.ppermute(dy, CTX, inner)
     right = lax.ppermute(dy, CTX, [(b, a) for a, b in inner])
     swap = lax.ppermute(dy, "core", pair)
@@ -315,19 +307,15 @@
         ],
         flops=20_000_000,
     )
-    hopped, acc_near = lax.optimization_barrier((hopped, acc_near))
-    turned = lax.ppermute(hopped, CTX, turn)
-    left, right, turned, crossed, acc_near = lax.optimization_barrier((left, right, turned, crossed, acc_near))
-    row = lax.axis_index("y")
-    detour = jnp.concatenate([turned, crossed])
-    left = jnp.where(row == 0, detour, left)
-    right = jnp.where(row == lax.axis_size("y") - 1, detour, right)
-    relay = lax.ppermute(jnp.where(core == 0, right, left), "core", pair)
+    crossed, left, right, acc_near = lax.optimization_barrier((crossed, left, right, acc_near))
+    halo = jax.ShapeDtypeStruct(dy.shape, dy.dtype)
+    left, right, send = call(pick_kernel, "pick", (halo,) * 3, (ids, crossed, left, right), "svvv", aliases={2: 0, 3: 1})
+    relay = lax.ppermute(send, "core", pair)
     acc_far, part_far = call(
         far_kernel,
         "far",
         (acc, part),
-        (core_id, swap, right, left, saved, coef, acc_near, part_near),
+        (ids, swap, right, left, saved, coef, acc_near, part_near),
         "svvvvvvv",
         flops=20_000_000,
     )
@@ -335,7 +323,7 @@
         last_kernel,
         "last",
         (jax.ShapeDtypeStruct((8, 18 * width // LANES, LANES), F32), jax.ShapeDtypeStruct((rows, width), jnp.bfloat16)),
-        (core_id, relay, saved, par, coef, acc_far, part_far),
+        (ids, relay, saved, par, coef, acc_far, part_far),
         "svvvvvv",
         scratch=[pltpu.VMEM((2, ROWS, width), F32)],
         flops=20_000_000,

time: 82.7 us -> 80.4 us (0.972)
  blocking collectives: 38.9 us -> 52.2 us
  starting transfers between devices: 21.4 us -> 9.34 us
  local copies, waits for them, and re-layouts: 3.02 us -> 0.03 us
  waiting for transfers between devices: 4.85 us -> 6.67 us
  other arithmetic: 1.25 us -> 0.03 us
  Pallas kernels: 12 us -> 11 us
    all_to_all x3, blocking collectives: 38.9 us -> 52.2 us  [body(): got = lax.all_to_all(sums, axes, 0, 0)]
    ppermute x4 -> x2, starting transfers between devices: 14.7 us -> 2.61 us  [the longest x1 1.92 us: body(): relay = lax.ppermute(send, 'core', pair)]
    ppermute x4 -> x2, waiting for transfers between devices: 4.84 us -> 0.01 us  [the longest x1 0.01 us: body(): relay = lax.ppermute(send, 'core', pair)]
    ppermute x1, waiting for transfers between devices: 0.01 us -> 4.04 us  [body(): right = lax.ppermute(dy, CTX, [(b, a) for a, b in inner])]
    ppermute x1, waiting for transfers between devices: 0.01 us -> 2.62 us  [body(): left = lax.ppermute(dy, CTX, inner)]
    unnamed x7 -> x0, local copies, waits for them, and re-layouts: 1.82 us -> none
    select_n x1 -> x0, other arithmetic: 1.21 us -> none  [body(): relay = lax.ppermute(jnp.where(core == 0, right, left), 'core', pair)]
    concatenate x1 -> x0, local copies, waits for them, and re-layouts: 1.17 us -> none  [body(): detour = jnp.concatenate([turned, crossed])]
  transfers between devices with their start and end apart: 7 -> 5, of which waited for: 2 -> 2; matrix products, arithmetic and copies ran while one was open for 3% -> 0% of each run, Pallas kernels for 11% -> 10%
where the time goes in v6:
time: 80.4 us; the launch traced here: 80 us
  blocking collectives  52.2 us (65%)
  Pallas kernels  11 us (14%)
  starting transfers between devices  9.34 us (12%)
  waiting for transfers between devices  6.67 us (8%)
    all_to_all x3, blocking collectives, body(): got = lax.all_to_all(sums, axes, 0, 0)  52.2 us
    pallas_call x5, Pallas kernels, call(): pl.pallas_call(kernel, out_shape=outs, in_specs=[pl.BlockSpec(memory_spac...  11 us
    ppermute x1, waiting for transfers between devices, body(): right = lax.ppermute(dy, CTX, [(b, a) for a, b in inner])  4.04 us
    ppermute x1, starting transfers between devices, body(): left = lax.ppermute(dy, CTX, inner)  3.51 us
    ppermute x1, waiting for transfers between devices, body(): left = lax.ppermute(dy, CTX, inner)  2.62 us
    ppermute x1, starting transfers between devices, body(): relay = lax.ppermute(send, 'core', pair)  1.92 us
    ppermute x1, starting transfers between devices, body(): swap = lax.ppermute(dy, 'core', pair)  1.92 us
  transfers between devices with their start and end apart: 5, of which 2 were waited for; matrix products, arithmetic and copies ran while one was open for 0% of the time, Pallas kernels for 10%

profile of v6, /device:TPU:64, one launch (start us, length us, event | category | flops | bytes accessed | tf_op | source)
XLA Modules:
  0.0 80.0 jit_solution(14387018152169113868)
XLA Ops:
  0.6 0.7 collective-permute-start
  1.3 3.5 %collective-permute-start.1 = (bf16[1024,256]{1,0:T(8,128)(2,1)}, bf16[1024,256]{1,0:T(8,128)(2,1)S(1)}, u32[]{:S(2)}, u32[]{:S(2)}) collective-permute-start(bf16[1024,256]{1,0:T(8,128)(2,1)} %bitcast.12), channel_id=1, source_target_pairs={{0,2},{2,4},{4,6},{6,8},{8,10},{10,12},{12,14},{1,3},{3,5},{5,7},{... | collective-permute-start | bytes 1572872 | tf_op jit(solution)/shard_map/ppermute | solution.py:287
  4.9 1.3 %collective-permute-start.2 = (bf16[1024,256]{1,0:T(8,128)(2,1)}, bf16[1024,256]{1,0:T(8,128)(2,1)S(1)}, u32[]{:S(2)}, u32[]{:S(2)}) collective-permute-start(bf16[1024,256]{1,0:T(8,128)(2,1)} %bitcast.13), channel_id=1, source_target_pairs={{2,0},{4,2},{6,4},{8,6},{10,8},{12,10},{14,12},{3,1},{5,3},{7,5},{... | collective-permute-start | bytes 1572872 | tf_op jit(solution)/shard_map/ppermute | solution.py:288
  6.2 1.9 %collective-permute-start.4 = (bf16[1024,256]{1,0:T(8,128)(2,1)}, bf16[1024,256]{1,0:T(8,128)(2,1)S(1)}, u32[]{:S(2)}, u32[]{:S(2)}) collective-permute-start(bf16[1024,256]{1,0:T(8,128)(2,1)} %bitcast.14), channel_id=1, source_target_pairs={{0,1},{1,0},{2,3},{3,2},{4,5},{5,4},{6,7},{7,6},{8,9},{9,8},{10,11... | collective-permute-start | bytes 1572872 | tf_op jit(solution)/shard_map/ppermute | solution.py:289
  8.1 5.6 %near.1 = (f32[2,16,256]{2,1,0:T(8,128)S(1)}, f32[1024,256]{1,0:T(8,128)S(1)}, f32[2,10,8,256]{3,2,1,0:T(8,128)S(1)}, f32[9,2,256]{2,1,0:T(2,128)S(1)}, bf16[7,1024,256]{2,1,0:T(8,128)(2,1)S(1)}) custom-call(bf16[1024,256]{1,0:T(8,128)(2,1)} %bitcast.15, bf16[1024,256]{1,0:T(8,128)(2,1)} %bitcast.10, bf16[3,1024,256]{2,1,0:T(8,128)(2,1)} %bitcast.8, ...), custom_call_target="tpu_custom_call" | custom-call | flops 20000000 | bytes 6000000 | tf_op jit(solution)/shard_map/near/pallas_call | solution.py:246
  13.7 0.0 collective-permute-done.cross_ref
  13.7 2.6 %collective-permute-done.1.left_in = bf16[1024,256]{1,0:T(8,128)(2,1)S(1)} collective-permute-done((bf16[1024,256]{1,0:T(8,128)(2,1)}, bf16[1024,256]{1,0:T(8,128)(2,1)S(1)}, u32[]{:S(2)}, u32[]{:S(2)}) %collective-permute-start.1) | collective-permute-done | bytes 524320 | tf_op jit(solution)/shard_map/ppermute | solution.py:287
  16.3 4.0 %collective-permute-done.2.right_in = bf16[1024,256]{1,0:T(8,128)(2,1)S(1)} collective-permute-done((bf16[1024,256]{1,0:T(8,128)(2,1)}, bf16[1024,256]{1,0:T(8,128)(2,1)S(1)}, u32[]{:S(2)}, u32[]{:S(2)}) %collective-permute-start.2) | collective-permute-done | bytes 524320 | tf_op jit(solution)/shard_map/ppermute | solution.py:288
  20.4 0.1 pick.1
  20.5 1.9 %collective-permute-start.3 = (bf16[1024,256]{1,0:T(8,128)(2,1)S(1)}, bf16[1024,256]{1,0:T(8,128)(2,1)S(1)}, u32[]{:S(2)}, u32[]{:S(2)}) collective-permute-start(bf16[1024,256]{1,0:T(8,128)(2,1)S(1)} %get-tuple-element.29), channel_id=1, source_target_pairs={{0,1},{1,0},{2,3},{3,2},{4,5},{5,4},{6,7},{7,6},{8,9},{9,8},{10,11... | collective-permute-start | bytes 1572872 | tf_op jit(solution)/shard_map/ppermute | solution.py:313
  22.4 0.0 collective-permute-done.4.swap_ref
  22.4 2.2 %far.1 = (f32[2,16,256]{2,1,0:T(8,128)S(1)}, f32[1024,256]{1,0:T(8,128)S(1)}) custom-call(s32[1]{0:T(128)} %bitcast.ids_ref, bf16[1024,256]{1,0:T(8,128)(2,1)S(1)} %collective-permute-done.4.swap_ref, bf16[1024,256]{1,0:T(8,128)(2,1)S(1)} %get-tuple-element.33.right_ref, bf16[1024,256]{1,0:T(8,128)(2,1)S(1)} %get-tuple-element.34.left_ref, ...), custom_call_target="tpu_custom_call" | custom-call | flops 20000000 | bytes 6000000 | tf_op jit(solution)/shard_map/far/pallas_call | solution.py:246
  24.6 0.0 collective-permute-done.3.relay_ref
  24.7 2.5 %last.1 = (f32[8,36,128]{2,1,0:T(8,128)S(1)}, bf16[1024,256]{1,0:T(8,128)(2,1)}) custom-call(s32[1]{0:T(128)} %bitcast.ids_ref, bf16[1024,256]{1,0:T(8,128)(2,1)S(1)} %collective-permute-done.3.relay_ref, bf16[7,1024,256]{2,1,0:T(8,128)(2,1)S(1)} %get-tuple-element.30.saved, f32[9,2,256]{2,1,0:T(2,128)S(1)} %get-tuple-element.31.par_ref, ...), custom_call_target="tpu_custom_call" | custom-call | flops 20000000 | bytes 6000000 | tf_op jit(solution)/shard_map/last/pallas_call | solution.py:246
  27.2 10.7 %all_to_all.15 = f32[8,36,128]{2,1,0:T(8,128)S(1)} all-to-all(f32[8,36,128]{2,1,0:T(8,128)S(1)} %get-tuple-element.40), channel_id=1, replica_groups=mesh['x'=4,'zl'=2,'zh'=4,'y'=8,'core'=2] {'x','core'}, dimensions={0} | all-to-all | bytes 294912 | tf_op jit(solution)/shard_map/all_to_all | solution.py:333
  37.9 24.3 %all_to_all.16 = f32[8,36,128]{2,1,0:T(8,128)S(1)} all-to-all(f32[8,36,128]{2,1,0:T(8,128)S(1)} %broadcast_in_dim.7), channel_id=1, replica_groups=mesh['x'=4,'zl'=2,'zh'=4,'y'=8,'core'=2] {'y'}, dimensions={0} | all-to-all | bytes 294912 | tf_op jit(solution)/shard_map/all_to_all | solution.py:333
  62.3 17.1 %all_to_all.17.refs_0_ = f32[8,36,128]{2,1,0:T(8,128)S(1)} all-to-all(f32[8,36,128]{2,1,0:T(8,128)S(1)} %broadcast_in_dim.8), channel_id=1, replica_groups=mesh['x'=4,'zl'=2,'zh'=4,'y'=8,'core'=2] {'zl','zh'}, dimensions={0} | all-to-all | bytes 294912 | tf_op jit(solution)/shard_map/all_to_all | solution.py:333
  79.4 0.6 finish.1
  (4 shorter events, 0.1 us)
Async XLA Ops:
  0.6 13.0 %collective-permute-start = (bf16[1024,256]{1,0:T(8,128)(2,1)}, bf16[1024,256]{1,0:T(8,128)(2,1)S(1)}, u32[]{:S(2)}, u32[]{:S(2)}) collective-permute-start(bf16[1024,256]{1,0:T(8,128)(2,1)} %bitcast.11), channel_id=1, source_target_pairs={{14,16},{15,17},{30,32},{31,33},{46,48},{47,49},{16,14},{17,15},{3... | collective-permute-start | bytes 1572872 | tf_op jit(solution)/shard_map/ppermute | solution.py:286
  1.3 15.0 %collective-permute-start.1 = (bf16[1024,256]{1,0:T(8,128)(2,1)}, bf16[1024,256]{1,0:T(8,128)(2,1)S(1)}, u32[]{:S(2)}, u32[]{:S(2)}) collective-permute-start(bf16[1024,256]{1,0:T(8,128)(2,1)} %bitcast.12), channel_id=1, source_target_pairs={{0,2},{2,4},{4,6},{6,8},{8,10},{10,12},{12,14},{1,3},{3,5},{5,7},{... | collective-permute-start | bytes 1572872 | tf_op jit(solution)/shard_map/ppermute | solution.py:287
  4.9 15.5 %collective-permute-start.2 = (bf16[1024,256]{1,0:T(8,128)(2,1)}, bf16[1024,256]{1,0:T(8,128)(2,1)S(1)}, u32[]{:S(2)}, u32[]{:S(2)}) collective-permute-start(bf16[1024,256]{1,0:T(8,128)(2,1)} %bitcast.13), channel_id=1, source_target_pairs={{2,0},{4,2},{6,4},{8,6},{10,8},{12,10},{14,12},{3,1},{5,3},{7,5},{... | collective-permute-start | bytes 1572872 | tf_op jit(solution)/shard_map/ppermute | solution.py:288
  6.2 16.2 %collective-permute-start.4 = (bf16[1024,256]{1,0:T(8,128)(2,1)}, bf16[1024,256]{1,0:T(8,128)(2,1)S(1)}, u32[]{:S(2)}, u32[]{:S(2)}) collective-permute-start(bf16[1024,256]{1,0:T(8,128)(2,1)} %bitcast.14), channel_id=1, source_target_pairs={{0,1},{1,0},{2,3},{3,2},{4,5},{5,4},{6,7},{7,6},{8,9},{9,8},{10,11... | collective-permute-start | bytes 1572872 | tf_op jit(solution)/shard_map/ppermute | solution.py:289
  20.5 4.2 %collective-permute-start.3 = (bf16[1024,256]{1,0:T(8,128)(2,1)S(1)}, bf16[1024,256]{1,0:T(8,128)(2,1)S(1)}, u32[]{:S(2)}, u32[]{:S(2)}) collective-permute-start(bf16[1024,256]{1,0:T(8,128)(2,1)S(1)} %get-tuple-element.29), channel_id=1, source_target_pairs={{0,1},{1,0},{2,3},{3,2},{4,5},{5,4},{6,7},{7,6},{8,9},{9,8},{10,11... | collective-permute-start | bytes 1572872 | tf_op jit(solution)/shard_map/ppermute | solution.py:313

commit v7 on v6

--- a/solution.py
+++ b/solution.py
@@ -76,8 +76,8 @@
     return sums, g
 
 
-def run(work, saved, coef_ref, acc_ref, start, finish):
-    for h in range(2):
+def run(work, saved, coef_ref, acc_ref, start, finish, halves=(0, 1), unroll=1):
+    for h in halves:
         cols = pl.ds(h * LANES, LANES)
 
         def step(r, accs):
@@ -108,7 +108,7 @@
             return tuple(accs)
 
         zero = jnp.zeros((STEP // 2, LANES), F32)
-        accs = lax.fori_loop(0, BLOCK // STEP, step, (zero,) * (SUMS * len(work)))
+        accs = lax.fori_loop(0, BLOCK // STEP, step, (zero,) * (SUMS * len(work)), unroll=unroll)
         for i, (b, _) in enumerate(work):
             for row in range(SUMS):
                 at = (b, pl.ds(row, 1), cols)
@@ -154,8 +154,8 @@
     run(work, saved, coef_ref, acc_ref, lambda n, r, cols: None, keep)
 
 
-def pick_kernel(ids_ref, cross_ref, left_in, right_in, left_ref, right_ref, send_ref):
-    core, place = ids_ref[0] % 2, ids_ref[0] // 2
+def pick_kernel(ids_ref, cross_ref, turn_ref, left_in, right_in, left_ref, right_ref, send_ref):
+    core, detour, place = ids_ref[0] % 2, ids_ref[0] // 2 % 2, ids_ref[0] // 4
 
     def copy(a, b):
         def step(i, carry):
@@ -165,8 +165,9 @@
 
         lax.fori_loop(0, NB, step, 0)
 
-    pl.when(place == 0)(lambda: copy(cross_ref, left_ref))
-    pl.when(place == 1)(lambda: copy(cross_ref, right_ref))
+    for i, to_ref in enumerate((left_ref, right_ref)):
+        pl.when((place == i) & (detour == 0))(lambda to_ref=to_ref: copy(cross_ref, to_ref))
+        pl.when((place == i) & (detour == 1))(lambda to_ref=to_ref: copy(turn_ref, to_ref))
     pl.when(core == 0)(lambda: copy(right_ref, send_ref))
     pl.when(core == 1)(lambda: copy(left_ref, send_ref))
 
@@ -185,10 +186,10 @@
         far = [[(right_ref, 2 * NB)], [(left_ref, 2 * NB)]]
         far[b] = [(swap_ref, NB)] + far[b]
         work = list(enumerate(far))
-        pl.when(core == b)(lambda work=work: run(work, saved, coef_ref, acc_ref, start, keep))
-
-
-def last_kernel(ids_ref, relay_ref, saved, par_ref, coef_ref, far_ref, part_ref, sums_ref, grad_ref, acc_ref):
+        pl.when(core == b)(lambda work=work: run(work, saved, coef_ref, acc_ref, start, keep, unroll=8))
+
+
+def last_kernel(ids_ref, relay_ref, saved, par_ref, coef_ref, far_ref, part_ref, sums_ref, grad_hbm, acc_ref, grad_ref, sems):
     core = ids_ref[0] % 2
     acc_ref[...] = far_ref[...]
 
@@ -198,11 +199,16 @@
     def keep(n, r, cols, value):
         grad_ref[rows_of(0, n, r), cols] = value.astype(grad_ref.dtype)
 
-    for b in range(2):
-        work = [(b, [(relay_ref, NB)])]
-        pl.when(core == 1 - b)(
-            lambda work=work: run(work, saved, coef_ref, acc_ref, start, keep)
-        )
+    copies = []
+    for h in range(2):
+        for b in range(2):
+            work = [(b, [(relay_ref, NB)])]
+            pl.when(core == 1 - b)(
+                lambda work=work, h=h: run(work, saved, coef_ref, acc_ref, start, keep, (h,), 8)
+            )
+        cols = pl.ds(h * LANES, LANES)
+        copies.append(pltpu.make_async_copy(grad_ref.at[:, cols], grad_hbm.at[:, cols], sems.at[h]))
+        copies[h].start()
     f = [[par_ref[2 * i + j] for j in range(2)] for i in range(2)]
     mix = [par_ref[4 + i] for i in range(LEVELS + 1)]
     acc = [acc_ref[:, i, :] for i in range(SUMS)]
@@ -222,6 +228,8 @@
                 sums_ref[0, pl.ds(at, 1), :] = value[b : b + 1, h * LANES : (h + 1) * LANES]
     for copy in range(1, sums_ref.shape[0]):
         sums_ref[copy] = sums_ref[0]
+    for copy in copies:
+        copy.wait()
 
 
 def finish_kernel(factor, got_ref, filters_ref, mixing_ref):
@@ -240,14 +248,14 @@
                     mixing_ref[j - 4, pl.ds(b, 1), cols] = row
 
 
-def call(kernel, name, outs, args, spaces, scratch=(), flops=0, aliases={}):
-    space = {"s": pltpu.SMEM, "v": pltpu.VMEM, "h": pltpu.HBM}
+def call(kernel, name, outs, args, spaces, scratch=(), flops=0, aliases={}, spaces_out=None):
+    space = {"s": pltpu.SMEM, "v": pltpu.VMEM, "h": pltpu.HBM, "a": pl.ANY}
     args = [pltpu.with_memory_space_constraint(a, pltpu.HBM) if k == "h" else a for a, k in zip(args, spaces)]
     return pl.pallas_call(
         kernel,
         out_shape=outs,
         in_specs=[pl.BlockSpec(memory_space=space[k]) for k in spaces],
-        out_specs=(pl.BlockSpec(memory_space=pltpu.VMEM),) * len(outs),
+        out_specs=tuple(pl.BlockSpec(memory_space=space[k]) for k in spaces_out or "v" * len(outs)),
         scratch_shapes=scratch,
         input_output_aliases=aliases,
         compiler_params=pltpu.CompilerParams(vmem_limit_bytes=8 * 1024 * 1024),
@@ -256,16 +264,31 @@
     )(*args)
 
 
+SEAM = ("zl",) + CTX
+
+
 def routes():
-    zs, ys, cores = (lax.axis_size(axis) for axis in CTX)
-
-    def at(z, y, c):
-        return (z * ys + y) * cores + c
+    halves, zs, ys, cores = (lax.axis_size(axis) for axis in SEAM)
+
+    def at(half, z, y, c):
+        return ((half * zs + z) * ys + y) * cores + c
 
     spots = [(z, c) for z in range(zs) for c in range(cores)]
-    inner = [(at(z, y, c), at(z, y + 1, c)) for z, c in spots for y in range(ys - 1)]
-    cross = [(at(z, ys - 1, c), at(z + 1, 0, c)) for z, c in spots if z + 1 < zs]
-    return inner, cross + [(b, a) for a, b in cross]
+    inner = [(at(0, z, y, c), at(0, z, y + 1, c)) for z, c in spots for y in range(ys - 1)]
+    cross, hop, turn = [], [], []
+    end = ys - 1
+    for half in range(halves):
+        for z, c in spots:
+            if z + 1 == zs:
+                continue
+            last, first = at(half, z, end, c), at(half, z + 1, 0, c)
+            if (half, c) != (0, 1):
+                cross += [(last, first), (first, last)]
+                continue
+            for a, middle, b in ((last, at(half, z + 1, end, c), first), (first, at(half, z, 0, c), last)):
+                hop.append((a, middle))
+                turn.append((middle, b))
+    return inner, cross, hop, turn
 
 
 def body(level_input, saved_forward, saved_reverse, filters, mixing, cotangent):
@@ -278,12 +301,14 @@
     acc = jax.ShapeDtypeStruct((2, ROWS, width), F32)
     part = jax.ShapeDtypeStruct((rows, width), F32)
     pair = [(0, 1), (1, 0)]
-    inner, cross = routes()
+    inner, cross, hop, turn = routes()
     y = lax.axis_index("y")
     place = jnp.where(y == 0, 0, jnp.where(y == lax.axis_size("y") - 1, 1, 2))
-    ids = (core + 2 * place).astype(jnp.int32).reshape(1)
+    detour = jnp.where(lax.axis_index("zl") == 0, core, 0)
+    ids = (core + 2 * detour + 4 * place).astype(jnp.int32).reshape(1)
     ids, dy = lax.optimization_barrier((ids, dy))
-    crossed = lax.ppermute(dy, CTX, cross)
+    crossed = lax.ppermute(dy, SEAM, cross)
+    hopped = lax.ppermute(dy, SEAM, hop)
     left = lax.ppermute(dy, CTX, inner)
     right = lax.ppermute(dy, CTX, [(b, a) for a, b in inner])
     swap = lax.ppermute(dy, "core", pair)
@@ -307,9 +332,11 @@
         ],
         flops=20_000_000,
     )
-    crossed, left, right, acc_near = lax.optimization_barrier((crossed, left, right, acc_near))
+    hopped, acc_near = lax.optimization_barrier((hopped, acc_near))
+    turned = lax.ppermute(hopped, SEAM, turn)
+    crossed, turned, left, right = lax.optimization_barrier((crossed, turned, left, right))
     halo = jax.ShapeDtypeStruct(dy.shape, dy.dtype)
-    left, right, send = call(pick_kernel, "pick", (halo,) * 3, (ids, crossed, left, right), "svvv", aliases={2: 0, 3: 1})
+    left, right, send = call(pick_kernel, "pick", (halo,) * 3, (ids, crossed, turned, left, right), "svvvv", aliases={3: 0, 4: 1})
     relay = lax.ppermute(send, "core", pair)
     acc_far, part_far = call(
         far_kernel,
@@ -325,7 +352,12 @@
         (jax.ShapeDtypeStruct((8, 18 * width // LANES, LANES), F32), jax.ShapeDtypeStruct((rows, width), jnp.bfloat16)),
         (ids, relay, saved, par, coef, acc_far, part_far),
         "svvvvvv",
-        scratch=[pltpu.VMEM((2, ROWS, width), F32)],
+        scratch=[
+            pltpu.VMEM((2, ROWS, width), F32),
+            pltpu.VMEM((rows, width), dy.dtype),
+            pltpu.SemaphoreType.DMA((2,)),
+        ],
+        spaces_out="va",
         flops=20_000_000,
     )
     groups = (("x", "core"), ("y",), ("zl", "zh"))

time: 80.4 us -> 76.8 us (0.955)
  blocking collectives: 52.2 us -> 48.4 us
  starting transfers between devices: 9.34 us -> 10.7 us
    all_to_all x3, blocking collectives: 52.2 us -> 48.4 us  [body(): got = lax.all_to_all(sums, axes, 0, 0)]
    ppermute x1 -> x3, starting transfers between devices: 0.69 us -> 2.08 us  [the longest x1 0.69 us: body(): hopped = lax.ppermute(dy, SEAM, hop)]
  transfers between devices with their start and end apart: 5 -> 7, of which waited for: 2 -> 2; matrix products, arithmetic and copies ran while one was open for 0% -> 0% of each run, Pallas kernels for 10% -> 10%
where the time goes in v7:
time: 76.8 us; the launch traced here: 76.5 us
  blocking collectives  48.4 us (63%)
  starting transfers between devices  10.7 us (14%)
  Pallas kernels  10.6 us (14%)
  waiting for transfers between devices  5.89 us (8%)
  between operations  0.81 us (1%)
    all_to_all x3, blocking collectives, body(): got = lax.all_to_all(sums, axes, 0, 0)  48.4 us
    pallas_call x5, Pallas kernels, call(): pl.pallas_call(kernel, out_shape=outs, in_specs=[pl.BlockSpec(memory_spac...  10.6 us
    ppermute x1, waiting for transfers between devices, body(): right = lax.ppermute(dy, CTX, [(b, a) for a, b in inner])  4.04 us
    ppermute x1, starting transfers between devices, body(): left = lax.ppermute(dy, CTX, inner)  3.51 us
    ppermute x1, starting transfers between devices, body(): swap = lax.ppermute(dy, 'core', pair)  1.92 us
    ppermute x1, starting transfers between devices, body(): relay = lax.ppermute(send, 'core', pair)  1.92 us
    ppermute x1, waiting for transfers between devices, body(): left = lax.ppermute(dy, CTX, inner)  1.84 us
  transfers between devices with their start and end apart: 7, of which 2 were waited for; matrix products, arithmetic and copies ran while one was open for 0% of the time, Pallas kernels for 10%

profile of v7, /device:TPU:64, one launch (start us, length us, event | category | flops | bytes accessed | tf_op | source)
XLA Modules:
  0.0 76.5 jit_solution(15934552821132746662)
XLA Ops:
  0.7 0.7 collective-permute-start.1
  1.4 0.7 collective-permute-start
  2.1 3.5 %collective-permute-start.3 = (bf16[1024,256]{1,0:T(8,128)(2,1)}, bf16[1024,256]{1,0:T(8,128)(2,1)S(1)}, u32[]{:S(2)}, u32[]{:S(2)}) collective-permute-start(bf16[1024,256]{1,0:T(8,128)(2,1)} %bitcast.13), channel_id=1, source_target_pairs={{0,2},{2,4},{4,6},{6,8},{8,10},{10,12},{12,14},{1,3},{3,5},{5,7},{... | collective-permute-start | bytes 1572872 | tf_op jit(solution)/shard_map/ppermute | solution.py:312
  5.6 1.3 %collective-permute-start.4 = (bf16[1024,256]{1,0:T(8,128)(2,1)}, bf16[1024,256]{1,0:T(8,128)(2,1)S(1)}, u32[]{:S(2)}, u32[]{:S(2)}) collective-permute-start(bf16[1024,256]{1,0:T(8,128)(2,1)} %bitcast.14), channel_id=1, source_target_pairs={{2,0},{4,2},{6,4},{8,6},{10,8},{12,10},{14,12},{3,1},{5,3},{7,5},{... | collective-permute-start | bytes 1572872 | tf_op jit(solution)/shard_map/ppermute | solution.py:313
  6.9 0.0 copy-start
  6.9 5.6 %near.1 = (f32[2,16,256]{2,1,0:T(8,128)S(1)}, f32[1024,256]{1,0:T(8,128)S(1)}, f32[2,10,8,256]{3,2,1,0:T(8,128)S(1)}, f32[9,2,256]{2,1,0:T(2,128)S(1)}, bf16[7,1024,256]{2,1,0:T(8,128)(2,1)S(1)}) custom-call(bf16[1024,256]{1,0:T(8,128)(2,1)} %bitcast.15, bf16[1024,256]{1,0:T(8,128)(2,1)} %bitcast.10, bf16[3,1024,256]{2,1,0:T(8,128)(2,1)} %bitcast.8, ...), custom_call_target="tpu_custom_call" | custom-call | flops 20000000 | bytes 6000000 | tf_op jit(solution)/shard_map/near/pallas_call | solution.py:254
  12.5 0.0 collective-permute-done.1
  12.5 0.7 collective-permute-start.2
  13.2 0.0 copy-done
  13.2 1.9 %collective-permute-start.6 = (bf16[1024,256]{1,0:T(8,128)(2,1)S(1)}, bf16[1024,256]{1,0:T(8,128)(2,1)S(1)}, u32[]{:S(2)}, u32[]{:S(2)}) collective-permute-start(bf16[1024,256]{1,0:T(8,128)(2,1)S(1)} %bitcast.16), channel_id=1, source_target_pairs={{0,1},{1,0},{2,3},{3,2},{4,5},{5,4},{6,7},{7,6},{8,9},{9,8},{10,11... | collective-permute-start | bytes 1572872 | tf_op jit(solution)/shard_map/ppermute | solution.py:314
  15.2 0.0 collective-permute-done.cross_ref
  15.2 1.8 %collective-permute-done.3.left_in = bf16[1024,256]{1,0:T(8,128)(2,1)S(1)} collective-permute-done((bf16[1024,256]{1,0:T(8,128)(2,1)}, bf16[1024,256]{1,0:T(8,128)(2,1)S(1)}, u32[]{:S(2)}, u32[]{:S(2)}) %collective-permute-start.3) | collective-permute-done | bytes 524320 | tf_op jit(solution)/shard_map/ppermute | solution.py:312
  17.0 4.0 %collective-permute-done.4.right_in = bf16[1024,256]{1,0:T(8,128)(2,1)S(1)} collective-permute-done((bf16[1024,256]{1,0:T(8,128)(2,1)}, bf16[1024,256]{1,0:T(8,128)(2,1)S(1)}, u32[]{:S(2)}, u32[]{:S(2)}) %collective-permute-start.4) | collective-permute-done | bytes 524320 | tf_op jit(solution)/shard_map/ppermute | solution.py:313
  21.1 0.0 collective-permute-done.2.turn_ref
  21.1 0.1 pick.1
  21.2 1.9 %collective-permute-start.5 = (bf16[1024,256]{1,0:T(8,128)(2,1)S(1)}, bf16[1024,256]{1,0:T(8,128)(2,1)S(1)}, u32[]{:S(2)}, u32[]{:S(2)}) collective-permute-start(bf16[1024,256]{1,0:T(8,128)(2,1)S(1)} %get-tuple-element.33), channel_id=1, source_target_pairs={{0,1},{1,0},{2,3},{3,2},{4,5},{5,4},{6,7},{7,6},{8,9},{9,8},{10,11... | collective-permute-start | bytes 1572872 | tf_op jit(solution)/shard_map/ppermute | solution.py:340
  23.1 0.0 collective-permute-done.6.swap_ref
  23.1 2.1 %far.1 = (f32[2,16,256]{2,1,0:T(8,128)S(1)}, f32[1024,256]{1,0:T(8,128)S(1)}) custom-call(s32[1]{0:T(128)} %bitcast.ids_ref, bf16[1024,256]{1,0:T(8,128)(2,1)S(1)} %collective-permute-done.6.swap_ref, bf16[1024,256]{1,0:T(8,128)(2,1)S(1)} %get-tuple-element.37.right_ref, bf16[1024,256]{1,0:T(8,128)(2,1)S(1)} %get-tuple-element.38.left_ref, ...), custom_call_target="tpu_custom_call" | custom-call | flops 20000000 | bytes 6000000 | tf_op jit(solution)/shard_map/far/pallas_call | solution.py:254
  25.2 0.0 collective-permute-done.5.relay_ref
  25.2 2.2 %last.1 = (f32[8,36,128]{2,1,0:T(8,128)S(1)}, bf16[1024,256]{1,0:T(8,128)(2,1)}) custom-call(s32[1]{0:T(128)} %bitcast.ids_ref, bf16[1024,256]{1,0:T(8,128)(2,1)S(1)} %collective-permute-done.5.relay_ref, bf16[7,1024,256]{2,1,0:T(8,128)(2,1)S(1)} %get-tuple-element.34.saved, f32[9,2,256]{2,1,0:T(2,128)S(1)} %get-tuple-element.35.par_ref, ...), custom_call_target="tpu_custom_call" | custom-call | flops 20000000 | bytes 6000000 | tf_op jit(solution)/shard_map/last/pallas_call | solution.py:254
  27.4 10.8 %all_to_all.15 = f32[8,36,128]{2,1,0:T(8,128)S(1)} all-to-all(f32[8,36,128]{2,1,0:T(8,128)S(1)} %get-tuple-element.44), channel_id=1, replica_groups=mesh['x'=4,'zl'=2,'zh'=4,'y'=8,'core'=2] {'x','core'}, dimensions={0} | all-to-all | bytes 294912 | tf_op jit(solution)/shard_map/all_to_all | solution.py:365
  38.2 20.5 %all_to_all.16 = f32[8,36,128]{2,1,0:T(8,128)S(1)} all-to-all(f32[8,36,128]{2,1,0:T(8,128)S(1)} %broadcast_in_dim.7), channel_id=1, replica_groups=mesh['x'=4,'zl'=2,'zh'=4,'y'=8,'core'=2] {'y'}, dimensions={0} | all-to-all | bytes 294912 | tf_op jit(solution)/shard_map/all_to_all | solution.py:365
  58.7 17.1 %all_to_all.17.refs_0_ = f32[8,36,128]{2,1,0:T(8,128)S(1)} all-to-all(f32[8,36,128]{2,1,0:T(8,128)S(1)} %broadcast_in_dim.8), channel_id=1, replica_groups=mesh['x'=4,'zl'=2,'zh'=4,'y'=8,'core'=2] {'zl','zh'}, dimensions={0} | all-to-all | bytes 294912 | tf_op jit(solution)/shard_map/all_to_all | solution.py:365
  75.9 0.6 finish.1
  (4 shorter events, 0.1 us)
Async XLA Ops:
  0.7 11.9 %collective-permute-start.1 = (bf16[1024,256]{1,0:T(8,128)(2,1)}, bf16[1024,256]{1,0:T(8,128)(2,1)S(1)}, u32[]{:S(2)}, u32[]{:S(2)}) collective-permute-start(bf16[1024,256]{1,0:T(8,128)(2,1)} %bitcast.11), channel_id=1, source_target_pairs={{15,31},{17,1},{31,47},{33,17},{47,63},{49,33},{143,159},{145,129}... | collective-permute-start | bytes 1572872 | tf_op jit(solution)/shard_map/ppermute | solution.py:311
  1.4 13.8 %collective-permute-start = (bf16[1024,256]{1,0:T(8,128)(2,1)}, bf16[1024,256]{1,0:T(8,128)(2,1)S(1)}, u32[]{:S(2)}, u32[]{:S(2)}) collective-permute-start(bf16[1024,256]{1,0:T(8,128)(2,1)} %bitcast.12), channel_id=1, source_target_pairs={{14,16},{16,14},{30,32},{32,30},{46,48},{48,46},{78,80},{80,78},{7... | collective-permute-start | bytes 1572872 | tf_op jit(solution)/shard_map/ppermute | solution.py:310
  2.1 15.0 %collective-permute-start.3 = (bf16[1024,256]{1,0:T(8,128)(2,1)}, bf16[1024,256]{1,0:T(8,128)(2,1)S(1)}, u32[]{:S(2)}, u32[]{:S(2)}) collective-permute-start(bf16[1024,256]{1,0:T(8,128)(2,1)} %bitcast.13), channel_id=1, source_target_pairs={{0,2},{2,4},{4,6},{6,8},{8,10},{10,12},{12,14},{1,3},{3,5},{5,7},{... | collective-permute-start | bytes 1572872 | tf_op jit(solution)/shard_map/ppermute | solution.py:312
  5.6 15.5 %collective-permute-start.4 = (bf16[1024,256]{1,0:T(8,128)(2,1)}, bf16[1024,256]{1,0:T(8,128)(2,1)S(1)}, u32[]{:S(2)}, u32[]{:S(2)}) collective-permute-start(bf16[1024,256]{1,0:T(8,128)(2,1)} %bitcast.14), channel_id=1, source_target_pairs={{2,0},{4,2},{6,4},{8,6},{10,8},{12,10},{14,12},{3,1},{5,3},{7,5},{... | collective-permute-start | bytes 1572872 | tf_op jit(solution)/shard_map/ppermute | solution.py:313
  6.9 6.4 %copy-start = (bf16[1,1024,256]{2,1,0:T(8,128)(2,1)S(1)}, bf16[1,1024,256]{2,1,0:T(8,128)(2,1)}, u32[]{:S(2)}) copy-start(bf16[1,1024,256]{2,1,0:T(8,128)(2,1)} %param.11) | copy-start | bytes 1572868
  12.5 8.5 %collective-permute-start.2 = (bf16[1024,256]{1,0:T(8,128)(2,1)S(1)}, bf16[1024,256]{1,0:T(8,128)(2,1)S(1)}, u32[]{:S(2)}, u32[]{:S(2)}) collective-permute-start(bf16[1024,256]{1,0:T(8,128)(2,1)S(1)} %collective-permute-done.1), channel_id=1, source_target_pairs={{31,17},{1,15},{47,33},{17,31},{63,49},{33,47},{159,145},{129,143}... | collective-permute-start | bytes 1572872 | tf_op jit(solution)/shard_map/ppermute | solution.py:336
  13.2 9.9 %collective-permute-start.6 = (bf16[1024,256]{1,0:T(8,128)(2,1)S(1)}, bf16[1024,256]{1,0:T(8,128)(2,1)S(1)}, u32[]{:S(2)}, u32[]{:S(2)}) collective-permute-start(bf16[1024,256]{1,0:T(8,128)(2,1)S(1)} %bitcast.16), channel_id=1, source_target_pairs={{0,1},{1,0},{2,3},{3,2},{4,5},{5,4},{6,7},{7,6},{8,9},{9,8},{10,11... | collective-permute-start | bytes 1572872 | tf_op jit(solution)/shard_map/ppermute | solution.py:314
  21.2 4.0 %collective-permute-start.5 = (bf16[1024,256]{1,0:T(8,128)(2,1)S(1)}, bf16[1024,256]{1,0:T(8,128)(2,1)S(1)}, u32[]{:S(2)}, u32[]{:S(2)}) collective-permute-start(bf16[1024,256]{1,0:T(8,128)(2,1)S(1)} %get-tuple-element.33), channel_id=1, source_target_pairs={{0,1},{1,0},{2,3},{3,2},{4,5},{5,4},{6,7},{7,6},{8,9},{9,8},{10,11... | collective-permute-start | bytes 1572872 | tf_op jit(solution)/shard_map/ppermute | solution.py:340

commit v8 on v7

--- a/solution.py
+++ b/solution.py
@@ -154,20 +154,26 @@
     run(work, saved, coef_ref, acc_ref, lambda n, r, cols: None, keep)
 
 
-def pick_kernel(ids_ref, cross_ref, turn_ref, left_in, right_in, left_ref, right_ref, send_ref):
-    core, detour, place = ids_ref[0] % 2, ids_ref[0] // 2 % 2, ids_ref[0] // 4
-
-    def copy(a, b):
+def pick_kernel(ids_ref, even_ref, odd_ref, cross_ref, turn_ref, left_ref, right_ref, send_ref):
+    ids = ids_ref[0]
+    core, detour, odd, place = ids % 2, ids // 2 % 2, ids // 4 % 2, ids // 8
+
+    def copy(a, *to):
         def step(i, carry):
             rows = pl.ds(pl.multiple_of(i * BLOCK, BLOCK), BLOCK)
-            b[rows, :] = a[rows, :]
+            value = a[rows, :]
+            for b in to:
+                b[rows, :] = value
             return carry
 
         lax.fori_loop(0, NB, step, 0)
 
-    for i, to_ref in enumerate((left_ref, right_ref)):
-        pl.when((place == i) & (detour == 0))(lambda to_ref=to_ref: copy(cross_ref, to_ref))
-        pl.when((place == i) & (detour == 1))(lambda to_ref=to_ref: copy(turn_ref, to_ref))
+    for side, to_ref in enumerate((left_ref, right_ref)):
+        edge = place == side
+        pl.when(edge & (detour == 0))(lambda to_ref=to_ref: copy(cross_ref, to_ref))
+        pl.when(edge & (detour == 1))(lambda to_ref=to_ref: copy(turn_ref, to_ref))
+        pl.when((place != side) & (odd != side))(lambda to_ref=to_ref: copy(even_ref, to_ref))
+        pl.when((place != side) & (odd == side))(lambda to_ref=to_ref: copy(odd_ref, to_ref))
     pl.when(core == 0)(lambda: copy(right_ref, send_ref))
     pl.when(core == 1)(lambda: copy(left_ref, send_ref))
 
@@ -248,7 +254,7 @@
                     mixing_ref[j - 4, pl.ds(b, 1), cols] = row
 
 
-def call(kernel, name, outs, args, spaces, scratch=(), flops=0, aliases={}, spaces_out=None):
+def call(kernel, name, outs, args, spaces, scratch=(), flops=0, spaces_out=None):
     space = {"s": pltpu.SMEM, "v": pltpu.VMEM, "h": pltpu.HBM, "a": pl.ANY}
     args = [pltpu.with_memory_space_constraint(a, pltpu.HBM) if k == "h" else a for a, k in zip(args, spaces)]
     return pl.pallas_call(
@@ -257,7 +263,6 @@
         in_specs=[pl.BlockSpec(memory_space=space[k]) for k in spaces],
         out_specs=tuple(pl.BlockSpec(memory_space=space[k]) for k in spaces_out or "v" * len(outs)),
         scratch_shapes=scratch,
-        input_output_aliases=aliases,
         compiler_params=pltpu.CompilerParams(vmem_limit_bytes=8 * 1024 * 1024),
         cost_estimate=pl.CostEstimate(flops=flops, bytes_accessed=6_000_000, transcendentals=0),
         name=name,
@@ -274,7 +279,8 @@
         return ((half * zs + z) * ys + y) * cores + c
 
     spots = [(z, c) for z in range(zs) for c in range(cores)]
-    inner = [(at(0, z, y, c), at(0, z, y + 1, c)) for z, c in spots for y in range(ys - 1)]
+    next_to = [[(at(0, z, y, c), at(0, z, y + 1, c)) for z, c in spots for y in range(odd, ys - 1, 2)] for odd in range(2)]
+    even, odd = [pairs + [(b, a) for a, b in pairs] for pairs in next_to]
     cross, hop, turn = [], [], []
     end = ys - 1
     for half in range(halves):
@@ -288,7 +294,7 @@
             for a, middle, b in ((last, at(half, z + 1, end, c), first), (first, at(half, z, 0, c), last)):
                 hop.append((a, middle))
                 turn.append((middle, b))
-    return inner, cross, hop, turn
+    return even, odd, cross, hop, turn
 
 
 def body(level_input, saved_forward, saved_reverse, filters, mixing, cotangent):
@@ -301,16 +307,16 @@
     acc = jax.ShapeDtypeStruct((2, ROWS, width), F32)
     part = jax.ShapeDtypeStruct((rows, width), F32)
     pair = [(0, 1), (1, 0)]
-    inner, cross, hop, turn = routes()
+    even, odd, cross, hop, turn = routes()
     y = lax.axis_index("y")
     place = jnp.where(y == 0, 0, jnp.where(y == lax.axis_size("y") - 1, 1, 2))
     detour = jnp.where(lax.axis_index("zl") == 0, core, 0)
-    ids = (core + 2 * detour + 4 * place).astype(jnp.int32).reshape(1)
+    ids = (core + 2 * detour + 4 * (y % 2) + 8 * place).astype(jnp.int32).reshape(1)
     ids, dy = lax.optimization_barrier((ids, dy))
     crossed = lax.ppermute(dy, SEAM, cross)
     hopped = lax.ppermute(dy, SEAM, hop)
-    left = lax.ppermute(dy, CTX, inner)
-    right = lax.ppermute(dy, CTX, [(b, a) for a, b in inner])
+    evens = lax.ppermute(dy, CTX, even)
+    odds = lax.ppermute(dy, CTX, odd)
     swap = lax.ppermute(dy, "core", pair)
     acc_near, part_near, coef, par, saved = call(
         near_kernel,
@@ -334,9 +340,9 @@
     )
     hopped, acc_near = lax.optimization_barrier((hopped, acc_near))
     turned = lax.ppermute(hopped, SEAM, turn)
-    crossed, turned, left, right = lax.optimization_barrier((crossed, turned, left, right))
+    crossed, turned, evens, odds = lax.optimization_barrier((crossed, turned, evens, odds))
     halo = jax.ShapeDtypeStruct(dy.shape, dy.dtype)
-    left, right, send = call(pick_kernel, "pick", (halo,) * 3, (ids, crossed, turned, left, right), "svvvv", aliases={3: 0, 4: 1})
+    left, right, send = call(pick_kernel, "pick", (halo,) * 3, (ids, evens, odds, crossed, turned), "svvvv")
     relay = lax.ppermute(send, "core", pair)
     acc_far, part_far = call(
         far_kernel,

time: 76.8 us -> 75.6 us (0.984)
  waiting for transfers between devices: 5.89 us -> 3.28 us
  blocking collectives: 48.4 us -> 50.4 us
    ppermute x2, waiting for transfers between devices: 5.88 us -> 3.27 us  [the longest x1 3.27 us: body(): evens = lax.ppermute(dy, CTX, even)]
    all_to_all x3, blocking collectives: 48.4 us -> 50.4 us  [body(): got = lax.all_to_all(sums, axes, 0, 0)]
  transfers between devices with their start and end apart: 7 -> 7, of which waited for: 2 -> 1; matrix products, arithmetic and copies ran while one was open for 0% -> 0% of each run, Pallas kernels for 10% -> 10%
where the time goes in v8:
time: 75.6 us; the launch traced here: 75.3 us
  blocking collectives  50.4 us (67%)
  Pallas kernels  10.6 us (14%)
  starting transfers between devices  10.1 us (13%)
  waiting for transfers between devices  3.28 us (4%)
  between operations  0.82 us (1%)
    all_to_all x3, blocking collectives, body(): got = lax.all_to_all(sums, axes, 0, 0)  50.4 us
    pallas_call x5, Pallas kernels, call(): pl.pallas_call(kernel, out_shape=outs, in_specs=[pl.BlockSpec(memory_spac...  10.6 us
    ppermute x1, starting transfers between devices, body(): evens = lax.ppermute(dy, CTX, even)  3.48 us
    ppermute x1, waiting for transfers between devices, body(): evens = lax.ppermute(dy, CTX, even)  3.27 us
    ppermute x1, starting transfers between devices, body(): relay = lax.ppermute(send, 'core', pair)  1.92 us
    ppermute x1, starting transfers between devices, body(): swap = lax.ppermute(dy, 'core', pair)  1.92 us
  transfers between devices with their start and end apart: 7, of which 1 were waited for; matrix products, arithmetic and copies ran while one was open for 0% of the time, Pallas kernels for 10%

profile of v8, /device:TPU:64, one launch (start us, length us, event | category | flops | bytes accessed | tf_op | source)
XLA Modules:
  0.0 75.3 jit_solution(5321566502639375929)
XLA Ops:
  0.7 0.7 collective-permute-start.1
  1.4 0.7 collective-permute-start
  2.1 3.5 %collective-permute-start.3 = (bf16[1024,256]{1,0:T(8,128)(2,1)}, bf16[1024,256]{1,0:T(8,128)(2,1)S(1)}, u32[]{:S(2)}, u32[]{:S(2)}) collective-permute-start(bf16[1024,256]{1,0:T(8,128)(2,1)} %bitcast.13), channel_id=1, source_target_pairs={{0,2},{4,6},{8,10},{12,14},{1,3},{5,7},{9,11},{13,15},{16,18},{20,... | collective-permute-start | bytes 1572872 | tf_op jit(solution)/shard_map/ppermute | solution.py:318
  5.6 0.7 collective-permute-start.4
  6.3 0.0 copy-start
  6.3 5.6 %near.1 = (f32[2,16,256]{2,1,0:T(8,128)S(1)}, f32[1024,256]{1,0:T(8,128)S(1)}, f32[2,10,8,256]{3,2,1,0:T(8,128)S(1)}, f32[9,2,256]{2,1,0:T(2,128)S(1)}, bf16[7,1024,256]{2,1,0:T(8,128)(2,1)S(1)}) custom-call(bf16[1024,256]{1,0:T(8,128)(2,1)} %bitcast.15, bf16[1024,256]{1,0:T(8,128)(2,1)} %bitcast.10, bf16[3,1024,256]{2,1,0:T(8,128)(2,1)} %bitcast.8, ...), custom_call_target="tpu_custom_call" | custom-call | flops 20000000 | bytes 6000000 | tf_op jit(solution)/shard_map/near/pallas_call | solution.py:260
  11.9 0.0 collective-permute-done.1
  11.9 0.7 collective-permute-start.2
  12.6 0.0 copy-done
  12.6 1.9 %collective-permute-start.6 = (bf16[1024,256]{1,0:T(8,128)(2,1)S(1)}, bf16[1024,256]{1,0:T(8,128)(2,1)S(1)}, u32[]{:S(2)}, u32[]{:S(2)}) collective-permute-start(bf16[1024,256]{1,0:T(8,128)(2,1)S(1)} %bitcast.16), channel_id=1, source_target_pairs={{0,1},{1,0},{2,3},{3,2},{4,5},{5,4},{6,7},{7,6},{8,9},{9,8},{10,11... | collective-permute-start | bytes 1572872 | tf_op jit(solution)/shard_map/ppermute | solution.py:320
  14.6 0.0 collective-permute-done.cross_ref
  14.6 3.3 %collective-permute-done.3.even_ref = bf16[1024,256]{1,0:T(8,128)(2,1)S(1)} collective-permute-done((bf16[1024,256]{1,0:T(8,128)(2,1)}, bf16[1024,256]{1,0:T(8,128)(2,1)S(1)}, u32[]{:S(2)}, u32[]{:S(2)}) %collective-permute-start.3) | collective-permute-done | bytes 524320 | tf_op jit(solution)/shard_map/ppermute | solution.py:318
  17.8 0.0 collective-permute-done.4.odd_ref
  17.8 0.0 collective-permute-done.2.turn_ref
  17.8 0.2 pick.1
  18.0 1.9 %collective-permute-start.5 = (bf16[1024,256]{1,0:T(8,128)(2,1)S(1)}, bf16[1024,256]{1,0:T(8,128)(2,1)S(1)}, u32[]{:S(2)}, u32[]{:S(2)}) collective-permute-start(bf16[1024,256]{1,0:T(8,128)(2,1)S(1)} %get-tuple-element.33), channel_id=1, source_target_pairs={{0,1},{1,0},{2,3},{3,2},{4,5},{5,4},{6,7},{7,6},{8,9},{9,8},{10,11... | collective-permute-start | bytes 1572872 | tf_op jit(solution)/shard_map/ppermute | solution.py:346
  20.0 0.0 collective-permute-done.6.swap_ref
  20.0 2.1 %far.1 = (f32[2,16,256]{2,1,0:T(8,128)S(1)}, f32[1024,256]{1,0:T(8,128)S(1)}) custom-call(s32[1]{0:T(128)} %bitcast.ids_ref, bf16[1024,256]{1,0:T(8,128)(2,1)S(1)} %collective-permute-done.6.swap_ref, bf16[1024,256]{1,0:T(8,128)(2,1)S(1)} %get-tuple-element.37.right_ref, bf16[1024,256]{1,0:T(8,128)(2,1)S(1)} %get-tuple-element.38.left_ref, ...), custom_call_target="tpu_custom_call" | custom-call | flops 20000000 | bytes 6000000 | tf_op jit(solution)/shard_map/far/pallas_call | solution.py:260
  22.0 0.0 collective-permute-done.5.relay_ref
  22.0 2.2 %last.1 = (f32[8,36,128]{2,1,0:T(8,128)S(1)}, bf16[1024,256]{1,0:T(8,128)(2,1)}) custom-call(s32[1]{0:T(128)} %bitcast.ids_ref, bf16[1024,256]{1,0:T(8,128)(2,1)S(1)} %collective-permute-done.5.relay_ref, bf16[7,1024,256]{2,1,0:T(8,128)(2,1)S(1)} %get-tuple-element.34.saved, f32[9,2,256]{2,1,0:T(2,128)S(1)} %get-tuple-element.35.par_ref, ...), custom_call_target="tpu_custom_call" | custom-call | flops 20000000 | bytes 6000000 | tf_op jit(solution)/shard_map/last/pallas_call | solution.py:260
  24.2 10.8 %all_to_all.15 = f32[8,36,128]{2,1,0:T(8,128)S(1)} all-to-all(f32[8,36,128]{2,1,0:T(8,128)S(1)} %get-tuple-element.44), channel_id=1, replica_groups=mesh['x'=4,'zl'=2,'zh'=4,'y'=8,'core'=2] {'x','core'}, dimensions={0} | all-to-all | bytes 294912 | tf_op jit(solution)/shard_map/all_to_all | solution.py:371
  35.0 23.7 %all_to_all.16 = f32[8,36,128]{2,1,0:T(8,128)S(1)} all-to-all(f32[8,36,128]{2,1,0:T(8,128)S(1)} %broadcast_in_dim.7), channel_id=1, replica_groups=mesh['x'=4,'zl'=2,'zh'=4,'y'=8,'core'=2] {'y'}, dimensions={0} | all-to-all | bytes 294912 | tf_op jit(solution)/shard_map/all_to_all | solution.py:371
  58.8 15.8 %all_to_all.17.refs_0_ = f32[8,36,128]{2,1,0:T(8,128)S(1)} all-to-all(f32[8,36,128]{2,1,0:T(8,128)S(1)} %broadcast_in_dim.8), channel_id=1, replica_groups=mesh['x'=4,'zl'=2,'zh'=4,'y'=8,'core'=2] {'zl','zh'}, dimensions={0} | all-to-all | bytes 294912 | tf_op jit(solution)/shard_map/all_to_all | solution.py:371
  74.6 0.6 finish.1
  (4 shorter events, 0.1 us)
Async XLA Ops:
  0.7 11.2 %collective-permute-start.1 = (bf16[1024,256]{1,0:T(8,128)(2,1)}, bf16[1024,256]{1,0:T(8,128)(2,1)S(1)}, u32[]{:S(2)}, u32[]{:S(2)}) collective-permute-start(bf16[1024,256]{1,0:T(8,128)(2,1)} %bitcast.11), channel_id=1, source_target_pairs={{15,31},{17,1},{31,47},{33,17},{47,63},{49,33},{143,159},{145,129}... | collective-permute-start | bytes 1572872 | tf_op jit(solution)/shard_map/ppermute | solution.py:317
  1.4 13.2 %collective-permute-start = (bf16[1024,256]{1,0:T(8,128)(2,1)}, bf16[1024,256]{1,0:T(8,128)(2,1)S(1)}, u32[]{:S(2)}, u32[]{:S(2)}) collective-permute-start(bf16[1024,256]{1,0:T(8,128)(2,1)} %bitcast.12), channel_id=1, source_target_pairs={{14,16},{16,14},{30,32},{32,30},{46,48},{48,46},{78,80},{80,78},{7... | collective-permute-start | bytes 1572872 | tf_op jit(solution)/shard_map/ppermute | solution.py:316
  2.1 15.8 %collective-permute-start.3 = (bf16[1024,256]{1,0:T(8,128)(2,1)}, bf16[1024,256]{1,0:T(8,128)(2,1)S(1)}, u32[]{:S(2)}, u32[]{:S(2)}) collective-permute-start(bf16[1024,256]{1,0:T(8,128)(2,1)} %bitcast.13), channel_id=1, source_target_pairs={{0,2},{4,6},{8,10},{12,14},{1,3},{5,7},{9,11},{13,15},{16,18},{20,... | collective-permute-start | bytes 1572872 | tf_op jit(solution)/shard_map/ppermute | solution.py:318
  5.6 12.3 %collective-permute-start.4 = (bf16[1024,256]{1,0:T(8,128)(2,1)}, bf16[1024,256]{1,0:T(8,128)(2,1)S(1)}, u32[]{:S(2)}, u32[]{:S(2)}) collective-permute-start(bf16[1024,256]{1,0:T(8,128)(2,1)} %bitcast.14), channel_id=1, source_target_pairs={{2,4},{6,8},{10,12},{3,5},{7,9},{11,13},{18,20},{22,24},{26,28},{1... | collective-permute-start | bytes 1572872 | tf_op jit(solution)/shard_map/ppermute | solution.py:319
  6.3 6.4 %copy-start = (bf16[1,1024,256]{2,1,0:T(8,128)(2,1)S(1)}, bf16[1,1024,256]{2,1,0:T(8,128)(2,1)}, u32[]{:S(2)}) copy-start(bf16[1,1024,256]{2,1,0:T(8,128)(2,1)} %param.11) | copy-start | bytes 1572868
  11.9 5.9 %collective-permute-start.2 = (bf16[1024,256]{1,0:T(8,128)(2,1)S(1)}, bf16[1024,256]{1,0:T(8,128)(2,1)S(1)}, u32[]{:S(2)}, u32[]{:S(2)}) collective-permute-start(bf16[1024,256]{1,0:T(8,128)(2,1)S(1)} %collective-permute-done.1), channel_id=1, source_target_pairs={{31,17},{1,15},{47,33},{17,31},{63,49},{33,47},{159,145},{129,143}... | collective-permute-start | bytes 1572872 | tf_op jit(solution)/shard_map/ppermute | solution.py:342
  12.6 7.3 %collective-permute-start.6 = (bf16[1024,256]{1,0:T(8,128)(2,1)S(1)}, bf16[1024,256]{1,0:T(8,128)(2,1)S(1)}, u32[]{:S(2)}, u32[]{:S(2)}) collective-permute-start(bf16[1024,256]{1,0:T(8,128)(2,1)S(1)} %bitcast.16), channel_id=1, source_target_pairs={{0,1},{1,0},{2,3},{3,2},{4,5},{5,4},{6,7},{7,6},{8,9},{9,8},{10,11... | collective-permute-start | bytes 1572872 | tf_op jit(solution)/shard_map/ppermute | solution.py:320
  18.0 4.0 %collective-permute-start.5 = (bf16[1024,256]{1,0:T(8,128)(2,1)S(1)}, bf16[1024,256]{1,0:T(8,128)(2,1)S(1)}, u32[]{:S(2)}, u32[]{:S(2)}) collective-permute-start(bf16[1024,256]{1,0:T(8,128)(2,1)S(1)} %get-tuple-element.33), channel_id=1, source_target_pairs={{0,1},{1,0},{2,3},{3,2},{4,5},{5,4},{6,7},{7,6},{8,9},{9,8},{10,11... | collective-permute-start | bytes 1572872 | tf_op jit(solution)/shard_map/ppermute | solution.py:346

commit v9 on v8

--- a/solution.py
+++ b/solution.py
@@ -18,6 +18,7 @@
 CTX = ("zh", "y", "core")
 SA, TA, SY, TY = 0, 1, 2, 6
 SUMS = 10
+SENT = 48
 ROWS = 16
 F00, F01, W0, W8, C0, CD = 0, 1, 2, 3, 4, 7
 COEFS = 10
@@ -195,9 +196,10 @@
         pl.when(core == b)(lambda work=work: run(work, saved, coef_ref, acc_ref, start, keep, unroll=8))
 
 
-def last_kernel(ids_ref, relay_ref, saved, par_ref, coef_ref, far_ref, part_ref, sums_ref, grad_hbm, acc_ref, grad_ref, sems):
+def last_kernel(ids_ref, relay_ref, saved, par_ref, coef_ref, far_ref, part_ref, sums_ref, grad_hbm, acc_ref, sum_ref, grad_ref, sems):
     core = ids_ref[0] % 2
     acc_ref[...] = far_ref[...]
+    sum_ref[...] = jnp.zeros_like(sum_ref)
 
     def start(n, r, cols):
         return part_ref[rows_of(0, n, r), cols].reshape(2, STEP // 2, LANES)
@@ -231,18 +233,29 @@
         for j, value in enumerate(sums):
             for h in range(2):
                 at = 2 * (b * 9 + j) + h
-                sums_ref[0, pl.ds(at, 1), :] = value[b : b + 1, h * LANES : (h + 1) * LANES]
-    for copy in range(1, sums_ref.shape[0]):
-        sums_ref[copy] = sums_ref[0]
+                sum_ref[pl.ds(at, 1), :] = value[b : b + 1, h * LANES : (h + 1) * LANES]
+    sent = sum_ref[...].astype(sums_ref.dtype)
+    for copy in range(sums_ref.shape[0]):
+        sums_ref[copy] = sent
     for copy in copies:
         copy.wait()
 
 
+def total_of(got_ref):
+    total = got_ref[0].astype(F32)
+    for i in range(1, got_ref.shape[0]):
+        total = total + got_ref[i].astype(F32)
+    return total
+
+
+def fold_kernel(got_ref, sums_ref):
+    total = total_of(got_ref).astype(sums_ref.dtype)
+    for copy in range(sums_ref.shape[0]):
+        sums_ref[copy] = total
+
+
 def finish_kernel(factor, got_ref, filters_ref, mixing_ref):
-    total = got_ref[0]
-    for i in range(1, got_ref.shape[0]):
-        total = total + got_ref[i]
-    total = total * factor
+    total = total_of(got_ref) * factor
     for b in range(2):
         for j in range(9):
             for h in range(2):
@@ -355,11 +368,12 @@
     sums, grad = call(
         last_kernel,
         "last",
-        (jax.ShapeDtypeStruct((8, 18 * width // LANES, LANES), F32), jax.ShapeDtypeStruct((rows, width), jnp.bfloat16)),
+        (jax.ShapeDtypeStruct((8, SENT, LANES), dy.dtype), jax.ShapeDtypeStruct((rows, width), jnp.bfloat16)),
         (ids, relay, saved, par, coef, acc_far, part_far),
         "svvvvvv",
         scratch=[
             pltpu.VMEM((2, ROWS, width), F32),
+            pltpu.VMEM((SENT, LANES), F32),
             pltpu.VMEM((rows, width), dy.dtype),
             pltpu.SemaphoreType.DMA((2,)),
         ],
@@ -370,7 +384,7 @@
     for i, axes in enumerate(groups):
         got = lax.all_to_all(sums, axes, 0, 0)
         if i + 1 < len(groups):
-            sums = jnp.broadcast_to(jnp.sum(got, axis=0)[None], sums.shape)
+            (sums,) = call(fold_kernel, "fold", (jax.ShapeDtypeStruct(sums.shape, sums.dtype),), (got,), "v")
     count = level_input.shape[0] * lax.axis_size(DP) * rows * ctx
     grad_filters, grad_mixing = call(
         lambda *refs: finish_kernel(1.0 / math.sqrt(count), *refs),

time: 75.6 us -> 73.6 us (0.974)
  blocking collectives: 50.4 us -> 48.3 us
    all_to_all x3, blocking collectives: 50.4 us -> 48.3 us  [body(): got = lax.all_to_all(sums, axes, 0, 0)]
    pallas_call x5 -> x7, Pallas kernels: 10.6 us -> 10.7 us  [call(): pl.pallas_call(kernel, out_shape=outs, in_specs=[pl.BlockSpec(memory_spac...]
  transfers between devices with their start and end apart: 7 -> 7, of which waited for: 1 -> 1; matrix products, arithmetic and copies ran while one was open for 0% -> 0% of each run, Pallas kernels for 10% -> 11%
where the time goes in v9:
time: 73.6 us; the launch traced here: 73.2 us
  blocking collectives  48.3 us (66%)
  Pallas kernels  10.7 us (15%)
  starting transfers between devices  10.1 us (14%)
  waiting for transfers between devices  3.28 us (4%)
  between operations  0.8 us (1%)
    all_to_all x3, blocking collectives, body(): got = lax.all_to_all(sums, axes, 0, 0)  48.3 us
    pallas_call x7, Pallas kernels, call(): pl.pallas_call(kernel, out_shape=outs, in_specs=[pl.BlockSpec(memory_spac...  10.7 us
    ppermute x1, starting transfers between devices, body(): evens = lax.ppermute(dy, CTX, even)  3.48 us
    ppermute x1, waiting for transfers between devices, body(): evens = lax.ppermute(dy, CTX, even)  3.27 us
    ppermute x1, starting transfers between devices, body(): relay = lax.ppermute(send, 'core', pair)  1.92 us
    ppermute x1, starting transfers between devices, body(): swap = lax.ppermute(dy, 'core', pair)  1.92 us
  transfers between devices with their start and end apart: 7, of which 1 were waited for; matrix products, arithmetic and copies ran while one was open for 0% of the time, Pallas kernels for 11%

profile of v9, /device:TPU:64, one launch (start us, length us, event | category | flops | bytes accessed | tf_op | source)
XLA Modules:
  0.0 73.2 jit_solution(12623337978671985917)
XLA Ops:
  0.7 0.7 collective-permute-start.1
  1.4 0.7 collective-permute-start
  2.1 3.5 %collective-permute-start.3 = (bf16[1024,256]{1,0:T(8,128)(2,1)}, bf16[1024,256]{1,0:T(8,128)(2,1)S(1)}, u32[]{:S(2)}, u32[]{:S(2)}) collective-permute-start(bf16[1024,256]{1,0:T(8,128)(2,1)} %bitcast.13), channel_id=1, source_target_pairs={{0,2},{4,6},{8,10},{12,14},{1,3},{5,7},{9,11},{13,15},{16,18},{20,... | collective-permute-start | bytes 1572872 | tf_op jit(solution)/shard_map/ppermute | solution.py:331
  5.6 0.7 collective-permute-start.4
  6.3 0.0 copy-start
  6.3 5.6 %near.1 = (f32[2,16,256]{2,1,0:T(8,128)S(1)}, f32[1024,256]{1,0:T(8,128)S(1)}, f32[2,10,8,256]{3,2,1,0:T(8,128)S(1)}, f32[9,2,256]{2,1,0:T(2,128)S(1)}, bf16[7,1024,256]{2,1,0:T(8,128)(2,1)S(1)}) custom-call(bf16[1024,256]{1,0:T(8,128)(2,1)} %bitcast.15, bf16[1024,256]{1,0:T(8,128)(2,1)} %bitcast.10, bf16[3,1024,256]{2,1,0:T(8,128)(2,1)} %bitcast.8, ...), custom_call_target="tpu_custom_call" | custom-call | flops 20000000 | bytes 6000000 | tf_op jit(solution)/shard_map/near/pallas_call | solution.py:273
  11.9 0.0 collective-permute-done.1
  11.9 0.7 collective-permute-start.2
  12.6 0.0 copy-done
  12.6 1.9 %collective-permute-start.6 = (bf16[1024,256]{1,0:T(8,128)(2,1)S(1)}, bf16[1024,256]{1,0:T(8,128)(2,1)S(1)}, u32[]{:S(2)}, u32[]{:S(2)}) collective-permute-start(bf16[1024,256]{1,0:T(8,128)(2,1)S(1)} %bitcast.16), channel_id=1, source_target_pairs={{0,1},{1,0},{2,3},{3,2},{4,5},{5,4},{6,7},{7,6},{8,9},{9,8},{10,11... | collective-permute-start | bytes 1572872 | tf_op jit(solution)/shard_map/ppermute | solution.py:333
  14.6 0.0 collective-permute-done.cross_ref
  14.6 3.3 %collective-permute-done.3.even_ref = bf16[1024,256]{1,0:T(8,128)(2,1)S(1)} collective-permute-done((bf16[1024,256]{1,0:T(8,128)(2,1)}, bf16[1024,256]{1,0:T(8,128)(2,1)S(1)}, u32[]{:S(2)}, u32[]{:S(2)}) %collective-permute-start.3) | collective-permute-done | bytes 524320 | tf_op jit(solution)/shard_map/ppermute | solution.py:331
  17.8 0.0 collective-permute-done.4.odd_ref
  17.8 0.0 collective-permute-done.2.turn_ref
  17.8 0.2 pick.1
  18.0 1.9 %collective-permute-start.5 = (bf16[1024,256]{1,0:T(8,128)(2,1)S(1)}, bf16[1024,256]{1,0:T(8,128)(2,1)S(1)}, u32[]{:S(2)}, u32[]{:S(2)}) collective-permute-start(bf16[1024,256]{1,0:T(8,128)(2,1)S(1)} %get-tuple-element.33), channel_id=1, source_target_pairs={{0,1},{1,0},{2,3},{3,2},{4,5},{5,4},{6,7},{7,6},{8,9},{9,8},{10,11... | collective-permute-start | bytes 1572872 | tf_op jit(solution)/shard_map/ppermute | solution.py:359
  20.0 0.0 collective-permute-done.6.swap_ref
  20.0 2.1 %far.1 = (f32[2,16,256]{2,1,0:T(8,128)S(1)}, f32[1024,256]{1,0:T(8,128)S(1)}) custom-call(s32[1]{0:T(128)} %bitcast.ids_ref, bf16[1024,256]{1,0:T(8,128)(2,1)S(1)} %collective-permute-done.6.swap_ref, bf16[1024,256]{1,0:T(8,128)(2,1)S(1)} %get-tuple-element.37.right_ref, bf16[1024,256]{1,0:T(8,128)(2,1)S(1)} %get-tuple-element.38.left_ref, ...), custom_call_target="tpu_custom_call" | custom-call | flops 20000000 | bytes 6000000 | tf_op jit(solution)/shard_map/far/pallas_call | solution.py:273
  22.0 0.0 collective-permute-done.5.relay_ref
  22.0 2.2 %last.1 = (bf16[8,48,128]{2,1,0:T(8,128)(2,1)S(1)}, bf16[1024,256]{1,0:T(8,128)(2,1)}) custom-call(s32[1]{0:T(128)} %bitcast.ids_ref, bf16[1024,256]{1,0:T(8,128)(2,1)S(1)} %collective-permute-done.5.relay_ref, bf16[7,1024,256]{2,1,0:T(8,128)(2,1)S(1)} %get-tuple-element.34.saved, f32[9,2,256]{2,1,0:T(2,128)S(1)} %get-tuple-element.35.par_ref, ...), custom_call_target="tpu_custom_call" | custom-call | flops 20000000 | bytes 6000000 | tf_op jit(solution)/shard_map/last/pallas_call | solution.py:273
  24.2 10.1 %all_to_all.15.got_ref = bf16[8,48,128]{2,1,0:T(8,128)(2,1)S(1)} all-to-all(bf16[8,48,128]{2,1,0:T(8,128)(2,1)S(1)} %get-tuple-element.44), channel_id=1, replica_groups=mesh['x'=4,'zl'=2,'zh'=4,'y'=8,'core'=2] {'x','core'}, dimensions={0} | all-to-all | bytes 196608 | tf_op jit(solution)/shard_map/all_to_all | solution.py:385
  34.3 22.9 %all_to_all.16.got_ref = bf16[8,48,128]{2,1,0:T(8,128)(2,1)S(1)} all-to-all(bf16[8,48,128]{2,1,0:T(8,128)(2,1)S(1)} %fold.2), channel_id=1, replica_groups=mesh['x'=4,'zl'=2,'zh'=4,'y'=8,'core'=2] {'y'}, dimensions={0} | all-to-all | bytes 196608 | tf_op jit(solution)/shard_map/all_to_all | solution.py:385
  57.3 15.3 %all_to_all.17.refs_0_ = bf16[8,48,128]{2,1,0:T(8,128)(2,1)S(1)} all-to-all(bf16[8,48,128]{2,1,0:T(8,128)(2,1)S(1)} %fold.3), channel_id=1, replica_groups=mesh['x'=4,'zl'=2,'zh'=4,'y'=8,'core'=2] {'zl','zh'}, dimensions={0} | all-to-all | bytes 196608 | tf_op jit(solution)/shard_map/all_to_all | solution.py:385
  72.6 0.6 finish.1
  (2 shorter events, 0.0 us)
Async XLA Ops:
  0.7 11.2 %collective-permute-start.1 = (bf16[1024,256]{1,0:T(8,128)(2,1)}, bf16[1024,256]{1,0:T(8,128)(2,1)S(1)}, u32[]{:S(2)}, u32[]{:S(2)}) collective-permute-start(bf16[1024,256]{1,0:T(8,128)(2,1)} %bitcast.11), channel_id=1, source_target_pairs={{15,31},{17,1},{31,47},{33,17},{47,63},{49,33},{143,159},{145,129}... | collective-permute-start | bytes 1572872 | tf_op jit(solution)/shard_map/ppermute | solution.py:330
  1.4 13.2 %collective-permute-start = (bf16[1024,256]{1,0:T(8,128)(2,1)}, bf16[1024,256]{1,0:T(8,128)(2,1)S(1)}, u32[]{:S(2)}, u32[]{:S(2)}) collective-permute-start(bf16[1024,256]{1,0:T(8,128)(2,1)} %bitcast.12), channel_id=1, source_target_pairs={{14,16},{16,14},{30,32},{32,30},{46,48},{48,46},{78,80},{80,78},{7... | collective-permute-start | bytes 1572872 | tf_op jit(solution)/shard_map/ppermute | solution.py:329
  2.1 15.8 %collective-permute-start.3 = (bf16[1024,256]{1,0:T(8,128)(2,1)}, bf16[1024,256]{1,0:T(8,128)(2,1)S(1)}, u32[]{:S(2)}, u32[]{:S(2)}) collective-permute-start(bf16[1024,256]{1,0:T(8,128)(2,1)} %bitcast.13), channel_id=1, source_target_pairs={{0,2},{4,6},{8,10},{12,14},{1,3},{5,7},{9,11},{13,15},{16,18},{20,... | collective-permute-start | bytes 1572872 | tf_op jit(solution)/shard_map/ppermute | solution.py:331
  5.6 12.3 %collective-permute-start.4 = (bf16[1024,256]{1,0:T(8,128)(2,1)}, bf16[1024,256]{1,0:T(8,128)(2,1)S(1)}, u32[]{:S(2)}, u32[]{:S(2)}) collective-permute-start(bf16[1024,256]{1,0:T(8,128)(2,1)} %bitcast.14), channel_id=1, source_target_pairs={{2,4},{6,8},{10,12},{3,5},{7,9},{11,13},{18,20},{22,24},{26,28},{1... | collective-permute-start | bytes 1572872 | tf_op jit(solution)/shard_map/ppermute | solution.py:332
  6.3 6.4 %copy-start = (bf16[1,1024,256]{2,1,0:T(8,128)(2,1)S(1)}, bf16[1,1024,256]{2,1,0:T(8,128)(2,1)}, u32[]{:S(2)}) copy-start(bf16[1,1024,256]{2,1,0:T(8,128)(2,1)} %param.11) | copy-start | bytes 1572868
  11.9 5.9 %collective-permute-start.2 = (bf16[1024,256]{1,0:T(8,128)(2,1)S(1)}, bf16[1024,256]{1,0:T(8,128)(2,1)S(1)}, u32[]{:S(2)}, u32[]{:S(2)}) collective-permute-start(bf16[1024,256]{1,0:T(8,128)(2,1)S(1)} %collective-permute-done.1), channel_id=1, source_target_pairs={{31,17},{1,15},{47,33},{17,31},{63,49},{33,47},{159,145},{129,143}... | collective-permute-start | bytes 1572872 | tf_op jit(solution)/shard_map/ppermute | solution.py:355
  12.6 7.3 %collective-permute-start.6 = (bf16[1024,256]{1,0:T(8,128)(2,1)S(1)}, bf16[1024,256]{1,0:T(8,128)(2,1)S(1)}, u32[]{:S(2)}, u32[]{:S(2)}) collective-permute-start(bf16[1024,256]{1,0:T(8,128)(2,1)S(1)} %bitcast.16), channel_id=1, source_target_pairs={{0,1},{1,0},{2,3},{3,2},{4,5},{5,4},{6,7},{7,6},{8,9},{9,8},{10,11... | collective-permute-start | bytes 1572872 | tf_op jit(solution)/shard_map/ppermute | solution.py:333
  18.0 4.0 %collective-permute-start.5 = (bf16[1024,256]{1,0:T(8,128)(2,1)S(1)}, bf16[1024,256]{1,0:T(8,128)(2,1)S(1)}, u32[]{:S(2)}, u32[]{:S(2)}) collective-permute-start(bf16[1024,256]{1,0:T(8,128)(2,1)S(1)} %get-tuple-element.33), channel_id=1, source_target_pairs={{0,1},{1,0},{2,3},{3,2},{4,5},{5,4},{6,7},{7,6},{8,9},{9,8},{10,11... | collective-permute-start | bytes 1572872 | tf_op jit(solution)/shard_map/ppermute | solution.py:359

commit v10 on v9

--- a/solution.py
+++ b/solution.py
@@ -77,8 +77,8 @@
     return sums, g
 
 
-def run(work, saved, coef_ref, acc_ref, start, finish, halves=(0, 1), unroll=1):
-    for h in halves:
+def run(work, saved, coef_ref, acc_ref, start, finish, unroll=1):
+    for h in range(2):
         cols = pl.ds(h * LANES, LANES)
 
         def step(r, accs):
@@ -196,7 +196,7 @@
         pl.when(core == b)(lambda work=work: run(work, saved, coef_ref, acc_ref, start, keep, unroll=8))
 
 
-def last_kernel(ids_ref, relay_ref, saved, par_ref, coef_ref, far_ref, part_ref, sums_ref, grad_hbm, acc_ref, sum_ref, grad_ref, sems):
+def last_kernel(ids_ref, relay_ref, saved, par_ref, coef_ref, far_ref, part_ref, sums_ref, grad_ref, acc_ref, sum_ref):
     core = ids_ref[0] % 2
     acc_ref[...] = far_ref[...]
     sum_ref[...] = jnp.zeros_like(sum_ref)
@@ -207,16 +207,11 @@
     def keep(n, r, cols, value):
         grad_ref[rows_of(0, n, r), cols] = value.astype(grad_ref.dtype)
 
-    copies = []
-    for h in range(2):
-        for b in range(2):
-            work = [(b, [(relay_ref, NB)])]
-            pl.when(core == 1 - b)(
-                lambda work=work, h=h: run(work, saved, coef_ref, acc_ref, start, keep, (h,), 8)
-            )
-        cols = pl.ds(h * LANES, LANES)
-        copies.append(pltpu.make_async_copy(grad_ref.at[:, cols], grad_hbm.at[:, cols], sems.at[h]))
-        copies[h].start()
+    for b in range(2):
+        work = [(b, [(relay_ref, NB)])]
+        pl.when(core == 1 - b)(
+            lambda work=work: run(work, saved, coef_ref, acc_ref, start, keep, unroll=8)
+        )
     f = [[par_ref[2 * i + j] for j in range(2)] for i in range(2)]
     mix = [par_ref[4 + i] for i in range(LEVELS + 1)]
     acc = [acc_ref[:, i, :] for i in range(SUMS)]
@@ -237,8 +232,6 @@
     sent = sum_ref[...].astype(sums_ref.dtype)
     for copy in range(sums_ref.shape[0]):
         sums_ref[copy] = sent
-    for copy in copies:
-        copy.wait()
 
 
 def total_of(got_ref):
@@ -254,7 +247,10 @@
         sums_ref[copy] = total
 
 
-def finish_kernel(factor, got_ref, filters_ref, mixing_ref):
+def finish_kernel(factor, got_ref, grad_ref, filters_hbm, mixing_hbm, grad_hbm, filters_ref, mixing_ref, sems):
+    moves = ((grad_ref, grad_hbm), (filters_ref, filters_hbm), (mixing_ref, mixing_hbm))
+    copies = [pltpu.make_async_copy(a, b, sems.at[i]) for i, (a, b) in enumerate(moves)]
+    copies[0].start()
     total = total_of(got_ref) * factor
     for b in range(2):
         for j in range(9):
@@ -265,6 +261,10 @@
                     filters_ref[b, j // 2, pl.ds(j % 2, 1), cols] = row
                 else:
                     mixing_ref[j - 4, pl.ds(b, 1), cols] = row
+    for copy in copies[1:]:
+        copy.start()
+    for copy in copies:
+        copy.wait()
 
 
 def call(kernel, name, outs, args, spaces, scratch=(), flops=0, spaces_out=None):
@@ -368,16 +368,13 @@
     sums, grad = call(
         last_kernel,
         "last",
-        (jax.ShapeDtypeStruct((8, SENT, LANES), dy.dtype), jax.ShapeDtypeStruct((rows, width), jnp.bfloat16)),
+        (jax.ShapeDtypeStruct((8, SENT, LANES), dy.dtype), pltpu.VMEM((rows, width), jnp.bfloat16)),
         (ids, relay, saved, par, coef, acc_far, part_far),
         "svvvvvv",
         scratch=[
             pltpu.VMEM((2, ROWS, width), F32),
             pltpu.VMEM((SENT, LANES), F32),
-            pltpu.VMEM((rows, width), dy.dtype),
-            pltpu.SemaphoreType.DMA((2,)),
         ],
-        spaces_out="va",
         flops=20_000_000,
     )
     groups = (("x", "core"), ("y",), ("zl", "zh"))
@@ -386,12 +383,18 @@
         if i + 1 < len(groups):
             (sums,) = call(fold_kernel, "fold", (jax.ShapeDtypeStruct(sums.shape, sums.dtype),), (got,), "v")
     count = level_input.shape[0] * lax.axis_size(DP) * rows * ctx
-    grad_filters, grad_mixing = call(
+    grad_filters, grad_mixing, grad = call(
         lambda *refs: finish_kernel(1.0 / math.sqrt(count), *refs),
         "finish",
-        (jax.ShapeDtypeStruct(filters.shape, F32), jax.ShapeDtypeStruct(mixing.shape, F32)),
-        (got,),
-        "v",
+        (jax.ShapeDtypeStruct(filters.shape, F32), jax.ShapeDtypeStruct(mixing.shape, F32), jax.ShapeDtypeStruct(grad.shape, grad.dtype)),
+        (got, grad),
+        "vv",
+        scratch=[
+            pltpu.VMEM(filters.shape, F32),
+            pltpu.VMEM(mixing.shape, F32),
+            pltpu.SemaphoreType.DMA((3,)),
+        ],
+        spaces_out="aaa",
     )
     return grad[None], grad_filters, jnp.swapaxes(grad_mixing, 0, 1)
 

time: 73.6 us -> 73.1 us (level)
  no operation moved by 1% of the time
where the time goes in v10:
time: 73.1 us; the launch traced here: 72.7 us
  blocking collectives  48.3 us (66%)
  Pallas kernels  10.2 us (14%)
  starting transfers between devices  10.1 us (14%)
  waiting for transfers between devices  3.28 us (4%)
  between operations  0.79 us (1%)
    all_to_all x3, blocking collectives, body(): got = lax.all_to_all(sums, axes, 0, 0)  48.3 us
    pallas_call x7, Pallas kernels, call(): pl.pallas_call(kernel, out_shape=outs, in_specs=[pl.BlockSpec(memory_spac...  10.2 us
    ppermute x1, starting transfers between devices, body(): evens = lax.ppermute(dy, CTX, even)  3.48 us
    ppermute x1, waiting for transfers between devices, body(): evens = lax.ppermute(dy, CTX, even)  3.27 us
    ppermute x1, starting transfers between devices, body(): swap = lax.ppermute(dy, 'core', pair)  1.92 us
    ppermute x1, starting transfers between devices, body(): relay = lax.ppermute(send, 'core', pair)  1.92 us
  transfers between devices with their start and end apart: 7, of which 1 were waited for; matrix products, arithmetic and copies ran while one was open for 0% of the time, Pallas kernels for 11%

profile of v10, /device:TPU:64, one launch (start us, length us, event | category | flops | bytes accessed | tf_op | source)
XLA Modules:
  0.0 72.7 jit_solution(9334300540567849690)
XLA Ops:
  0.7 0.7 collective-permute-start.1
  1.4 0.7 collective-permute-start
  2.1 3.5 %collective-permute-start.3 = (bf16[1024,256]{1,0:T(8,128)(2,1)}, bf16[1024,256]{1,0:T(8,128)(2,1)S(1)}, u32[]{:S(2)}, u32[]{:S(2)}) collective-permute-start(bf16[1024,256]{1,0:T(8,128)(2,1)} %bitcast.13), channel_id=1, source_target_pairs={{0,2},{4,6},{8,10},{12,14},{1,3},{5,7},{9,11},{13,15},{16,18},{20,... | collective-permute-start | bytes 1572872 | tf_op jit(solution)/shard_map/ppermute | solution.py:331
  5.6 0.7 collective-permute-start.4
  6.3 0.0 copy-start
  6.3 5.6 %near.1 = (f32[2,16,256]{2,1,0:T(8,128)S(1)}, f32[1024,256]{1,0:T(8,128)S(1)}, f32[2,10,8,256]{3,2,1,0:T(8,128)S(1)}, f32[9,2,256]{2,1,0:T(2,128)S(1)}, bf16[7,1024,256]{2,1,0:T(8,128)(2,1)S(1)}) custom-call(bf16[1024,256]{1,0:T(8,128)(2,1)} %bitcast.15, bf16[1024,256]{1,0:T(8,128)(2,1)} %bitcast.10, bf16[3,1024,256]{2,1,0:T(8,128)(2,1)} %bitcast.8, ...), custom_call_target="tpu_custom_call" | custom-call | flops 20000000 | bytes 6000000 | tf_op jit(solution)/shard_map/near/pallas_call | solution.py:273
  11.9 0.0 collective-permute-done.1
  11.9 0.7 collective-permute-start.2
  12.6 0.0 copy-done
  12.6 1.9 %collective-permute-start.6 = (bf16[1024,256]{1,0:T(8,128)(2,1)S(1)}, bf16[1024,256]{1,0:T(8,128)(2,1)S(1)}, u32[]{:S(2)}, u32[]{:S(2)}) collective-permute-start(bf16[1024,256]{1,0:T(8,128)(2,1)S(1)} %bitcast.16), channel_id=1, source_target_pairs={{0,1},{1,0},{2,3},{3,2},{4,5},{5,4},{6,7},{7,6},{8,9},{9,8},{10,11... | collective-permute-start | bytes 1572872 | tf_op jit(solution)/shard_map/ppermute | solution.py:333
  14.6 0.0 collective-permute-done.cross_ref
  14.6 3.3 %collective-permute-done.3.even_ref = bf16[1024,256]{1,0:T(8,128)(2,1)S(1)} collective-permute-done((bf16[1024,256]{1,0:T(8,128)(2,1)}, bf16[1024,256]{1,0:T(8,128)(2,1)S(1)}, u32[]{:S(2)}, u32[]{:S(2)}) %collective-permute-start.3) | collective-permute-done | bytes 524320 | tf_op jit(solution)/shard_map/ppermute | solution.py:331
  17.8 0.0 collective-permute-done.4.odd_ref
  17.8 0.0 collective-permute-done.2.turn_ref
  17.8 0.2 pick.1
  18.0 1.9 %collective-permute-start.5 = (bf16[1024,256]{1,0:T(8,128)(2,1)S(1)}, bf16[1024,256]{1,0:T(8,128)(2,1)S(1)}, u32[]{:S(2)}, u32[]{:S(2)}) collective-permute-start(bf16[1024,256]{1,0:T(8,128)(2,1)S(1)} %get-tuple-element.34), channel_id=1, source_target_pairs={{0,1},{1,0},{2,3},{3,2},{4,5},{5,4},{6,7},{7,6},{8,9},{9,8},{10,11... | collective-permute-start | bytes 1572872 | tf_op jit(solution)/shard_map/ppermute | solution.py:359
  20.0 0.0 collective-permute-done.6.swap_ref
  20.0 2.1 %far.1 = (f32[2,16,256]{2,1,0:T(8,128)S(1)}, f32[1024,256]{1,0:T(8,128)S(1)}) custom-call(s32[1]{0:T(128)} %bitcast.ids_ref, bf16[1024,256]{1,0:T(8,128)(2,1)S(1)} %collective-permute-done.6.swap_ref, bf16[1024,256]{1,0:T(8,128)(2,1)S(1)} %get-tuple-element.38.right_ref, bf16[1024,256]{1,0:T(8,128)(2,1)S(1)} %get-tuple-element.39.left_ref, ...), custom_call_target="tpu_custom_call" | custom-call | flops 20000000 | bytes 6000000 | tf_op jit(solution)/shard_map/far/pallas_call | solution.py:273
  22.0 0.0 collective-permute-done.5.relay_ref
  22.0 1.5 %last.1 = (bf16[8,48,128]{2,1,0:T(8,128)(2,1)S(1)}, bf16[1024,256]{1,0:T(8,128)(2,1)S(1)}) custom-call(s32[1]{0:T(128)} %bitcast.ids_ref, bf16[1024,256]{1,0:T(8,128)(2,1)S(1)} %collective-permute-done.5.relay_ref, bf16[7,1024,256]{2,1,0:T(8,128)(2,1)S(1)} %get-tuple-element.35.saved, f32[9,2,256]{2,1,0:T(2,128)S(1)} %get-tuple-element.36.par_ref, ...), custom_call_target="tpu_custom_call" | custom-call | flops 20000000 | bytes 6000000 | tf_op jit(solution)/shard_map/last/pallas_call | solution.py:273
  23.5 10.1 %all_to_all.15.got_ref = bf16[8,48,128]{2,1,0:T(8,128)(2,1)S(1)} all-to-all(bf16[8,48,128]{2,1,0:T(8,128)(2,1)S(1)} %get-tuple-element.44), channel_id=1, replica_groups=mesh['x'=4,'zl'=2,'zh'=4,'y'=8,'core'=2] {'x','core'}, dimensions={0} | all-to-all | bytes 196608 | tf_op jit(solution)/shard_map/all_to_all | solution.py:382
  33.6 22.9 %all_to_all.16.got_ref = bf16[8,48,128]{2,1,0:T(8,128)(2,1)S(1)} all-to-all(bf16[8,48,128]{2,1,0:T(8,128)(2,1)S(1)} %fold.2), channel_id=1, replica_groups=mesh['x'=4,'zl'=2,'zh'=4,'y'=8,'core'=2] {'y'}, dimensions={0} | all-to-all | bytes 196608 | tf_op jit(solution)/shard_map/all_to_all | solution.py:382
  56.6 15.3 %all_to_all.17.refs_0_ = bf16[8,48,128]{2,1,0:T(8,128)(2,1)S(1)} all-to-all(bf16[8,48,128]{2,1,0:T(8,128)(2,1)S(1)} %fold.3), channel_id=1, replica_groups=mesh['x'=4,'zl'=2,'zh'=4,'y'=8,'core'=2] {'zl','zh'}, dimensions={0} | all-to-all | bytes 196608 | tf_op jit(solution)/shard_map/all_to_all | solution.py:382
  71.9 0.8 %finish.1 = (f32[2,2,2,256]{3,2,1,0:T(2,128)}, f32[5,2,256]{2,1,0:T(2,128)}, bf16[1024,256]{1,0:T(8,128)(2,1)}) custom-call(bf16[8,48,128]{2,1,0:T(8,128)(2,1)S(1)} %all_to_all.17.refs_0_, bf16[1024,256]{1,0:T(8,128)(2,1)S(1)} %get-tuple-element.45.refs_1_), custom_call_target="tpu_custom_call" | custom-call | bytes 6000000 | tf_op jit(solution)/shard_map/finish/pallas_call | solution.py:273
  (2 shorter events, 0.0 us)
Async XLA Ops:
  0.7 11.2 %collective-permute-start.1 = (bf16[1024,256]{1,0:T(8,128)(2,1)}, bf16[1024,256]{1,0:T(8,128)(2,1)S(1)}, u32[]{:S(2)}, u32[]{:S(2)}) collective-permute-start(bf16[1024,256]{1,0:T(8,128)(2,1)} %bitcast.11), channel_id=1, source_target_pairs={{15,31},{17,1},{31,47},{33,17},{47,63},{49,33},{143,159},{145,129}... | collective-permute-start | bytes 1572872 | tf_op jit(solution)/shard_map/ppermute | solution.py:330
  1.4 13.2 %collective-permute-start = (bf16[1024,256]{1,0:T(8,128)(2,1)}, bf16[1024,256]{1,0:T(8,128)(2,1)S(1)}, u32[]{:S(2)}, u32[]{:S(2)}) collective-permute-start(bf16[1024,256]{1,0:T(8,128)(2,1)} %bitcast.12), channel_id=1, source_target_pairs={{14,16},{16,14},{30,32},{32,30},{46,48},{48,46},{78,80},{80,78},{7... | collective-permute-start | bytes 1572872 | tf_op jit(solution)/shard_map/ppermute | solution.py:329
  2.1 15.8 %collective-permute-start.3 = (bf16[1024,256]{1,0:T(8,128)(2,1)}, bf16[1024,256]{1,0:T(8,128)(2,1)S(1)}, u32[]{:S(2)}, u32[]{:S(2)}) collective-permute-start(bf16[1024,256]{1,0:T(8,128)(2,1)} %bitcast.13), channel_id=1, source_target_pairs={{0,2},{4,6},{8,10},{12,14},{1,3},{5,7},{9,11},{13,15},{16,18},{20,... | collective-permute-start | bytes 1572872 | tf_op jit(solution)/shard_map/ppermute | solution.py:331
  5.6 12.3 %collective-permute-start.4 = (bf16[1024,256]{1,0:T(8,128)(2,1)}, bf16[1024,256]{1,0:T(8,128)(2,1)S(1)}, u32[]{:S(2)}, u32[]{:S(2)}) collective-permute-start(bf16[1024,256]{1,0:T(8,128)(2,1)} %bitcast.14), channel_id=1, source_target_pairs={{2,4},{6,8},{10,12},{3,5},{7,9},{11,13},{18,20},{22,24},{26,28},{1... | collective-permute-start | bytes 1572872 | tf_op jit(solution)/shard_map/ppermute | solution.py:332
  6.3 6.4 %copy-start = (bf16[1,1024,256]{2,1,0:T(8,128)(2,1)S(1)}, bf16[1,1024,256]{2,1,0:T(8,128)(2,1)}, u32[]{:S(2)}) copy-start(bf16[1,1024,256]{2,1,0:T(8,128)(2,1)} %param.11) | copy-start | bytes 1572868
  11.9 5.9 %collective-permute-start.2 = (bf16[1024,256]{1,0:T(8,128)(2,1)S(1)}, bf16[1024,256]{1,0:T(8,128)(2,1)S(1)}, u32[]{:S(2)}, u32[]{:S(2)}) collective-permute-start(bf16[1024,256]{1,0:T(8,128)(2,1)S(1)} %collective-permute-done.1), channel_id=1, source_target_pairs={{31,17},{1,15},{47,33},{17,31},{63,49},{33,47},{159,145},{129,143}... | collective-permute-start | bytes 1572872 | tf_op jit(solution)/shard_map/ppermute | solution.py:355
  12.6 7.3 %collective-permute-start.6 = (bf16[1024,256]{1,0:T(8,128)(2,1)S(1)}, bf16[1024,256]{1,0:T(8,128)(2,1)S(1)}, u32[]{:S(2)}, u32[]{:S(2)}) collective-permute-start(bf16[1024,256]{1,0:T(8,128)(2,1)S(1)} %bitcast.16), channel_id=1, source_target_pairs={{0,1},{1,0},{2,3},{3,2},{4,5},{5,4},{6,7},{7,6},{8,9},{9,8},{10,11... | collective-permute-start | bytes 1572872 | tf_op jit(solution)/shard_map/ppermute | solution.py:333
  18.0 4.0 %collective-permute-start.5 = (bf16[1024,256]{1,0:T(8,128)(2,1)S(1)}, bf16[1024,256]{1,0:T(8,128)(2,1)S(1)}, u32[]{:S(2)}, u32[]{:S(2)}) collective-permute-start(bf16[1024,256]{1,0:T(8,128)(2,1)S(1)} %get-tuple-element.34), channel_id=1, source_target_pairs={{0,1},{1,0},{2,3},{3,2},{4,5},{5,4},{6,7},{7,6},{8,9},{9,8},{10,11... | collective-permute-start | bytes 1572872 | tf_op jit(solution)/shard_map/ppermute | solution.py:359

commit v11 on v10

--- a/solution.py
+++ b/solution.py
@@ -18,7 +18,7 @@
 CTX = ("zh", "y", "core")
 SA, TA, SY, TY = 0, 1, 2, 6
 SUMS = 10
-SENT = 48
+SENT = 40
 ROWS = 16
 F00, F01, W0, W8, C0, CD = 0, 1, 2, 3, 4, 7
 COEFS = 10
@@ -368,7 +368,7 @@
     sums, grad = call(
         last_kernel,
         "last",
-        (jax.ShapeDtypeStruct((8, SENT, LANES), dy.dtype), pltpu.VMEM((rows, width), jnp.bfloat16)),
+        (jax.ShapeDtypeStruct((8, SENT, LANES), F32), pltpu.VMEM((rows, width), jnp.bfloat16)),
         (ids, relay, saved, par, coef, acc_far, part_far),
         "svvvvvv",
         scratch=[

time: 73.1 us -> 75.1 us (1.027)
  blocking collectives: 48.3 us -> 50.3 us
    all_to_all x3, blocking collectives: 48.3 us -> 50.3 us  [body(): got = lax.all_to_all(sums, axes, 0, 0)]
where the time goes in v11:
time: 75.1 us; the launch traced here: 74.7 us
  blocking collectives  50.3 us (67%)
  Pallas kernels  10.2 us (14%)
  starting transfers between devices  10.1 us (13%)
  waiting for transfers between devices  3.28 us (4%)
  between operations  0.79 us (1%)
    all_to_all x3, blocking collectives, body(): got = lax.all_to_all(sums, axes, 0, 0)  50.3 us
    pallas_call x7, Pallas kernels, call(): pl.pallas_call(kernel, out_shape=outs, in_specs=[pl.BlockSpec(memory_spac...  10.2 us
    ppermute x1, starting transfers between devices, body(): evens = lax.ppermute(dy, CTX, even)  3.48 us
    ppermute x1, waiting for transfers between devices, body(): evens = lax.ppermute(dy, CTX, even)  3.27 us
    ppermute x1, starting transfers between devices, body(): swap = lax.ppermute(dy, 'core', pair)  1.92 us
    ppermute x1, starting transfers between devices, body(): relay = lax.ppermute(send, 'core', pair)  1.92 us
  transfers between devices with their start and end apart: 7, of which 1 were waited for; matrix products, arithmetic and copies ran while one was open for 0% of the time, Pallas kernels for 11%

profile of v11, /device:TPU:64, one launch (start us, length us, event | category | flops | bytes accessed | tf_op | source)
XLA Modules:
  0.0 74.7 jit_solution(521045839340029383)
XLA Ops:
  0.7 0.7 collective-permute-start.1
  1.4 0.7 collective-permute-start
  2.1 3.5 %collective-permute-start.3 = (bf16[1024,256]{1,0:T(8,128)(2,1)}, bf16[1024,256]{1,0:T(8,128)(2,1)S(1)}, u32[]{:S(2)}, u32[]{:S(2)}) collective-permute-start(bf16[1024,256]{1,0:T(8,128)(2,1)} %bitcast.13), channel_id=1, source_target_pairs={{0,2},{4,6},{8,10},{12,14},{1,3},{5,7},{9,11},{13,15},{16,18},{20,... | collective-permute-start | bytes 1572872 | tf_op jit(solution)/shard_map/ppermute | solution.py:331
  5.6 0.7 collective-permute-start.4
  6.3 0.0 copy-start
  6.3 5.6 %near.1 = (f32[2,16,256]{2,1,0:T(8,128)S(1)}, f32[1024,256]{1,0:T(8,128)S(1)}, f32[2,10,8,256]{3,2,1,0:T(8,128)S(1)}, f32[9,2,256]{2,1,0:T(2,128)S(1)}, bf16[7,1024,256]{2,1,0:T(8,128)(2,1)S(1)}) custom-call(bf16[1024,256]{1,0:T(8,128)(2,1)} %bitcast.15, bf16[1024,256]{1,0:T(8,128)(2,1)} %bitcast.10, bf16[3,1024,256]{2,1,0:T(8,128)(2,1)} %bitcast.8, ...), custom_call_target="tpu_custom_call" | custom-call | flops 20000000 | bytes 6000000 | tf_op jit(solution)/shard_map/near/pallas_call | solution.py:273
  11.9 0.0 collective-permute-done.1
  11.9 0.7 collective-permute-start.2
  12.6 0.0 copy-done
  12.6 1.9 %collective-permute-start.6 = (bf16[1024,256]{1,0:T(8,128)(2,1)S(1)}, bf16[1024,256]{1,0:T(8,128)(2,1)S(1)}, u32[]{:S(2)}, u32[]{:S(2)}) collective-permute-start(bf16[1024,256]{1,0:T(8,128)(2,1)S(1)} %bitcast.16), channel_id=1, source_target_pairs={{0,1},{1,0},{2,3},{3,2},{4,5},{5,4},{6,7},{7,6},{8,9},{9,8},{10,11... | collective-permute-start | bytes 1572872 | tf_op jit(solution)/shard_map/ppermute | solution.py:333
  14.6 0.0 collective-permute-done.cross_ref
  14.6 3.3 %collective-permute-done.3.even_ref = bf16[1024,256]{1,0:T(8,128)(2,1)S(1)} collective-permute-done((bf16[1024,256]{1,0:T(8,128)(2,1)}, bf16[1024,256]{1,0:T(8,128)(2,1)S(1)}, u32[]{:S(2)}, u32[]{:S(2)}) %collective-permute-start.3) | collective-permute-done | bytes 524320 | tf_op jit(solution)/shard_map/ppermute | solution.py:331
  17.8 0.0 collective-permute-done.4.odd_ref
  17.8 0.0 collective-permute-done.2.turn_ref
  17.8 0.2 pick.1
  18.0 1.9 %collective-permute-start.5 = (bf16[1024,256]{1,0:T(8,128)(2,1)S(1)}, bf16[1024,256]{1,0:T(8,128)(2,1)S(1)}, u32[]{:S(2)}, u32[]{:S(2)}) collective-permute-start(bf16[1024,256]{1,0:T(8,128)(2,1)S(1)} %get-tuple-element.34), channel_id=1, source_target_pairs={{0,1},{1,0},{2,3},{3,2},{4,5},{5,4},{6,7},{7,6},{8,9},{9,8},{10,11... | collective-permute-start | bytes 1572872 | tf_op jit(solution)/shard_map/ppermute | solution.py:359
  20.0 0.0 collective-permute-done.6.swap_ref
  20.0 2.1 %far.1 = (f32[2,16,256]{2,1,0:T(8,128)S(1)}, f32[1024,256]{1,0:T(8,128)S(1)}) custom-call(s32[1]{0:T(128)} %bitcast.ids_ref, bf16[1024,256]{1,0:T(8,128)(2,1)S(1)} %collective-permute-done.6.swap_ref, bf16[1024,256]{1,0:T(8,128)(2,1)S(1)} %get-tuple-element.38.right_ref, bf16[1024,256]{1,0:T(8,128)(2,1)S(1)} %get-tuple-element.39.left_ref, ...), custom_call_target="tpu_custom_call" | custom-call | flops 20000000 | bytes 6000000 | tf_op jit(solution)/shard_map/far/pallas_call | solution.py:273
  22.0 0.0 collective-permute-done.5.relay_ref
  22.0 1.5 %last.1 = (f32[8,40,128]{2,1,0:T(8,128)S(1)}, bf16[1024,256]{1,0:T(8,128)(2,1)S(1)}) custom-call(s32[1]{0:T(128)} %bitcast.ids_ref, bf16[1024,256]{1,0:T(8,128)(2,1)S(1)} %collective-permute-done.5.relay_ref, bf16[7,1024,256]{2,1,0:T(8,128)(2,1)S(1)} %get-tuple-element.35.saved, f32[9,2,256]{2,1,0:T(2,128)S(1)} %get-tuple-element.36.par_ref, ...), custom_call_target="tpu_custom_call" | custom-call | flops 20000000 | bytes 6000000 | tf_op jit(solution)/shard_map/last/pallas_call | solution.py:273
  23.5 10.8 %all_to_all.15.got_ref = f32[8,40,128]{2,1,0:T(8,128)S(1)} all-to-all(f32[8,40,128]{2,1,0:T(8,128)S(1)} %get-tuple-element.44), channel_id=1, replica_groups=mesh['x'=4,'zl'=2,'zh'=4,'y'=8,'core'=2] {'x','core'}, dimensions={0} | all-to-all | bytes 327680 | tf_op jit(solution)/shard_map/all_to_all | solution.py:382
  34.3 23.7 %all_to_all.16.got_ref = f32[8,40,128]{2,1,0:T(8,128)S(1)} all-to-all(f32[8,40,128]{2,1,0:T(8,128)S(1)} %fold.2), channel_id=1, replica_groups=mesh['x'=4,'zl'=2,'zh'=4,'y'=8,'core'=2] {'y'}, dimensions={0} | all-to-all | bytes 327680 | tf_op jit(solution)/shard_map/all_to_all | solution.py:382
  58.1 15.8 %all_to_all.17.refs_0_ = f32[8,40,128]{2,1,0:T(8,128)S(1)} all-to-all(f32[8,40,128]{2,1,0:T(8,128)S(1)} %fold.3), channel_id=1, replica_groups=mesh['x'=4,'zl'=2,'zh'=4,'y'=8,'core'=2] {'zl','zh'}, dimensions={0} | all-to-all | bytes 327680 | tf_op jit(solution)/shard_map/all_to_all | solution.py:382
  73.9 0.8 %finish.1 = (f32[2,2,2,256]{3,2,1,0:T(2,128)}, f32[5,2,256]{2,1,0:T(2,128)}, bf16[1024,256]{1,0:T(8,128)(2,1)}) custom-call(f32[8,40,128]{2,1,0:T(8,128)S(1)} %all_to_all.17.refs_0_, bf16[1024,256]{1,0:T(8,128)(2,1)S(1)} %get-tuple-element.45.refs_1_), custom_call_target="tpu_custom_call" | custom-call | bytes 6000000 | tf_op jit(solution)/shard_map/finish/pallas_call | solution.py:273
  (2 shorter events, 0.0 us)
Async XLA Ops:
  0.7 11.2 %collective-permute-start.1 = (bf16[1024,256]{1,0:T(8,128)(2,1)}, bf16[1024,256]{1,0:T(8,128)(2,1)S(1)}, u32[]{:S(2)}, u32[]{:S(2)}) collective-permute-start(bf16[1024,256]{1,0:T(8,128)(2,1)} %bitcast.11), channel_id=1, source_target_pairs={{15,31},{17,1},{31,47},{33,17},{47,63},{49,33},{143,159},{145,129}... | collective-permute-start | bytes 1572872 | tf_op jit(solution)/shard_map/ppermute | solution.py:330
  1.4 13.2 %collective-permute-start = (bf16[1024,256]{1,0:T(8,128)(2,1)}, bf16[1024,256]{1,0:T(8,128)(2,1)S(1)}, u32[]{:S(2)}, u32[]{:S(2)}) collective-permute-start(bf16[1024,256]{1,0:T(8,128)(2,1)} %bitcast.12), channel_id=1, source_target_pairs={{14,16},{16,14},{30,32},{32,30},{46,48},{48,46},{78,80},{80,78},{7... | collective-permute-start | bytes 1572872 | tf_op jit(solution)/shard_map/ppermute | solution.py:329
  2.1 15.8 %collective-permute-start.3 = (bf16[1024,256]{1,0:T(8,128)(2,1)}, bf16[1024,256]{1,0:T(8,128)(2,1)S(1)}, u32[]{:S(2)}, u32[]{:S(2)}) collective-permute-start(bf16[1024,256]{1,0:T(8,128)(2,1)} %bitcast.13), channel_id=1, source_target_pairs={{0,2},{4,6},{8,10},{12,14},{1,3},{5,7},{9,11},{13,15},{16,18},{20,... | collective-permute-start | bytes 1572872 | tf_op jit(solution)/shard_map/ppermute | solution.py:331
  5.6 12.3 %collective-permute-start.4 = (bf16[1024,256]{1,0:T(8,128)(2,1)}, bf16[1024,256]{1,0:T(8,128)(2,1)S(1)}, u32[]{:S(2)}, u32[]{:S(2)}) collective-permute-start(bf16[1024,256]{1,0:T(8,128)(2,1)} %bitcast.14), channel_id=1, source_target_pairs={{2,4},{6,8},{10,12},{3,5},{7,9},{11,13},{18,20},{22,24},{26,28},{1... | collective-permute-start | bytes 1572872 | tf_op jit(solution)/shard_map/ppermute | solution.py:332
  6.3 6.4 %copy-start = (bf16[1,1024,256]{2,1,0:T(8,128)(2,1)S(1)}, bf16[1,1024,256]{2,1,0:T(8,128)(2,1)}, u32[]{:S(2)}) copy-start(bf16[1,1024,256]{2,1,0:T(8,128)(2,1)} %param.11) | copy-start | bytes 1572868
  11.9 5.9 %collective-permute-start.2 = (bf16[1024,256]{1,0:T(8,128)(2,1)S(1)}, bf16[1024,256]{1,0:T(8,128)(2,1)S(1)}, u32[]{:S(2)}, u32[]{:S(2)}) collective-permute-start(bf16[1024,256]{1,0:T(8,128)(2,1)S(1)} %collective-permute-done.1), channel_id=1, source_target_pairs={{31,17},{1,15},{47,33},{17,31},{63,49},{33,47},{159,145},{129,143}... | collective-permute-start | bytes 1572872 | tf_op jit(solution)/shard_map/ppermute | solution.py:355
  12.6 7.3 %collective-permute-start.6 = (bf16[1024,256]{1,0:T(8,128)(2,1)S(1)}, bf16[1024,256]{1,0:T(8,128)(2,1)S(1)}, u32[]{:S(2)}, u32[]{:S(2)}) collective-permute-start(bf16[1024,256]{1,0:T(8,128)(2,1)S(1)} %bitcast.16), channel_id=1, source_target_pairs={{0,1},{1,0},{2,3},{3,2},{4,5},{5,4},{6,7},{7,6},{8,9},{9,8},{10,11... | collective-permute-start | bytes 1572872 | tf_op jit(solution)/shard_map/ppermute | solution.py:333
  18.0 4.0 %collective-permute-start.5 = (bf16[1024,256]{1,0:T(8,128)(2,1)S(1)}, bf16[1024,256]{1,0:T(8,128)(2,1)S(1)}, u32[]{:S(2)}, u32[]{:S(2)}) collective-permute-start(bf16[1024,256]{1,0:T(8,128)(2,1)S(1)} %get-tuple-element.34), channel_id=1, source_target_pairs={{0,1},{1,0},{2,3},{3,2},{4,5},{5,4},{6,7},{7,6},{8,9},{9,8},{10,11... | collective-permute-start | bytes 1572872 | tf_op jit(solution)/shard_map/ppermute | solution.py:359

commit v12 on v10

--- a/solution.py
+++ b/solution.py
@@ -155,9 +155,9 @@
     run(work, saved, coef_ref, acc_ref, lambda n, r, cols: None, keep)
 
 
-def pick_kernel(ids_ref, even_ref, odd_ref, cross_ref, turn_ref, left_ref, right_ref, send_ref):
+def pick_kernel(ids_ref, even_ref, odd_ref, cross_ref, turn_ref, late_ref, send_ref):
     ids = ids_ref[0]
-    core, detour, odd, place = ids % 2, ids // 2 % 2, ids // 4 % 2, ids // 8
+    core, detour, odd, edge = ids % 2, ids // 2 % 2, ids // 4 % 2, ids // 8
 
     def copy(a, *to):
         def step(i, carry):
@@ -169,18 +169,14 @@
 
         lax.fori_loop(0, NB, step, 0)
 
-    for side, to_ref in enumerate((left_ref, right_ref)):
-        edge = place == side
-        pl.when(edge & (detour == 0))(lambda to_ref=to_ref: copy(cross_ref, to_ref))
-        pl.when(edge & (detour == 1))(lambda to_ref=to_ref: copy(turn_ref, to_ref))
-        pl.when((place != side) & (odd != side))(lambda to_ref=to_ref: copy(even_ref, to_ref))
-        pl.when((place != side) & (odd == side))(lambda to_ref=to_ref: copy(odd_ref, to_ref))
-    pl.when(core == 0)(lambda: copy(right_ref, send_ref))
-    pl.when(core == 1)(lambda: copy(left_ref, send_ref))
-
-
-def far_kernel(ids_ref, swap_ref, right_ref, left_ref, saved, coef_ref, near_ref, part_ref, acc_ref, out_ref):
-    core = ids_ref[0] % 2
+    pl.when((edge == 1) & (detour == 0))(lambda: copy(cross_ref, late_ref))
+    pl.when((edge == 1) & (detour == 1))(lambda: copy(turn_ref, late_ref))
+    pl.when(core == odd)(lambda: copy(even_ref, send_ref))
+    pl.when(core != odd)(lambda: copy(late_ref, send_ref))
+
+
+def far_kernel(ids_ref, swap_ref, even_ref, late_ref, saved, coef_ref, near_ref, part_ref, acc_ref, out_ref):
+    core, odd = ids_ref[0] % 2, ids_ref[0] // 4 % 2
     acc_ref[...] = near_ref[...]
 
     def start(n, r, cols):
@@ -190,10 +186,14 @@
         out_ref[rows_of(0, n, r), cols] = value
 
     for b in range(2):
-        far = [[(right_ref, 2 * NB)], [(left_ref, 2 * NB)]]
-        far[b] = [(swap_ref, NB)] + far[b]
-        work = list(enumerate(far))
-        pl.when(core == b)(lambda work=work: run(work, saved, coef_ref, acc_ref, start, keep, unroll=8))
+        for o in range(2):
+            right, left = (late_ref, even_ref) if o else (even_ref, late_ref)
+            far = [[(right, 2 * NB)], [(left, 2 * NB)]]
+            far[b] = [(swap_ref, NB)] + far[b]
+            work = list(enumerate(far))
+            pl.when((core == b) & (odd == o))(
+                lambda work=work: run(work, saved, coef_ref, acc_ref, start, keep, unroll=8)
+            )
 
 
 def last_kernel(ids_ref, relay_ref, saved, par_ref, coef_ref, far_ref, part_ref, sums_ref, grad_ref, acc_ref, sum_ref):
@@ -267,7 +267,7 @@
         copy.wait()
 
 
-def call(kernel, name, outs, args, spaces, scratch=(), flops=0, spaces_out=None):
+def call(kernel, name, outs, args, spaces, scratch=(), flops=0, spaces_out=None, aliases={}):
     space = {"s": pltpu.SMEM, "v": pltpu.VMEM, "h": pltpu.HBM, "a": pl.ANY}
     args = [pltpu.with_memory_space_constraint(a, pltpu.HBM) if k == "h" else a for a, k in zip(args, spaces)]
     return pl.pallas_call(
@@ -276,6 +276,7 @@
         in_specs=[pl.BlockSpec(memory_space=space[k]) for k in spaces],
         out_specs=tuple(pl.BlockSpec(memory_space=space[k]) for k in spaces_out or "v" * len(outs)),
         scratch_shapes=scratch,
+        input_output_aliases=aliases,
         compiler_params=pltpu.CompilerParams(vmem_limit_bytes=8 * 1024 * 1024),
         cost_estimate=pl.CostEstimate(flops=flops, bytes_accessed=6_000_000, transcendentals=0),
         name=name,
@@ -322,9 +323,9 @@
     pair = [(0, 1), (1, 0)]
     even, odd, cross, hop, turn = routes()
     y = lax.axis_index("y")
-    place = jnp.where(y == 0, 0, jnp.where(y == lax.axis_size("y") - 1, 1, 2))
+    edge = jnp.where((y == 0) | (y == lax.axis_size("y") - 1), 1, 0)
     detour = jnp.where(lax.axis_index("zl") == 0, core, 0)
-    ids = (core + 2 * detour + 4 * (y % 2) + 8 * place).astype(jnp.int32).reshape(1)
+    ids = (core + 2 * detour + 4 * (y % 2) + 8 * edge).astype(jnp.int32).reshape(1)
     ids, dy = lax.optimization_barrier((ids, dy))
     crossed = lax.ppermute(dy, SEAM, cross)
     hopped = lax.ppermute(dy, SEAM, hop)
@@ -355,13 +356,13 @@
     turned = lax.ppermute(hopped, SEAM, turn)
     crossed, turned, evens, odds = lax.optimization_barrier((crossed, turned, evens, odds))
     halo = jax.ShapeDtypeStruct(dy.shape, dy.dtype)
-    left, right, send = call(pick_kernel, "pick", (halo,) * 3, (ids, evens, odds, crossed, turned), "svvvv")
+    late, send = call(pick_kernel, "pick", (halo,) * 2, (ids, evens, odds, crossed, turned), "svvvv", aliases={2: 0})
     relay = lax.ppermute(send, "core", pair)
     acc_far, part_far = call(
         far_kernel,
         "far",
         (acc, part),
-        (ids, swap, right, left, saved, coef, acc_near, part_near),
+        (ids, swap, evens, late, saved, coef, acc_near, part_near),
         "svvvvvvv",
         flops=20_000_000,
     )

time: 73.1 us -> 73.1 us (level)
  the two profiles are of different devices: /device:TPU:64 before, /device:TPU:2 now
where the time goes in v12:
time: 73.1 us; the launch traced here: 72.7 us
  blocking collectives  39.7 us (54%)
  starting transfers between devices  22 us (30%)
  Pallas kernels  10.2 us (14%)
  between operations  0.82 us (1%)
    all_to_all x3, blocking collectives, body(): got = lax.all_to_all(sums, axes, 0, 0)  39.7 us
    pallas_call x7, Pallas kernels, call(): pl.pallas_call(kernel, out_shape=outs, in_specs=[pl.BlockSpec(memory_spac...  10.2 us
    ppermute x1, starting transfers between devices, body(): swap = lax.ppermute(dy, 'core', pair)  9.75 us
    ppermute x1, starting transfers between devices, body(): relay = lax.ppermute(send, 'core', pair)  5.98 us
    ppermute x1, starting transfers between devices, body(): evens = lax.ppermute(dy, CTX, even)  3.48 us
  transfers between devices with their start and end apart: 7, of which 0 were waited for; matrix products, arithmetic and copies ran while one was open for 0% of the time, Pallas kernels for 11%

profile of v12, /device:TPU:2, one launch (start us, length us, event | category | flops | bytes accessed | tf_op | source)
XLA Modules:
  0.0 72.7 jit_solution(12041471399279609486)
XLA Ops:
  0.7 0.7 collective-permute-start.1
  1.4 0.7 collective-permute-start
  2.1 3.5 %collective-permute-start.3 = (bf16[1024,256]{1,0:T(8,128)(2,1)}, bf16[1024,256]{1,0:T(8,128)(2,1)S(1)}, u32[]{:S(2)}, u32[]{:S(2)}) collective-permute-start(bf16[1024,256]{1,0:T(8,128)(2,1)} %bitcast.13), channel_id=1, source_target_pairs={{0,2},{4,6},{8,10},{12,14},{1,3},{5,7},{9,11},{13,15},{16,18},{20,... | collective-permute-start | bytes 1572872 | tf_op jit(solution)/shard_map/ppermute | solution.py:332
  5.6 0.7 collective-permute-start.4
  6.3 0.0 copy-start
  6.3 5.6 %near.1 = (f32[2,16,256]{2,1,0:T(8,128)S(1)}, f32[1024,256]{1,0:T(8,128)S(1)}, f32[2,10,8,256]{3,2,1,0:T(8,128)S(1)}, f32[9,2,256]{2,1,0:T(2,128)S(1)}, bf16[7,1024,256]{2,1,0:T(8,128)(2,1)S(1)}) custom-call(bf16[1024,256]{1,0:T(8,128)(2,1)} %bitcast.15, bf16[1024,256]{1,0:T(8,128)(2,1)} %bitcast.10, bf16[3,1024,256]{2,1,0:T(8,128)(2,1)} %bitcast.8, ...), custom_call_target="tpu_custom_call" | custom-call | flops 20000000 | bytes 6000000 | tf_op jit(solution)/shard_map/near/pallas_call | solution.py:273
  11.9 0.0 collective-permute-done.1
  11.9 0.7 collective-permute-start.2
  12.6 0.0 copy-done
  12.6 9.8 %collective-permute-start.6 = (bf16[1024,256]{1,0:T(8,128)(2,1)S(1)}, bf16[1024,256]{1,0:T(8,128)(2,1)S(1)}, u32[]{:S(2)}, u32[]{:S(2)}) collective-permute-start(bf16[1024,256]{1,0:T(8,128)(2,1)S(1)} %bitcast.16), channel_id=1, source_target_pairs={{0,1},{1,0},{2,3},{3,2},{4,5},{5,4},{6,7},{7,6},{8,9},{9,8},{10,11... | collective-permute-start | bytes 1572872 | tf_op jit(solution)/shard_map/ppermute | solution.py:334
  22.4 0.0 collective-permute-done.cross_ref
  22.4 0.0 collective-permute-done.3.even_ref
  22.4 0.0 collective-permute-done.4.odd_ref
  22.4 0.0 collective-permute-done.2.turn_ref
  22.4 0.1 pick.1
  22.6 6.0 %collective-permute-start.5 = (bf16[1024,256]{1,0:T(8,128)(2,1)S(1)}, bf16[1024,256]{1,0:T(8,128)(2,1)S(1)}, u32[]{:S(2)}, u32[]{:S(2)}) collective-permute-start(bf16[1024,256]{1,0:T(8,128)(2,1)S(1)} %get-tuple-element.33), channel_id=1, source_target_pairs={{0,1},{1,0},{2,3},{3,2},{4,5},{5,4},{6,7},{7,6},{8,9},{9,8},{10,11... | collective-permute-start | bytes 1572872 | tf_op jit(solution)/shard_map/ppermute | solution.py:360
  28.6 0.0 collective-permute-done.6.swap_ref
  28.6 2.1 %far.1 = (f32[2,16,256]{2,1,0:T(8,128)S(1)}, f32[1024,256]{1,0:T(8,128)S(1)}) custom-call(s32[1]{0:T(128)} %bitcast.ids_ref, bf16[1024,256]{1,0:T(8,128)(2,1)S(1)} %collective-permute-done.6.swap_ref, bf16[1024,256]{1,0:T(8,128)(2,1)S(1)} %collective-permute-done.3.even_ref, bf16[1024,256]{1,0:T(8,128)(2,1)S(1)} %get-tuple-element.37.late_ref, ...), custom_call_target="tpu_custom_call" | custom-call | flops 20000000 | bytes 6000000 | tf_op jit(solution)/shard_map/far/pallas_call | solution.py:273
  30.6 0.0 collective-permute-done.5.relay_ref
  30.7 1.5 %last.1 = (bf16[8,48,128]{2,1,0:T(8,128)(2,1)S(1)}, bf16[1024,256]{1,0:T(8,128)(2,1)S(1)}) custom-call(s32[1]{0:T(128)} %bitcast.ids_ref, bf16[1024,256]{1,0:T(8,128)(2,1)S(1)} %collective-permute-done.5.relay_ref, bf16[7,1024,256]{2,1,0:T(8,128)(2,1)S(1)} %get-tuple-element.34.saved, f32[9,2,256]{2,1,0:T(2,128)S(1)} %get-tuple-element.35.par_ref, ...), custom_call_target="tpu_custom_call" | custom-call | flops 20000000 | bytes 6000000 | tf_op jit(solution)/shard_map/last/pallas_call | solution.py:273
  32.1 9.0 %all_to_all.15.got_ref = bf16[8,48,128]{2,1,0:T(8,128)(2,1)S(1)} all-to-all(bf16[8,48,128]{2,1,0:T(8,128)(2,1)S(1)} %get-tuple-element.42), channel_id=1, replica_groups=mesh['x'=4,'zl'=2,'zh'=4,'y'=8,'core'=2] {'x','core'}, dimensions={0} | all-to-all | bytes 196608 | tf_op jit(solution)/shard_map/all_to_all | solution.py:383
  41.1 13.2 %all_to_all.16.got_ref = bf16[8,48,128]{2,1,0:T(8,128)(2,1)S(1)} all-to-all(bf16[8,48,128]{2,1,0:T(8,128)(2,1)S(1)} %fold.2), channel_id=1, replica_groups=mesh['x'=4,'zl'=2,'zh'=4,'y'=8,'core'=2] {'y'}, dimensions={0} | all-to-all | bytes 196608 | tf_op jit(solution)/shard_map/all_to_all | solution.py:383
  54.3 17.6 %all_to_all.17.refs_0_ = bf16[8,48,128]{2,1,0:T(8,128)(2,1)S(1)} all-to-all(bf16[8,48,128]{2,1,0:T(8,128)(2,1)S(1)} %fold.3), channel_id=1, replica_groups=mesh['x'=4,'zl'=2,'zh'=4,'y'=8,'core'=2] {'zl','zh'}, dimensions={0} | all-to-all | bytes 196608 | tf_op jit(solution)/shard_map/all_to_all | solution.py:383
  71.9 0.8 %finish.1 = (f32[2,2,2,256]{3,2,1,0:T(2,128)}, f32[5,2,256]{2,1,0:T(2,128)}, bf16[1024,256]{1,0:T(8,128)(2,1)}) custom-call(bf16[8,48,128]{2,1,0:T(8,128)(2,1)S(1)} %all_to_all.17.refs_0_, bf16[1024,256]{1,0:T(8,128)(2,1)S(1)} %get-tuple-element.43.refs_1_), custom_call_target="tpu_custom_call" | custom-call | bytes 6000000 | tf_op jit(solution)/shard_map/finish/pallas_call | solution.py:273
  (2 shorter events, 0.0 us)
Async XLA Ops:
  0.7 11.2 %collective-permute-start.1 = (bf16[1024,256]{1,0:T(8,128)(2,1)}, bf16[1024,256]{1,0:T(8,128)(2,1)S(1)}, u32[]{:S(2)}, u32[]{:S(2)}) collective-permute-start(bf16[1024,256]{1,0:T(8,128)(2,1)} %bitcast.11), channel_id=1, source_target_pairs={{15,31},{17,1},{31,47},{33,17},{47,63},{49,33},{143,159},{145,129}... | collective-permute-start | bytes 1572872 | tf_op jit(solution)/shard_map/ppermute | solution.py:331
  1.4 21.0 %collective-permute-start = (bf16[1024,256]{1,0:T(8,128)(2,1)}, bf16[1024,256]{1,0:T(8,128)(2,1)S(1)}, u32[]{:S(2)}, u32[]{:S(2)}) collective-permute-start(bf16[1024,256]{1,0:T(8,128)(2,1)} %bitcast.12), channel_id=1, source_target_pairs={{14,16},{16,14},{30,32},{32,30},{46,48},{48,46},{78,80},{80,78},{7... | collective-permute-start | bytes 1572872 | tf_op jit(solution)/shard_map/ppermute | solution.py:330
  2.1 20.3 %collective-permute-start.3 = (bf16[1024,256]{1,0:T(8,128)(2,1)}, bf16[1024,256]{1,0:T(8,128)(2,1)S(1)}, u32[]{:S(2)}, u32[]{:S(2)}) collective-permute-start(bf16[1024,256]{1,0:T(8,128)(2,1)} %bitcast.13), channel_id=1, source_target_pairs={{0,2},{4,6},{8,10},{12,14},{1,3},{5,7},{9,11},{13,15},{16,18},{20,... | collective-permute-start | bytes 1572872 | tf_op jit(solution)/shard_map/ppermute | solution.py:332
  5.6 16.9 %collective-permute-start.4 = (bf16[1024,256]{1,0:T(8,128)(2,1)}, bf16[1024,256]{1,0:T(8,128)(2,1)S(1)}, u32[]{:S(2)}, u32[]{:S(2)}) collective-permute-start(bf16[1024,256]{1,0:T(8,128)(2,1)} %bitcast.14), channel_id=1, source_target_pairs={{2,4},{6,8},{10,12},{3,5},{7,9},{11,13},{18,20},{22,24},{26,28},{1... | collective-permute-start | bytes 1572872 | tf_op jit(solution)/shard_map/ppermute | solution.py:333
  6.3 6.4 %copy-start = (bf16[1,1024,256]{2,1,0:T(8,128)(2,1)S(1)}, bf16[1,1024,256]{2,1,0:T(8,128)(2,1)}, u32[]{:S(2)}) copy-start(bf16[1,1024,256]{2,1,0:T(8,128)(2,1)} %param.11) | copy-start | bytes 1572868
  11.9 10.5 %collective-permute-start.2 = (bf16[1024,256]{1,0:T(8,128)(2,1)S(1)}, bf16[1024,256]{1,0:T(8,128)(2,1)S(1)}, u32[]{:S(2)}, u32[]{:S(2)}) collective-permute-start(bf16[1024,256]{1,0:T(8,128)(2,1)S(1)} %collective-permute-done.1), channel_id=1, source_target_pairs={{31,17},{1,15},{47,33},{17,31},{63,49},{33,47},{159,145},{129,143}... | collective-permute-start | bytes 1572872 | tf_op jit(solution)/shard_map/ppermute | solution.py:356
  12.6 15.9 %collective-permute-start.6 = (bf16[1024,256]{1,0:T(8,128)(2,1)S(1)}, bf16[1024,256]{1,0:T(8,128)(2,1)S(1)}, u32[]{:S(2)}, u32[]{:S(2)}) collective-permute-start(bf16[1024,256]{1,0:T(8,128)(2,1)S(1)} %bitcast.16), channel_id=1, source_target_pairs={{0,1},{1,0},{2,3},{3,2},{4,5},{5,4},{6,7},{7,6},{8,9},{9,8},{10,11... | collective-permute-start | bytes 1572872 | tf_op jit(solution)/shard_map/ppermute | solution.py:334
  22.6 8.1 %collective-permute-start.5 = (bf16[1024,256]{1,0:T(8,128)(2,1)S(1)}, bf16[1024,256]{1,0:T(8,128)(2,1)S(1)}, u32[]{:S(2)}, u32[]{:S(2)}) collective-permute-start(bf16[1024,256]{1,0:T(8,128)(2,1)S(1)} %get-tuple-element.33), channel_id=1, source_target_pairs={{0,1},{1,0},{2,3},{3,2},{4,5},{5,4},{6,7},{7,6},{8,9},{9,8},{10,11... | collective-permute-start | bytes 1572872 | tf_op jit(solution)/shard_map/ppermute | solution.py:360
